TPU v7x, 32 devices: a whole 2x2x4 slice. The times are simulated.
32 devices in a mesh: ctx: 8 (over z, y), wt: 4 (over x, core).
Axes of the slice: x: 2, y: 2, z: 4, core: 2. Of those that a mesh axis runs over, the one named last changes fastest.
Arguments:
- tokens: bfloat16 [1024, 768], P('ctx'), may hold values from -6 to 6
- first_gain: float32 [768], replicated, may hold values from 0.1 to 1.9
- qkv_weight: bfloat16 [768, 3, 768], P(None, None, 'wt'), may hold values from -0.21875 to 0.21875
- attn_weight: bfloat16 [768, 768], P('wt'), as said below
- second_gain: float32 [768], replicated, may hold values from 0.1 to 1.9
- in_weight: bfloat16 [768, 2, 1152], P(None, None, 'wt'), may hold values from -0.21875 to 0.21875
- mlp_weight: bfloat16 [1152, 768], P('wt'), may hold values from -0.1875 to 0.1875
- cotangent: bfloat16 [1024, 768], P('ctx'), as said below
Outputs:
- output: bfloat16 [1024, 768], P('ctx')
- tokens_grad: bfloat16 [1024, 768], P('ctx')
- first_gain_grad: float32 [768], replicated
- qkv_weight_grad: float32 [768, 3, 768], P(None, None, 'wt')
- attn_weight_grad: float32 [768, 768], P('wt')
- second_gain_grad: float32 [768], replicated
- in_weight_grad: float32 [768, 2, 1152], P(None, None, 'wt')
- mlp_weight_grad: float32 [1152, 768], P('wt')
Inputs may be any that keep to these rules, and one draw needn't show every extreme that they name: `attn_weight`: dense real entries, independent from element to element. `cotangent`: dense real entries of order one in every row.
All inputs are finite; a program needn't handle non-finite values.
Results may differ from a plain program's by a relative error of at most 0.025.
Values may be sent and summed in bfloat16 or wider, within the bound.
No kernel may reach another device: no remote copies, remote signals or barrier semaphores. Data moves between devices by JAX's collectives and lax.ppermute only.
A program may use at most 128 MiB of HBM per device.

v0:
```python
import jax
import jax.numpy as jnp
from jax import lax
from jax.sharding import PartitionSpec as P

HEAD = 64


rope_base = 160000.0
norm_epsilon = 1e-05


def layer_norm(values):
    center = values - jnp.mean(values, axis=-1, keepdims=True)
    return center * lax.rsqrt(jnp.mean(center * center, axis=-1, keepdims=True) + norm_epsilon)


def rotate(values, positions, direction):
    half_width = values.shape[-1] // 2
    frequency = rope_base ** (
        -(jnp.arange(half_width).astype(jnp.float32) * 2.0 / values.shape[-1])
    )
    angles = positions[:, None] * frequency[None, :]
    cosine_part = jnp.cos(angles)[:, None, :]
    sine_part = jnp.sin(angles)[:, None, :]
    lower_half = values[..., :half_width]
    upper_half = values[..., half_width:]
    return jnp.concatenate(
        [
            lower_half * cosine_part - direction * upper_half * sine_part,
            upper_half * cosine_part + direction * lower_half * sine_part,
        ],
        axis=-1,
    )


def block_size_for(shard_rows):
    candidate = shard_rows * max(1, 1024 // shard_rows)
    return candidate


def score_terms(
    query_block, grad_block, logsum_block, delta_block, key_block, value_block, score_scale
):
    scores = (
        jnp.einsum("thd,shd->ths", query_block, key_block, preferred_element_type=jnp.float32)
        * score_scale
    )
    chances = jnp.exp(scores - logsum_block[..., None])
    chance_grad = jnp.einsum(
        "thd,shd->ths", grad_block, value_block, preferred_element_type=jnp.float32
    )
    score_grad = (chances * (chance_grad - delta_block[..., None])).astype(jnp.bfloat16)
    return (chances.astype(jnp.bfloat16), score_grad)


def body(
    tokens, first_gain, qkv_weight, attn_weight, second_gain, in_weight, mlp_weight, cotangent
):
    row_count = tokens.shape[0]
    local_width = qkv_weight.shape[2]
    heads_here = local_width // HEAD
    score_scale = HEAD ** (-0.5)
    positions = (lax.axis_index("ctx") * row_count + jnp.arange(row_count, dtype=jnp.int32)).astype(
        jnp.float32
    )
    inputs = tokens.astype(jnp.float32)
    normed_first, first_pull = jax.vjp(layer_norm, inputs)
    first_input = (normed_first * first_gain).astype(jnp.bfloat16)
    projected = jnp.einsum(
        "td,dsh->tsh", first_input, qkv_weight, preferred_element_type=jnp.float32
    )
    shaped = projected.reshape(row_count, 3, heads_here, HEAD)
    query_rows = rotate(shaped[:, 0], positions, 1.0).astype(jnp.bfloat16)
    key_rows = rotate(shaped[:, 1], positions, 1.0).astype(jnp.bfloat16)
    value_rows = shaped[:, 2].astype(jnp.bfloat16)
    key_flat = key_rows.reshape(row_count, local_width)
    value_flat = value_rows.reshape(row_count, local_width)
    start_state = (
        jnp.full((row_count, heads_here), -1e30, jnp.float32),
        jnp.zeros((row_count, heads_here), jnp.float32),
        jnp.zeros((row_count, heads_here, HEAD), jnp.float32),
    )
    key_piece = lax.all_gather(key_flat, "ctx", axis=0, tiled=True)
    value_piece = lax.all_gather(value_flat, "ctx", axis=0, tiled=True)
    piece_rows = key_piece.shape[0]
    block_size = block_size_for(row_count)
    key_blocks = key_piece.reshape(piece_rows // block_size, block_size, heads_here, HEAD)
    value_blocks = value_piece.reshape(piece_rows // block_size, block_size, heads_here, HEAD)

    def forward_visit(state, block_item):
        running_max, running_sum, weighted = state
        key_block, value_block = block_item
        scores = (
            jnp.einsum("thd,shd->ths", query_rows, key_block, preferred_element_type=jnp.float32)
            * score_scale
        )
        new_max = jnp.maximum(running_max, jnp.max(scores, axis=-1))
        factor = jnp.exp(running_max - new_max)
        exponent = jnp.exp(scores - new_max[..., None])
        running_sum = running_sum * factor + jnp.sum(exponent, axis=-1)
        weighted = weighted * factor[..., None] + jnp.einsum(
            "ths,shd->thd",
            exponent.astype(jnp.bfloat16),
            value_block,
            preferred_element_type=jnp.float32,
        )
        return ((new_max, running_sum, weighted), None)

    result = lax.scan(forward_visit, start_state, (key_blocks, value_blocks))
    running_max, running_sum, weighted = result[0]
    attended_exact = weighted / running_sum[..., None]
    logsum = running_max + jnp.log(running_sum)
    attended = attended_exact.astype(jnp.bfloat16).reshape(row_count, local_width)
    branch = lax.psum(
        jnp.dot(attended, attn_weight, preferred_element_type=jnp.float32).astype(jnp.bfloat16),
        "wt",
    ).astype(jnp.float32)
    middle = inputs + branch
    normed_second, second_pull = jax.vjp(layer_norm, middle)
    second_input = (normed_second * second_gain).astype(jnp.bfloat16)
    gate_up = jnp.einsum("td,dsf->tsf", second_input, in_weight, preferred_element_type=jnp.float32)

    def activate(pair):
        return jax.nn.gelu(pair[:, 0], approximate=False) * pair[:, 1]

    hidden_exact, activate_back = jax.vjp(activate, gate_up)
    hidden = hidden_exact.astype(jnp.bfloat16)
    mlp_branch = lax.psum(
        jnp.dot(hidden, mlp_weight, preferred_element_type=jnp.float32).astype(jnp.bfloat16), "wt"
    ).astype(jnp.float32)
    output = (middle + mlp_branch).astype(jnp.bfloat16)
    hidden_grad = jnp.einsum("td,fd->tf", cotangent, mlp_weight, preferred_element_type=jnp.float32)
    mlp_weight_grad = jnp.einsum("tf,td->fd", hidden, cotangent, preferred_element_type=jnp.float32)
    gate_up_grad = activate_back(hidden_grad)[0].astype(jnp.bfloat16)
    second_part = jnp.einsum(
        "tsf,dsf->td", gate_up_grad, in_weight, preferred_element_type=jnp.float32
    )
    in_weight_grad = jnp.einsum(
        "td,tsf->dsf", second_input, gate_up_grad, preferred_element_type=jnp.float32
    )
    second_grad = lax.psum(second_part.astype(jnp.bfloat16), "wt").astype(jnp.float32)
    second_gain_grad = jnp.sum(second_grad * normed_second, axis=0)
    middle_grad = cotangent.astype(jnp.float32) + second_pull(second_grad * second_gain)[0]
    branch_grad = middle_grad.astype(jnp.bfloat16)
    attended_grad = jnp.einsum(
        "td,hd->th", branch_grad, attn_weight, preferred_element_type=jnp.float32
    )
    attn_weight_grad = jnp.einsum(
        "th,td->hd", attended, branch_grad, preferred_element_type=jnp.float32
    )
    grad_rows = attended_grad.astype(jnp.bfloat16).reshape(row_count, heads_here, HEAD)
    row_delta = jnp.sum(grad_rows.astype(jnp.float32) * attended_exact, axis=-1)
    zero_rows = jnp.zeros((row_count, heads_here, HEAD), jnp.float32)
    query_acc = zero_rows
    key_piece = lax.all_gather(key_flat, "ctx", axis=0, tiled=True)
    value_piece = lax.all_gather(value_flat, "ctx", axis=0, tiled=True)
    piece_rows = key_piece.shape[0]
    block_size = block_size_for(row_count)
    key_blocks = key_piece.reshape(piece_rows // block_size, block_size, heads_here, HEAD)
    value_blocks = value_piece.reshape(piece_rows // block_size, block_size, heads_here, HEAD)

    def backward_visit(partial_value, block_item):
        key_block, value_block = block_item
        chance_low, score_grad = score_terms(
            query_rows, grad_rows, logsum, row_delta, key_block, value_block, score_scale
        )
        partial_value = (
            partial_value
            + jnp.einsum("ths,shd->thd", score_grad, key_block, preferred_element_type=jnp.float32)
            * score_scale
        )
        key_term = (
            jnp.einsum("ths,thd->shd", score_grad, query_rows, preferred_element_type=jnp.float32)
            * score_scale
        )
        value_term = jnp.einsum(
            "ths,thd->shd", chance_low, grad_rows, preferred_element_type=jnp.float32
        )
        return (partial_value, (key_term, value_term))

    query_acc, terms = lax.scan(backward_visit, query_acc, (key_blocks, value_blocks))
    key_total = terms[0].reshape(piece_rows, local_width)
    value_total = terms[1].reshape(piece_rows, local_width)
    key_sum, value_sum = (
        lax.psum_scatter(key_total, "ctx", scatter_dimension=0, tiled=True),
        lax.psum_scatter(value_total, "ctx", scatter_dimension=0, tiled=True),
    )
    key_grad = key_sum.reshape(row_count, heads_here, HEAD)
    value_grad = value_sum.reshape(row_count, heads_here, HEAD)
    query_back = rotate(query_acc, positions, -1.0)
    key_back = rotate(key_grad, positions, -1.0)
    projected_grad = (
        jnp.stack([query_back, key_back, value_grad], axis=1)
        .reshape(row_count, 3, local_width)
        .astype(jnp.bfloat16)
    )
    first_part = jnp.einsum(
        "tsh,dsh->td", projected_grad, qkv_weight, preferred_element_type=jnp.float32
    )
    qkv_weight_grad = jnp.einsum(
        "td,tsh->dsh", first_input, projected_grad, preferred_element_type=jnp.float32
    )
    first_grad = lax.psum(first_part.astype(jnp.bfloat16), "wt").astype(jnp.float32)
    first_gain_grad = jnp.sum(first_grad * normed_first, axis=0)
    tokens_grad = (middle_grad + first_pull(first_grad * first_gain)[0]).astype(jnp.bfloat16)
    summed = lax.psum(
        (
            first_gain_grad,
            qkv_weight_grad,
            attn_weight_grad,
            second_gain_grad,
            in_weight_grad,
            mlp_weight_grad,
        ),
        "ctx",
    )
    return (output, tokens_grad, summed[0], summed[1], summed[2], summed[3], summed[4], summed[5])


def solution(mesh):
    return jax.shard_map(
        body,
        mesh=mesh,
        in_specs=(
            P("ctx", None),
            P(),
            P(None, None, "wt"),
            P("wt", None),
            P(),
            P(None, None, "wt"),
            P("wt", None),
            P("ctx", None),
        ),
        out_specs=(
            P("ctx", None),
            P("ctx", None),
            P(),
            P(None, None, "wt"),
            P("wt", None),
            P(),
            P(None, None, "wt"),
            P("wt", None),
        ),
        check_vma=False,
    )
```

profile of v0, /device:TPU:0, one launch (start us, length us, event | category | flops | bytes accessed | tf_op | source)
XLA Modules:
  0.0 508.3 jit_solution(16255735428320030982)
XLA Ops:
  7.2 1.1 convert_reduce_fusion
  8.4 1.1 fusion.29
  9.5 1.4 fusion.69
  11.0 29.0 %all_gather.9 = bf16[1024,192]{0,1:T(8,128)(2,1)S(1)} all-gather(bf16[128,192]{0,1:T(8,128)(2,1)S(1)} %bitcast.203), channel_id=1, replica_groups=mesh['ctx'=8,'wt'=4] {'ctx'}, dimensions={0}, use_global_device_ids=true | all-gather | bytes 442368 | tf_op jit(solution)/shard_map/all_gather | solution.py:85
  40.8 27.1 %all_gather.8 = bf16[1024,192]{0,1:T(8,128)(2,1)S(1)} all-gather(bf16[128,192]{0,1:T(8,128)(2,1)S(1)} %bitcast.204), channel_id=1, replica_groups=mesh['ctx'=8,'wt'=4] {'ctx'}, dimensions={0}, use_global_device_ids=true | all-gather | bytes 442368 | tf_op jit(solution)/shard_map/all_gather | solution.py:84
  71.3 2.0 fusion.74
  73.3 27.3 %all-reduce.10.cloned.1.call-done = bf16[128,768]{1,0:T(8,128)(2,1)} async-done(((bf16[128,768]{1,0:T(8,128)(2,1)}), bf16[128,768]{1,0:T(8,128)(2,1)}) %all-reduce.10.cloned.1.call-update) | async-done | bytes 196624 | tf_op jit(solution)/shard_map/psum | solution.py:115
  100.5 1.1 fusion.32
  101.6 1.1 multiply_reduce_fusion
  102.8 1.8 fusion.65
  107.5 31.8 %all-reduce.12.cloned.1.call-done = bf16[128,768]{1,0:T(8,128)(2,1)} async-done(((bf16[128,768]{1,0:T(8,128)(2,1)}), bf16[128,768]{1,0:T(8,128)(2,1)}) %all-reduce.12.cloned.1.call-update) | async-done | bytes 196624 | tf_op jit(solution)/shard_map/psum | solution.py:142
  139.3 1.9 fusion.27
  141.1 1.2 fusion.71
  143.7 1.2 fusion.1
  145.8 1.3 convolution_multiply_fusion.1
  147.1 2.0 fusion.13
  149.2 2.1 convolution_convert_fusion
  151.3 2.1 fusion.76
  153.4 1.7 fusion.56
  155.1 1.0 fusion.75
  156.4 53.9 %reduce-scatter.3.cloned.1.call-done = f32[128,192]{0,1:T(8,128)} async-done(((f32[1024,192]{0,1:T(8,128)}), f32[128,192]{0,1:T(8,128)}) %reduce-scatter.3.cloned.1.call-update) | async-done | bytes 98320 | tf_op jit(solution)/shard_map/reduce_scatter | solution.py:186
  211.3 65.4 %reduce-scatter.5.cloned.1.call-done = f32[128,192]{0,1:T(8,128)} async-done(((f32[1024,192]{0,1:T(8,128)}), f32[128,192]{0,1:T(8,128)}) %reduce-scatter.5.cloned.1.call-update) | async-done | bytes 98320 | tf_op jit(solution)/shard_map/reduce_scatter | solution.py:187
  277.6 1.0 fusion.8
  278.7 1.7 fusion.67
  280.4 30.8 %all-reduce.16.cloned.1.call-done = (bf16[128,768]{1,0:T(8,128)(2,1)}, bf16[128,768]{1,0:T(8,128)(2,1)}) async-done(((bf16[128,768]{1,0:T(8,128)(2,1)}, bf16[128,768]{1,0:T(8,128)(2,1)}), (bf16[128,768]{1,0:T(8,128)(2,1)}, bf16[128,768]{1,0:T(8,128)(2,1)})) %all-reduce.16.cloned.1.call-update) | async-done | bytes 393232 | tf_op jit(solution)/shard_map/psum | solution.py:129
  311.2 1.1 fusion.30
  312.3 1.2 fusion.28
  313.6 22.8 %all-reduce.2 = (f32[768]{0:T(1024)}, f32[768]{0:T(1024)}) all-reduce(f32[768]{0:T(1024)S(1)} %get-tuple-element.51, f32[768]{0:T(1024)S(1)} %copy-done.34), channel_id=1, replica_groups=mesh['ctx'=8,'wt'=4] {'ctx'}, use_global_device_ids=true, to_apply=%region_18.19 | all-reduce | flops 1536 | bytes 12288 | tf_op jit(solution)/shard_map/psum | solution.py:207
  336.4 2.0 add_convert_fusion
  338.3 156.7 %all-reduce.14.cloned.1.call-done = (f32[768,3,192]{0,2,1:T(8,128)}, f32[192,768]{1,0:T(8,128)}, f32[768,2,288]{0,2,1:T(8,128)}, f32[288,768]{1,0:T(8,128)}) async-done(((f32[768,3,192]{0,2,1:T(8,128)}, f32[192,768]{1,0:T(8,128)}, f32[768,2,288]{0,2,1:T(8,128)}, f32[288,768]{1,0:T(8,128)}), (f32[768,3,192]{0,2,1:T(8,128)}, f32[192,768]{1,0:T(8,128)}, f32[768,2,288]{0,2,1:T(8,128)}, ...) | async-done | bytes 5013520 | tf_op jit(solution)/shard_map/psum | solution.py:207
  495.0 2.9 copy.32
  498.8 1.2 copy.34
  (136 shorter events, 13.9 us)
Async XLA Ops:
  7.2 93.3 %all-reduce.10.cloned.1.call-start = ((), (), s32[]{:S(2)}) async-start(), calls=%async_computation.2 | async-start | bytes 393216 | tf_op jit(solution)/shard_map/psum | solution.py:115
  40.0 29.3 %copy-start.5 = (bf16[1024,192]{0,1:T(8,128)(2,1)}, bf16[1024,192]{0,1:T(8,128)(2,1)S(1)}, u32[]{:S(2)}) copy-start(bf16[1024,192]{0,1:T(8,128)(2,1)S(1)} %all_gather.9) | copy-start | bytes 1179652
  40.8 27.8 %copy-start.24 = (bf16[128,3,32]{0,2,1:T(8,128)(2,1)}, bf16[128,3,32]{0,2,1:T(8,128)(2,1)S(1)}, u32[]{:S(2)}) copy-start(bf16[128,3,32]{0,2,1:T(8,128)(2,1)S(1)} %get-tuple-element.85) | copy-start | bytes 73732
  40.8 27.8 %copy-start.26 = (bf16[128,3,32]{0,2,1:T(8,128)(2,1)}, bf16[128,3,32]{0,2,1:T(8,128)(2,1)S(1)}, u32[]{:S(2)}) copy-start(bf16[128,3,32]{0,2,1:T(8,128)(2,1)S(1)} %get-tuple-element.86) | copy-start | bytes 73732
  69.3 31.3 %copy-start.1 = (bf16[128,768]{1,0:T(8,128)(2,1)S(1)}, bf16[128,768]{1,0:T(8,128)(2,1)}, u32[]{:S(2)}) copy-start(bf16[128,768]{1,0:T(8,128)(2,1)} %param.8) | copy-start | bytes 589828
  70.3 32.5 %copy-start.29 = (f32[768]{0:T(1024)S(1)}, f32[768]{0:T(1024)}, u32[]{:S(2)}) copy-start(f32[768]{0:T(1024)} %param.12) | copy-start | bytes 9220
  71.2 68.0 %all-reduce.12.cloned.1.call-start = ((), (), s32[]{:S(2)}) async-start(), calls=%async_computation.3 | async-start | bytes 393216 | tf_op jit(solution)/shard_map/psum | solution.py:142
  100.5 4.1 copy-start.18
  101.6 39.5 %copy-start.35 = (f32[128]{0:T(128)}, f32[128]{0:T(128)S(1)}, u32[]{:S(2)}) copy-start(f32[128]{0:T(128)S(1)} %broadcast_multiply_fusion.1) | copy-start | bytes 1540
  102.8 38.3 %copy-start.37 = (f32[128]{0:T(128)}, f32[128]{0:T(128)S(1)}, u32[]{:S(2)}) copy-start(f32[128]{0:T(128)S(1)} %fusion.58) | copy-start | bytes 1540
  104.6 34.6 %copy-start.2 = (bf16[128,768]{1,0:T(8,128)(2,1)S(1)}, bf16[128,768]{1,0:T(8,128)(2,1)}, u32[]{:S(2)}) copy-start(bf16[128,768]{1,0:T(8,128)(2,1)} %all-reduce.10.cloned.1.call-done) | copy-start | bytes 589828
  107.4 103.0 %reduce-scatter.3.cloned.1.call-start = ((), (), s32[]{:S(2)}) async-start(), calls=%async_computation.4 | async-start | bytes 884736 | tf_op jit(solution)/shard_map/reduce_scatter | solution.py:186
  139.2 4.0 copy-start.23
  139.3 4.4 copy-start.6
  147.1 129.6 %reduce-scatter.5.cloned.1.call-start = ((), (), s32[]{:S(2)}) async-start(), calls=%async_computation.5 | async-start | bytes 884736 | tf_op jit(solution)/shard_map/reduce_scatter | solution.py:187
  149.1 4.3 copy-start.15
  149.1 4.3 copy-start.17
  149.1 4.3 copy-start.30
  149.1 4.3 copy-start.36
  149.1 4.3 copy-start.38
  149.2 162.0 %all-reduce.16.cloned.1.call-start = ((), (), s32[]{:S(2)}) async-start(), calls=%async_computation.7 | async-start | bytes 786432 | tf_op jit(solution)/shard_map/psum | solution.py:129
  151.3 3.8 copy-start.13
  155.1 55.3 %copy-start.31 = (f32[128,32]{0,1:T(8,128)S(1)}, f32[128,32]{0,1:T(8,128)}, u32[]{:S(2)}) copy-start(f32[128,32]{0,1:T(8,128)} %get-tuple-element.96) | copy-start | bytes 49156
  156.4 122.3 %copy-start.28 = (f32[768]{0:T(1024)S(1)}, f32[768]{0:T(1024)}, u32[]{:S(2)}) copy-start(f32[768]{0:T(1024)} %param.9) | copy-start | bytes 9220
  156.4 122.3 %copy-start.33 = (f32[128]{0:T(128)S(1)}, f32[128]{0:T(128)}, u32[]{:S(2)}) copy-start(f32[128]{0:T(128)} %copy-done.32) | copy-start | bytes 1540
  156.4 122.3 %copy-start.40 = (f32[128]{0:T(128)S(1)}, f32[128]{0:T(128)}, u32[]{:S(2)}) copy-start(f32[128]{0:T(128)} %copy-done.39) | copy-start | bytes 1540
  278.6 216.4 %all-reduce.14.cloned.1.call-start = ((), (), s32[]{:S(2)}) async-start(), calls=%async_computation.6 | async-start | bytes 10027008 | tf_op jit(solution)/shard_map/psum | solution.py:207
  280.4 31.9 %copy-start.44 = (f32[128]{0:T(128)S(1)}, f32[128]{0:T(128)}, u32[]{:S(2)}) copy-start(f32[128]{0:T(128)} %copy-done.43) | copy-start | bytes 1540
  280.4 33.2 %copy-start.34 = (f32[768]{0:T(1024)S(1)}, f32[768]{0:T(1024)}, u32[]{:S(2)}) copy-start(f32[768]{0:T(1024)} %get-tuple-element.49) | copy-start | bytes 9220
  280.4 56.0 %copy-start.9 = (f32[128,768]{1,0:T(8,128)S(1)}, f32[128,768]{1,0:T(8,128)}, u32[]{:S(2)}) copy-start(f32[128,768]{1,0:T(8,128)} %copy-done.8) | copy-start | bytes 1179652
  280.4 56.0 %copy-start.42 = (f32[128]{0:T(128)S(1)}, f32[128]{0:T(128)}, u32[]{:S(2)}) copy-start(f32[128]{0:T(128)} %copy-done.41) | copy-start | bytes 1540
  495.0 3.8 copy-start.11
  (19 other events, 36.8 us)
Sparse Core Ops, SparseCore 0:
  71.4 29.1 all-reduce.9
  107.5 31.6 all-reduce.11
  147.2 63.1 reduce-scatter.2
  214.5 62.1 reduce-scatter.4
  279.4 31.7 all-reduce.15
  316.1 178.8 all-reduce.13
where the time goes:
time: 509 us; the launch traced here: 508 us
  waiting for transfers between devices  366 us (72%)
  blocking collectives  78.9 us (16%)
  matrix products  23.1 us (5%)
  other arithmetic  16.4 us (3%)
  between operations  14.6 us (3%)
  local copies, waits for them, and re-layouts  9.09 us (2%)
    psum x1, waiting for transfers between devices, body(): lax.psum((first_gain_grad, qkv_weight_grad, attn_weight_grad, second_gain...  157 us
    reduce_scatter x1, waiting for transfers between devices, body(): lax.psum_scatter(value_total, 'ctx', scatter_dimension=0, tiled=True)  65.4 us
    reduce_scatter x1, waiting for transfers between devices, body(): lax.psum_scatter(key_total, 'ctx', scatter_dimension=0, tiled=True)  53.9 us
    psum x1, waiting for transfers between devices, body(): lax.psum(second_part.astype(jnp.bfloat16), 'wt').astype(jnp.float32)  31.8 us
    psum x1, waiting for transfers between devices, body(): lax.psum(jnp.dot(hidden, mlp_weight, preferred_element_type=jnp.float32)....  30.8 us
    all_gather x1, blocking collectives, body(): value_piece = lax.all_gather(value_flat, 'ctx', axis=0, tiled=True)  29 us
    psum x1, waiting for transfers between devices, body(): lax.psum(jnp.dot(attended, attn_weight, preferred_element_type=jnp.float3...  27.3 us
    all_gather x1, blocking collectives, body(): key_piece = lax.all_gather(key_flat, 'ctx', axis=0, tiled=True)  27.1 us
  transfers between devices with their start and end apart: 6, of which 6 were waited for; matrix products, arithmetic and copies ran while one was open for 4% of the time, Pallas kernels for 0%

commit v1 on v0

--- a/solution.py
+++ b/solution.py
@@ -1,6 +1,10 @@
+import functools
+
 import jax
 import jax.numpy as jnp
 from jax import lax
+from jax.experimental import pallas as pl
+from jax.experimental.pallas import tpu as pltpu
 from jax.sharding import PartitionSpec as P
 
 HEAD = 64
@@ -54,7 +58,7 @@
     return (chances.astype(jnp.bfloat16), score_grad)
 
 
-def body(
+def split_body(
     tokens, first_gain, qkv_weight, attn_weight, second_gain, in_weight, mlp_weight, cotangent
 ):
     row_count = tokens.shape[0]
@@ -218,9 +222,436 @@
     return (output, tokens_grad, summed[0], summed[1], summed[2], summed[3], summed[4], summed[5])
 
 
+F32 = jnp.float32
+BF16 = jnp.bfloat16
+NT = (((1,), (1,)), ((), ()))
+TN = (((0,), (0,)), ((), ()))
+REPLICATED_TOKENS = 2048
+
+
+def mm(a, b, dims=(((1,), (0,)), ((), ()))):
+    return lax.dot_general(a, b, dims, preferred_element_type=F32)
+
+
+def norm_parts(values):
+    center = values - jnp.mean(values, axis=-1, keepdims=True)
+    scale = lax.rsqrt(jnp.mean(center * center, axis=-1, keepdims=True) + norm_epsilon)
+    return center * scale, scale
+
+
+def norm_back(grad, normed, scale):
+    mean_grad = jnp.mean(grad, axis=-1, keepdims=True)
+    mean_both = jnp.mean(grad * normed, axis=-1, keepdims=True)
+    return scale * (grad - mean_grad - normed * mean_both)
+
+
+def call(kernel, outs, args, scratch=(), flops=0, cells=0):
+    in_specs = [
+        pl.BlockSpec(memory_space=pltpu.SMEM if a.dtype == jnp.int32 else pltpu.VMEM) for a in args
+    ]
+    moved = sum(a.size * a.dtype.itemsize for a in args) + sum(
+        o.size * o.dtype.itemsize for o in outs
+    )
+    return pl.pallas_call(
+        kernel,
+        out_shape=outs,
+        in_specs=in_specs,
+        out_specs=[pl.BlockSpec(memory_space=pltpu.VMEM)] * len(outs),
+        scratch_shapes=list(scratch),
+        compiler_params=pltpu.CompilerParams(vmem_limit_bytes=40 * 1024 * 1024),
+        cost_estimate=pl.CostEstimate(flops=flops, bytes_accessed=moved, transcendentals=cells),
+    )(*args)
+
+
+def attention_kernel(
+    heads,
+    place,
+    mine,
+    other,
+    gain,
+    weight,
+    cosine,
+    sine,
+    tok_ref,
+    first_ref,
+    qkv_ref,
+    att_ref,
+    lse_ref,
+):
+    here, core = place[0], place[1]
+    blocks, half, width = mine.shape
+    rows = 2 * half
+    tokens = blocks * rows
+    local = heads * HEAD
+
+    def norm_block(b, carry):
+        source = jnp.bitwise_xor(b, here)
+        own, far = mine[source], other[source]
+        low = core == 0
+        block = jnp.concatenate(
+            [jnp.where(low, own, far), jnp.where(low, far, own)], axis=0
+        )
+        at = pl.ds(pl.multiple_of(b * rows, rows), rows)
+        tok_ref[at, :] = block
+        normed, _ = norm_parts(block.astype(F32))
+        first_ref[at, :] = (normed * gain[...]).astype(BF16)
+        return carry
+
+    lax.fori_loop(0, blocks, norm_block, 0)
+    chunk = 256
+    for start in range(0, tokens, chunk):
+        at = slice(start, start + chunk)
+        raw = mm(weight[...], first_ref[at, :], NT)
+        cos, sin = cosine[:, at], sine[:, at]
+        for part in range(2):
+            for head in range(heads):
+                base = part * local + head * HEAD
+                lower = raw[base : base + HEAD // 2]
+                upper = raw[base + HEAD // 2 : base + HEAD]
+                turned = jnp.concatenate(
+                    [lower * cos - upper * sin, upper * cos + lower * sin], axis=0
+                ).astype(BF16)
+                if part == 0:
+                    turned = turned * jnp.asarray(HEAD ** (-0.5), BF16)
+                qkv_ref[base : base + HEAD, at] = turned
+        qkv_ref[2 * local :, at] = raw[2 * local :].astype(BF16)
+    lse_ref[...] = jnp.zeros_like(lse_ref)
+    for head in range(heads):
+        base = head * HEAD
+        keys = qkv_ref[local + base : local + base + HEAD, :].T
+        values = qkv_ref[2 * local + base : 2 * local + base + HEAD, :]
+        for start in range(0, tokens, chunk):
+            at = slice(start, start + chunk)
+            scores = mm(keys, qkv_ref[base : base + HEAD, at])
+            top = jnp.max(scores, axis=0, keepdims=True)
+            exponent = jnp.exp(scores - top)
+            total = jnp.sum(exponent, axis=0, keepdims=True)
+            weighted = mm(values, exponent.astype(BF16))
+            att_ref[base : base + HEAD, at] = (weighted / total).astype(BF16)
+            lse_ref[head : head + 1, at] = top + jnp.log(total)
+
+
+def cdf_terms(gate):
+    half = 0.5 * (1.0 + lax.erf(gate * (0.5**0.5)))
+    slope = half + gate * (jnp.exp(-0.5 * gate * gate) * 0.3989422804014327)
+    return half, slope
+
+
+def mlp_kernel(
+    place,
+    tok,
+    att,
+    attn_weight,
+    gain,
+    in_weight,
+    mlp_weight,
+    cot,
+    middle_ref,
+    second_ref,
+    part_ref,
+    hidden_ref,
+    gate_ref,
+    out_ref,
+    all_hidden,
+    all_att,
+):
+    here, quarter, side = place[0], place[2], place[3]
+    tokens, width = tok.shape
+    parts, local, _ = att.shape
+    sides, units, _ = mlp_weight.shape
+    for p in range(parts):
+        all_att[p * local : (p + 1) * local, :] = att[jnp.bitwise_xor(quarter, p)]
+    chunk = 256
+    for start in range(0, tokens, chunk):
+        at = slice(start, start + chunk)
+        attended = all_att[:, at].T
+        middle = tok[at, :].astype(F32)
+        branch = mm(attended[:, :local], attn_weight[quarter])
+        for p in range(1, parts):
+            branch += mm(
+                attended[:, p * local : (p + 1) * local], attn_weight[jnp.bitwise_xor(quarter, p)]
+            )
+        middle = middle + branch
+        middle_ref[at, :] = middle
+        normed, _ = norm_parts(middle)
+        second = (normed * gain[...]).astype(BF16)
+        second_ref[at, :] = second
+        cot_rows = cot[at, :]
+        total = None
+        for p in range(sides):
+            r = jnp.bitwise_xor(side, p)
+            gate_up = mm(in_weight[r], second, NT)
+            gate, up = gate_up[:units], gate_up[units:]
+            half, slope = cdf_terms(gate)
+            active = gate * half
+            all_hidden[r, :, at] = (active * up).astype(BF16)
+            back = mm(mlp_weight[r], cot_rows, NT)
+            grads = jnp.concatenate([slope * up * back, active * back], axis=0).astype(BF16)
+            gate_ref[r, :, at] = grads
+            piece = mm(grads.T, in_weight[r])
+            total = piece if total is None else total + piece
+        part_ref[at, :] = total.astype(BF16)
+    rows = out_ref.shape[0]
+    own = pl.ds(pl.multiple_of(here * rows, rows), rows)
+    total = None
+    for p in range(sides):
+        r = jnp.bitwise_xor(side, p)
+        piece = mm(all_hidden[r, :, own].T, mlp_weight[r])
+        total = piece if total is None else total + piece
+    out_ref[...] = total.astype(BF16)
+    hidden_ref[...] = all_hidden[0]
+
+
+def back_kernel(
+    heads,
+    place,
+    middle,
+    part_a,
+    part_b,
+    cot,
+    gain,
+    attn_weight,
+    qkv,
+    lse,
+    weight,
+    cosine,
+    sine,
+    gain_ref,
+    branch_ref,
+    own_ref,
+    grad_ref,
+    first_ref,
+    back_rows,
+):
+    here = place[0]
+    tokens, width = middle.shape
+    rows = own_ref.shape[0]
+    local = heads * HEAD
+    gain_ref[...] = jnp.zeros_like(gain_ref)
+
+    def norm_block(b, carry):
+        at = pl.ds(pl.multiple_of(b * rows, rows), rows)
+        second = part_a[at, :].astype(F32) + part_b[at, :].astype(F32)
+        normed, scale = norm_parts(middle[at, :])
+        gain_ref[...] += jnp.sum(second * normed, axis=0, keepdims=True)
+        grad = cot[at, :].astype(F32) + norm_back(second * gain[...], normed, scale)
+        branch_ref[at, :] = grad.astype(BF16)
+
+        @pl.when(b == here)
+        def _():
+            own_ref[...] = grad
+
+        return carry
+
+    lax.fori_loop(0, tokens // rows, norm_block, 0)
+    chunk = 256
+    for start in range(0, tokens, chunk):
+        at = slice(start, start + chunk)
+        back_rows[:, at] = mm(attn_weight[...], branch_ref[at, :], NT).astype(BF16)
+    scale = HEAD ** (-0.5)
+    for head in range(heads):
+        base = head * HEAD
+        keys_t = qkv[local + base : local + base + HEAD, :]
+        keys = keys_t.T
+        values = qkv[2 * local + base : 2 * local + base + HEAD, :].T
+        key_grad = jnp.zeros((tokens, HEAD), F32)
+        value_grad = jnp.zeros((tokens, HEAD), F32)
+        for start in range(0, tokens, chunk):
+            at = slice(start, start + chunk)
+            query = qkv[base : base + HEAD, at]
+            out_grad = back_rows[base : base + HEAD, at]
+            chances = jnp.exp(mm(keys, query) - lse[head : head + 1, at])
+            chance_grad = mm(values, out_grad)
+            delta = jnp.sum(chances * chance_grad, axis=0, keepdims=True)
+            score_grad = (chances * (chance_grad - delta)).astype(BF16)
+            query_grad = mm(keys_t, score_grad) * scale
+            key_grad += mm(score_grad, query.T)
+            value_grad += mm(chances.astype(BF16), out_grad.T)
+            cos, sin = cosine[:, at], sine[:, at]
+            lower, upper = query_grad[: HEAD // 2], query_grad[HEAD // 2 :]
+            grad_ref[base : base + HEAD, at] = jnp.concatenate(
+                [lower * cos + upper * sin, upper * cos - lower * sin], axis=0
+            ).astype(BF16)
+        turned = key_grad.T
+        lower, upper = turned[: HEAD // 2], turned[HEAD // 2 :]
+        cos, sin = cosine[...], sine[...]
+        grad_ref[local + base : local + base + HEAD, :] = jnp.concatenate(
+            [lower * cos + upper * sin, upper * cos - lower * sin], axis=0
+        ).astype(BF16)
+        grad_ref[2 * local + base : 2 * local + base + HEAD, :] = value_grad.T.astype(BF16)
+    own = pl.ds(pl.multiple_of(here * rows, rows), rows)
+    first_ref[...] = mm(grad_ref[:, own].T, weight[...]).astype(BF16)
+
+
+def gather_halves(rows_here, core, spots):
+    rows, width = rows_here.shape
+    half = lax.dynamic_slice_in_dim(rows_here, core * (rows // 2), rows // 2, axis=0)
+    pieces = [half]
+    for step in range(1, spots):
+        pieces.append(
+            lax.ppermute(half, "ctx", [(spot, spot ^ step) for spot in range(spots)])
+        )
+    mine = jnp.stack(pieces)
+    return mine, swap(mine, 1)
+
+
+def swap(value, mask):
+    return lax.ppermute(value, "wt", [(spot, spot ^ mask) for spot in range(4)])
+
+
+def replicated_body(
+    spots,
+    tokens,
+    first_gain,
+    qkv_weight,
+    attn_weight,
+    second_gain,
+    in_weight,
+    mlp_weight,
+    cotangent,
+):
+    rows, width = tokens.shape
+    total_rows = rows * spots
+    local = qkv_weight.shape[2]
+    heads = local // HEAD
+    units = mlp_weight.shape[0]
+    here, quarter = lax.axis_index("ctx"), lax.axis_index("wt")
+    core, side = quarter % 2, quarter // 2
+    place = jnp.stack([here, core, quarter, side]).astype(jnp.int32)
+    frequency = rope_base ** (-(jnp.arange(HEAD // 2).astype(F32) * 2.0 / HEAD))
+    angles = frequency[:, None] * jnp.arange(total_rows).astype(F32)[None, :]
+    cosine, sine = jnp.cos(angles), jnp.sin(angles)
+    qkv_t = jnp.transpose(qkv_weight, (1, 2, 0)).reshape(3 * local, width)
+    in_t = jnp.transpose(in_weight, (1, 2, 0)).reshape(2 * units, width)
+
+    mine, other = gather_halves(tokens, core, spots)
+    attn_pair = jnp.stack([attn_weight, swap(attn_weight, 2)])
+    in_pair = jnp.stack([in_t, swap(in_t, 2)])
+    mlp_pair = jnp.stack([mlp_weight, swap(mlp_weight, 2)])
+    attn_far = swap(attn_pair, 1)
+    attn_all = jnp.stack([attn_pair[0], attn_far[0], attn_pair[1], attn_far[1]])
+
+    tok_all, first_input, qkv, att, lse = call(
+        functools.partial(attention_kernel, heads),
+        [
+            jax.ShapeDtypeStruct((total_rows, width), BF16),
+            jax.ShapeDtypeStruct((total_rows, width), BF16),
+            jax.ShapeDtypeStruct((3 * local, total_rows), BF16),
+            jax.ShapeDtypeStruct((local, total_rows), BF16),
+            jax.ShapeDtypeStruct((8, total_rows), F32),
+        ],
+        [place, mine, other, first_gain[None, :], qkv_t, cosine, sine],
+        flops=2 * total_rows * local * (3 * width + 8 * total_rows),
+        cells=heads * total_rows * total_rows,
+    )
+    cotangent, _ = lax.optimization_barrier((cotangent, mine))
+    cot_mine, cot_other = gather_halves(cotangent, core, spots)
+    cot_low = jnp.where(core == 0, cot_mine, cot_other)
+    cot_high = jnp.where(core == 0, cot_other, cot_mine)
+    cot_xor = jnp.stack([cot_low, cot_high], axis=1).reshape(spots, rows, width)
+    cot_all = jnp.concatenate(
+        [lax.dynamic_index_in_dim(cot_xor, here ^ b, 0, keepdims=False) for b in range(spots)], 0
+    )
+
+    att_pair = jnp.stack([att, swap(att, 2)])
+    att_far = swap(att_pair, 1)
+    att_all = jnp.stack([att_pair[0], att_far[0], att_pair[1], att_far[1]])
+    middle, second_input, second_part, hidden, gate_grad, out_part = call(
+        mlp_kernel,
+        [
+            jax.ShapeDtypeStruct((total_rows, width), F32),
+            jax.ShapeDtypeStruct((total_rows, width), BF16),
+            jax.ShapeDtypeStruct((total_rows, width), BF16),
+            jax.ShapeDtypeStruct((units, total_rows), BF16),
+            jax.ShapeDtypeStruct((2, 2 * units, total_rows), BF16),
+            jax.ShapeDtypeStruct((rows, width), BF16),
+        ],
+        [place, tok_all, att_all, attn_all, second_gain[None, :], in_pair, mlp_pair, cot_all],
+        scratch=[
+            pltpu.VMEM((2, units, total_rows), BF16),
+            pltpu.VMEM((4 * local, total_rows), BF16),
+        ],
+        flops=2 * total_rows * width * (4 * local + 10 * units),
+        cells=4 * units * total_rows,
+    )
+    second_far = swap(second_part, 1)
+    out_far = swap(out_part, 1)
+
+    second_gain_grad, branch_grad, middle_grad, grad_t, first_part = call(
+        functools.partial(back_kernel, heads),
+        [
+            jax.ShapeDtypeStruct((1, width), F32),
+            jax.ShapeDtypeStruct((total_rows, width), BF16),
+            jax.ShapeDtypeStruct((rows, width), F32),
+            jax.ShapeDtypeStruct((3 * local, total_rows), BF16),
+            jax.ShapeDtypeStruct((rows, width), BF16),
+        ],
+        [
+            place,
+            middle,
+            second_part,
+            second_far,
+            cot_all,
+            second_gain[None, :],
+            attn_weight,
+            qkv,
+            lse,
+            qkv_t,
+            cosine,
+            sine,
+        ],
+        scratch=[pltpu.VMEM((local, total_rows), BF16)],
+        flops=2 * total_rows * local * (width + 20 * total_rows),
+        cells=heads * total_rows * total_rows,
+    )
+    qkv_grad = mm(grad_t, first_input)
+    gain_part = jnp.sum(qkv_t.astype(F32) * qkv_grad, axis=0) / first_gain
+    gain_high = gain_part.astype(BF16)
+    gain_low = (gain_part - gain_high.astype(F32)).astype(BF16)
+    gain_rows = jnp.concatenate([gain_high[None], gain_low[None], jnp.zeros((14, width), BF16)], 0)
+    message = jnp.concatenate([first_part, gain_rows], 0)
+    pair = message.astype(F32) + swap(message, 1).astype(F32)
+    pair_low = pair.astype(BF16)
+    gain_pair = pair[rows] + pair[rows + 1]
+    gain_top = gain_pair.astype(BF16)
+    gain_rest = (gain_pair - gain_top.astype(F32)).astype(BF16)
+    across = jnp.concatenate([pair_low[:rows], gain_top[None], gain_rest[None], pair_low[rows + 2 :]], 0)
+    far = swap(across, 2)
+    first_sum = across.astype(F32) + far.astype(F32)
+    first_gain_grad = first_sum[rows] + first_sum[rows + 1]
+    first_grad = first_sum[:rows]
+
+    attn_grad = mm(att, branch_grad)
+    in_grad = mm(gate_grad[0], second_input)
+    mlp_grad = mm(hidden, cot_all)
+    own_middle = lax.dynamic_slice_in_dim(middle, here * rows, rows, axis=0)
+    output = (own_middle + (out_part.astype(F32) + out_far.astype(F32))).astype(BF16)
+    normed, scale = norm_parts(tokens.astype(F32))
+    tokens_grad = (middle_grad + norm_back(first_grad * first_gain, normed, scale)).astype(BF16)
+    return (
+        output,
+        tokens_grad,
+        first_gain_grad,
+        jnp.transpose(qkv_grad.reshape(3, local, width), (2, 0, 1)),
+        attn_grad,
+        second_gain_grad[0],
+        jnp.transpose(in_grad.reshape(2, units, width), (2, 0, 1)),
+        mlp_grad,
+    )
+
+
+def body(sizes, tokens, *rest):
+    spots, lanes = sizes["ctx"], sizes["wt"]
+    rows = tokens.shape[0]
+    small = spots * rows <= REPLICATED_TOKENS and rows % 128 == 0 and (spots * rows) % 256 == 0
+    if small and lanes == 4 and spots & (spots - 1) == 0:
+        return replicated_body(spots, tokens, *rest)
+    return split_body(tokens, *rest)
+
+
 def solution(mesh):
     return jax.shard_map(
-        body,
+        functools.partial(body, dict(mesh.shape)),
         mesh=mesh,
         in_specs=(
             P("ctx", None),

time: 509 us -> 144 us (0.28)
  waiting for transfers between devices: 366 us -> 37 us
  blocking collectives: 78.9 us -> 0 us
  Pallas kernels: 0 us -> 44.2 us
  starting transfers between devices: 0.25 us -> 36.8 us
  matrix products: 23.1 us -> 7.46 us
  between operations: 14.6 us -> 1.69 us
  other arithmetic: 16.4 us -> 5.86 us
    psum x4 -> x0, waiting for transfers between devices: 246 us -> none  [the longest x1 157 us: body(): lax.psum((first_gain_grad, qkv_weight_grad, attn_weight_grad, second_gain...]
    reduce_scatter x2 -> x0, waiting for transfers between devices: 119 us -> none  [the longest x1 65.4 us: body(): lax.psum_scatter(value_total, 'ctx', scatter_dimension=0, tiled=True)]
    all_gather x2 -> x0, blocking collectives: 56.1 us -> none  [the longest x1 29 us: body(): value_piece = lax.all_gather(value_flat, 'ctx', axis=0, tiled=True)]
    pallas_call x0 -> x3, Pallas kernels: none -> 44.2 us  [call(): pl.pallas_call(kernel, out_shape=outs, in_specs=in_specs, out_specs=[pl.B...]
    ppermute x0 -> x26, waiting for transfers between devices: none -> 37 us  [the longest x14 20.7 us: gather_halves(): lax.ppermute(half, 'ctx', [(spot, spot ^ step) for spot in range(spots)])]
    ppermute x0 -> x26, starting transfers between devices: none -> 36.8 us  [the longest x14 29.1 us: gather_halves(): lax.ppermute(half, 'ctx', [(spot, spot ^ step) for spot in range(spots)])]
    psum x1 -> x0, blocking collectives: 22.8 us -> none  [body(): lax.psum((first_gain_grad, qkv_weight_grad, attn_weight_grad, second_gain...]
    dot_general x16 -> x4, matrix products: 20 us -> 7.46 us  [mm(): return lax.dot_general(a, b, dims, preferred_element_type=F32)]
  transfers between devices with their start and end apart: 6 -> 26, of which waited for: 6 -> 9; matrix products, arithmetic and copies ran while one was open for 4% -> 10% of each run, Pallas kernels for 0% -> 21%
where the time goes in v1:
time: 144 us; the launch traced here: 141 us
  Pallas kernels  44.2 us (31%)
  waiting for transfers between devices  37 us (26%)
  starting transfers between devices  36.8 us (26%)
  local copies, waits for them, and re-layouts  8.05 us (6%)
  matrix products  7.46 us (5%)
  other arithmetic  5.86 us (4%)
  between operations  1.69 us (1%)
    pallas_call x3, Pallas kernels, call(): pl.pallas_call(kernel, out_shape=outs, in_specs=in_specs, out_specs=[pl.B...  44.2 us
    ppermute x14, starting transfers between devices, gather_halves(): lax.ppermute(half, 'ctx', [(spot, spot ^ step) for spot in range(spots)])  29.1 us
    ppermute x14, waiting for transfers between devices, gather_halves(): lax.ppermute(half, 'ctx', [(spot, spot ^ step) for spot in range(spots)])  20.7 us
    ppermute x12, waiting for transfers between devices, swap(): return lax.ppermute(value, 'wt', [(spot, spot ^ mask) for spot in range(4)])  16.3 us
    ppermute x12, starting transfers between devices, swap(): return lax.ppermute(value, 'wt', [(spot, spot ^ mask) for spot in range(4)])  7.77 us
    dot_general x4, matrix products, mm(): return lax.dot_general(a, b, dims, preferred_element_type=F32)  7.46 us
    unnamed x61, local copies, waits for them, and re-layouts  4.56 us
  transfers between devices with their start and end apart: 26, of which 9 were waited for; matrix products, arithmetic and copies ran while one was open for 10% of the time, Pallas kernels for 21%

profile of v1, /device:TPU:0, one launch (start us, length us, event | category | flops | bytes accessed | tf_op | source)
XLA Modules:
  0.0 141.0 jit_solution(3319230662060278312)
XLA Ops:
  1.6 3.0 %collective-permute-start = (bf16[64,768]{1,0:T(8,128)(2,1)S(1)}, bf16[64,768]{1,0:T(8,128)(2,1)S(1)}, u32[]{:S(2)}, u32[]{:S(2)}) collective-permute-start(bf16[64,768]{1,0:T(8,128)(2,1)S(1)} %get-tuple-element.47), channel_id=1, source_target_pairs={{0,4},{4,0},{8,12},{12,8},{16,20},{20,16},{24,28},{28,24},{1,5},{5... | collective-permute-start | bytes 294920 | tf_op jit(solution)/shard_map/ppermute | solution.py:492
  4.7 1.6 %collective-permute-start.1 = (bf16[64,768]{1,0:T(8,128)(2,1)S(1)}, bf16[64,768]{1,0:T(8,128)(2,1)S(1)}, u32[]{:S(2)}, u32[]{:S(2)}) collective-permute-start(bf16[64,768]{1,0:T(8,128)(2,1)S(1)} %get-tuple-element.47), channel_id=1, source_target_pairs={{0,8},{4,12},{8,0},{12,4},{16,24},{20,28},{24,16},{28,20},{1,9},{5... | collective-permute-start | bytes 294920 | tf_op jit(solution)/shard_map/ppermute | solution.py:492
  6.2 3.0 %collective-permute-start.3 = (bf16[64,768]{1,0:T(8,128)(2,1)S(1)}, bf16[64,768]{1,0:T(8,128)(2,1)S(1)}, u32[]{:S(2)}, u32[]{:S(2)}) collective-permute-start(bf16[64,768]{1,0:T(8,128)(2,1)S(1)} %get-tuple-element.47), channel_id=1, source_target_pairs={{0,16},{4,20},{8,24},{12,28},{16,0},{20,4},{24,8},{28,12},{1,17},{... | collective-permute-start | bytes 294920 | tf_op jit(solution)/shard_map/ppermute | solution.py:492
  9.2 1.3 collective-permute-start.4
  12.5 3.6 %collective-permute-start.5 = (bf16[64,768]{1,0:T(8,128)(2,1)S(1)}, bf16[64,768]{1,0:T(8,128)(2,1)S(1)}, u32[]{:S(2)}, u32[]{:S(2)}) collective-permute-start(bf16[64,768]{1,0:T(8,128)(2,1)S(1)} %get-tuple-element.47), channel_id=1, source_target_pairs={{0,24},{4,28},{8,16},{12,20},{16,8},{20,12},{24,0},{28,4},{1,25},{... | collective-permute-start | bytes 294920 | tf_op jit(solution)/shard_map/ppermute | solution.py:492
  16.2 1.7 %collective-permute-start.10 = (bf16[192,768]{1,0:T(8,128)(2,1)}, bf16[192,768]{1,0:T(8,128)(2,1)S(1)}, u32[]{:S(2)}, u32[]{:S(2)}) collective-permute-start(bf16[192,768]{1,0:T(8,128)(2,1)} %attn_weight.1), channel_id=1, source_target_pairs={{0,2},{1,3},{2,0},{3,1},{4,6},{5,7},{6,4},{7,5},{8,10},{9,11},{10,... | collective-permute-start | bytes 884744 | tf_op jit(solution)/shard_map/ppermute | solution.py:499
  18.4 6.0 %collective-permute-done.4 = bf16[64,768]{1,0:T(8,128)(2,1)S(1)} collective-permute-done((bf16[64,768]{1,0:T(8,128)(2,1)S(1)}, bf16[64,768]{1,0:T(8,128)(2,1)S(1)}, u32[]{:S(2)}, u32[]{:S(2)}) %collective-permute-start.4) | collective-permute-done | bytes 98336 | tf_op jit(solution)/shard_map/ppermute | solution.py:492
  24.4 1.5 %collective-permute-start.13 = (bf16[288,768]{1,0:T(8,128)(2,1)}, bf16[288,768]{1,0:T(8,128)(2,1)S(1)}, u32[]{:S(2)}, u32[]{:S(2)}) collective-permute-start(bf16[288,768]{1,0:T(8,128)(2,1)} %param.14), channel_id=1, source_target_pairs={{0,2},{1,3},{2,0},{3,1},{4,6},{5,7},{6,4},{7,5},{8,10},{9,11},{10,... | collective-permute-start | bytes 1327112 | tf_op jit(solution)/shard_map/ppermute | solution.py:499
  27.0 2.2 %collective-permute-start.15 = (bf16[64,768]{1,0:T(8,128)(2,1)S(1)}, bf16[64,768]{1,0:T(8,128)(2,1)S(1)}, u32[]{:S(2)}, u32[]{:S(2)}) collective-permute-start(bf16[64,768]{1,0:T(8,128)(2,1)S(1)} %get-tuple-element.45), channel_id=1, source_target_pairs={{0,8},{4,12},{8,0},{12,4},{16,24},{20,28},{24,16},{28,20},{1,9},{5... | collective-permute-start | bytes 294920 | tf_op jit(solution)/shard_map/ppermute | solution.py:492
  29.2 1.5 %collective-permute-done.14 = bf16[64,768]{1,0:T(8,128)(2,1)S(1)} collective-permute-done((bf16[64,768]{1,0:T(8,128)(2,1)S(1)}, bf16[64,768]{1,0:T(8,128)(2,1)S(1)}, u32[]{:S(2)}, u32[]{:S(2)}) %collective-permute-start.14) | collective-permute-done | bytes 98336 | tf_op jit(solution)/shard_map/ppermute | solution.py:492
  30.7 2.4 %collective-permute-start.16 = (bf16[64,768]{1,0:T(8,128)(2,1)S(1)}, bf16[64,768]{1,0:T(8,128)(2,1)S(1)}, u32[]{:S(2)}, u32[]{:S(2)}) collective-permute-start(bf16[64,768]{1,0:T(8,128)(2,1)S(1)} %get-tuple-element.45), channel_id=1, source_target_pairs={{0,12},{4,8},{8,4},{12,0},{16,28},{20,24},{24,20},{28,16},{1,13},{... | collective-permute-start | bytes 294920 | tf_op jit(solution)/shard_map/ppermute | solution.py:492
  33.1 1.8 %collective-permute-start.17 = (bf16[64,768]{1,0:T(8,128)(2,1)S(1)}, bf16[64,768]{1,0:T(8,128)(2,1)S(1)}, u32[]{:S(2)}, u32[]{:S(2)}) collective-permute-start(bf16[64,768]{1,0:T(8,128)(2,1)S(1)} %get-tuple-element.45), channel_id=1, source_target_pairs={{0,16},{4,20},{8,24},{12,28},{16,0},{20,4},{24,8},{28,12},{1,17},{... | collective-permute-start | bytes 294920 | tf_op jit(solution)/shard_map/ppermute | solution.py:492
  35.0 2.2 %collective-permute-done.16 = bf16[64,768]{1,0:T(8,128)(2,1)S(1)} collective-permute-done((bf16[64,768]{1,0:T(8,128)(2,1)S(1)}, bf16[64,768]{1,0:T(8,128)(2,1)S(1)}, u32[]{:S(2)}, u32[]{:S(2)}) %collective-permute-start.16) | collective-permute-done | bytes 98336 | tf_op jit(solution)/shard_map/ppermute | solution.py:492
  37.2 2.7 %collective-permute-start.18 = (bf16[64,768]{1,0:T(8,128)(2,1)S(1)}, bf16[64,768]{1,0:T(8,128)(2,1)S(1)}, u32[]{:S(2)}, u32[]{:S(2)}) collective-permute-start(bf16[64,768]{1,0:T(8,128)(2,1)S(1)} %get-tuple-element.45), channel_id=1, source_target_pairs={{0,20},{4,16},{8,28},{12,24},{16,4},{20,0},{24,12},{28,8},{1,21},{... | collective-permute-start | bytes 294920 | tf_op jit(solution)/shard_map/ppermute | solution.py:492
  39.8 4.0 %collective-permute-done.17 = bf16[64,768]{1,0:T(8,128)(2,1)S(1)} collective-permute-done((bf16[64,768]{1,0:T(8,128)(2,1)S(1)}, bf16[64,768]{1,0:T(8,128)(2,1)S(1)}, u32[]{:S(2)}, u32[]{:S(2)}) %collective-permute-start.17) | collective-permute-done | bytes 98336 | tf_op jit(solution)/shard_map/ppermute | solution.py:492
  43.8 2.8 %collective-permute-start.19 = (bf16[64,768]{1,0:T(8,128)(2,1)S(1)}, bf16[64,768]{1,0:T(8,128)(2,1)S(1)}, u32[]{:S(2)}, u32[]{:S(2)}) collective-permute-start(bf16[64,768]{1,0:T(8,128)(2,1)S(1)} %get-tuple-element.45), channel_id=1, source_target_pairs={{0,24},{4,28},{8,16},{12,20},{16,8},{20,12},{24,0},{28,4},{1,25},{... | collective-permute-start | bytes 294920 | tf_op jit(solution)/shard_map/ppermute | solution.py:492
  46.7 3.6 %collective-permute-done.19 = bf16[64,768]{1,0:T(8,128)(2,1)S(1)} collective-permute-done((bf16[64,768]{1,0:T(8,128)(2,1)S(1)}, bf16[64,768]{1,0:T(8,128)(2,1)S(1)}, u32[]{:S(2)}, u32[]{:S(2)}) %collective-permute-start.19) | collective-permute-done | bytes 98336 | tf_op jit(solution)/shard_map/ppermute | solution.py:492
  50.3 3.7 %collective-permute-start.20 = (bf16[64,768]{1,0:T(8,128)(2,1)S(1)}, bf16[64,768]{1,0:T(8,128)(2,1)S(1)}, u32[]{:S(2)}, u32[]{:S(2)}) collective-permute-start(bf16[64,768]{1,0:T(8,128)(2,1)S(1)} %get-tuple-element.45), channel_id=1, source_target_pairs={{0,28},{4,24},{8,20},{12,16},{16,12},{20,8},{24,4},{28,0},{1,29},{... | collective-permute-start | bytes 294920 | tf_op jit(solution)/shard_map/ppermute | solution.py:492
  54.2 3.4 %collective-permute-done.20 = bf16[64,768]{1,0:T(8,128)(2,1)S(1)} collective-permute-done((bf16[64,768]{1,0:T(8,128)(2,1)S(1)}, bf16[64,768]{1,0:T(8,128)(2,1)S(1)}, u32[]{:S(2)}, u32[]{:S(2)}) %collective-permute-start.20) | collective-permute-done | bytes 98336 | tf_op jit(solution)/shard_map/ppermute | solution.py:492
  57.8 12.2 %shard_map.143 = (bf16[1024,768]{1,0:T(8,128)(2,1)S(1)}, bf16[1024,768]{1,0:T(8,128)(2,1)S(1)}, bf16[576,1024]{1,0:T(8,128)(2,1)S(1)}, bf16[192,1024]{1,0:T(8,128)(2,1)S(1)}, f32[8,1024]{1,0:T(8,128)S(1)}) custom-call(s32[4]{0:T(128)S(1)} %pad_add_fusion.place, bf16[8,64,768]{2,1,0:T(8,128)(2,1)S(1)} %bitcast_dynamic-update-slice_fusion.16.mine, ...), custom_call_target="tpu_custom_call" | custom-call | flops 4127195136 | bytes 7474192 | tf_op jit(solution)/shard_map/pallas_call | solution.py:255
  71.2 1.5 %collective-permute-start.8 = (bf16[192,1024]{1,0:T(8,128)(2,1)S(1)}, bf16[192,1024]{1,0:T(8,128)(2,1)S(1)}, u32[]{:S(2)}, u32[]{:S(2)}) collective-permute-start(bf16[192,1024]{1,0:T(8,128)(2,1)S(1)} %get-tuple-element.26), channel_id=1, source_target_pairs={{0,2},{1,3},{2,0},{3,1},{4,6},{5,7},{6,4},{7,5},{8,10},{9,11},{10,... | collective-permute-start | bytes 1179656 | tf_op jit(solution)/shard_map/ppermute | solution.py:499
  73.4 9.3 %collective-permute-done.8 = bf16[192,1024]{1,0:T(8,128)(2,1)S(1)} collective-permute-done((bf16[192,1024]{1,0:T(8,128)(2,1)S(1)}, bf16[192,1024]{1,0:T(8,128)(2,1)S(1)}, u32[]{:S(2)}, u32[]{:S(2)}) %collective-permute-start.8) | collective-permute-done | bytes 393248 | tf_op jit(solution)/shard_map/ppermute | solution.py:499
  83.1 2.0 %collective-permute-done.9 = bf16[2,192,1024]{2,1,0:T(8,128)(2,1)S(1)} collective-permute-done((bf16[2,192,1024]{2,1,0:T(8,128)(2,1)S(1)}, bf16[2,192,1024]{2,1,0:T(8,128)(2,1)S(1)}, u32[]{:S(2)}, u32[]{:S(2)}) %collective-permute-start.9) | collective-permute-done | bytes 786464 | tf_op jit(solution)/shard_map/ppermute | solution.py:499
  85.4 14.6 %shard_map.144 = (f32[1024,768]{1,0:T(8,128)}, bf16[1024,768]{1,0:T(8,128)(2,1)S(1)}, bf16[1024,768]{1,0:T(8,128)(2,1)}, bf16[288,1024]{1,0:T(8,128)(2,1)S(1)}, ...) custom-call(s32[4]{0:T(128)S(1)} %pad_add_fusion.place, bf16[1024,768]{1,0:T(8,128)(2,1)S(1)} %get-tuple-element.25.tok, ...), custom_call_target="tpu_custom_call" | custom-call | flops 5737807872 | bytes 17992720 | tf_op jit(solution)/shard_map/pallas_call | solution.py:255
  102.7 1.4 slice.47
  104.5 1.5 %fusion.19 = f32[288,768]{1,0:T(8,128)} fusion(bf16[288,1024]{1,0:T(8,128)(2,1)S(1)} %get-tuple-element.41, bf16[1024,768]{1,0:T(8,128)(2,1)S(1)} %copy-done.3), kind=kOutput, calls=%fused_computation.77 | convolution fusion | flops 452984832 | bytes 3047424 | tf_op jit(solution)/shard_map/dot_general | solution.py:233
  106.1 2.3 %fusion = f32[768,2,288]{0,2,1:T(8,128)} fusion(bf16[2,288,1024]{2,1,0:T(8,128)(2,1)S(1)} %bitcast.107, bf16[1024,768]{1,0:T(8,128)(2,1)S(1)} %copy-done.10), kind=kOutput, calls=%fused_computation.4 | convolution fusion | flops 905969664 | bytes 4521984 | tf_op jit(solution)/shard_map/dot_general | solution.py:233
  109.4 17.4 %shard_map.145 = (f32[1,768]{1,0:T(1,128)S(1)}, bf16[1024,768]{1,0:T(8,128)(2,1)S(1)}, f32[128,768]{1,0:T(8,128)S(1)}, bf16[576,1024]{1,0:T(8,128)(2,1)S(1)}, bf16[128,768]{1,0:T(8,128)(2,1)S(1)}) custom-call(s32[4]{0:T(128)S(1)} %pad_add_fusion.place, f32[1024,768]{1,0:T(8,128)S(1)} %copy-done.1, bf16[1024,768]{1,0:T(8,128)(2,1)} %get-tuple-element.30.part_a, ...), custom_call_target="tpu_custom_call" | custom-call | flops 8355053568 | bytes 13867024 | tf_op jit(solution)/shard_map/pallas_call | solution.py:255
  126.8 2.3 %multiply_reduce_fusion = (f32[768]{0:T(1024)S(1)}, f32[576,768]{1,0:T(8,128)}) fusion(bf16[768,3,192]{0,2,1:T(8,128)(2,1)S(1)} %copy-done.6, bf16[576,1024]{1,0:T(8,128)(2,1)S(1)} %get-tuple-element.35, bf16[1024,768]{1,0:T(8,128)(2,1)S(1)} %copy-done.8), kind=kOutput, calls=%fused_computation.1 | convolution fusion | flops 907296000 | bytes 5409792 | tf_op jit(solution)/shard_map/dot_general | solution.py:233
  131.1 1.6 %collective-permute-start.25 = (bf16[144,768]{1,0:T(8,128)(2,1)S(1)}, bf16[144,768]{1,0:T(8,128)(2,1)S(1)}, u32[]{:S(2)}, u32[]{:S(2)}) collective-permute-start(bf16[144,768]{1,0:T(8,128)(2,1)S(1)} %pad_maximum_fusion.7), channel_id=1, source_target_pairs={{0,2},{1,3},{2,0},{3,1},{4,6},{5,7},{6,4},{7,5},{8,10},{9,11},{10,... | collective-permute-start | bytes 663560 | tf_op jit(solution)/shard_map/ppermute | solution.py:499
  132.6 1.3 fusion.18
  133.9 4.9 %collective-permute-done.25 = bf16[144,768]{1,0:T(8,128)(2,1)S(1)} collective-permute-done((bf16[144,768]{1,0:T(8,128)(2,1)S(1)}, bf16[144,768]{1,0:T(8,128)(2,1)S(1)}, u32[]{:S(2)}, u32[]{:S(2)}) %collective-permute-start.25) | collective-permute-done | bytes 221216 | tf_op jit(solution)/shard_map/ppermute | solution.py:499
  (130 shorter events, 15.1 us)
Async XLA Ops:
  0.6 25.4 %copy-start.17 = (bf16[128,768]{1,0:T(8,128)(2,1)S(1)}, bf16[128,768]{1,0:T(8,128)(2,1)}, u32[]{:S(2)}) copy-start(bf16[128,768]{1,0:T(8,128)(2,1)} %param.15) | copy-start | bytes 589828
  1.6 10.9 %collective-permute-start = (bf16[64,768]{1,0:T(8,128)(2,1)S(1)}, bf16[64,768]{1,0:T(8,128)(2,1)S(1)}, u32[]{:S(2)}, u32[]{:S(2)}) collective-permute-start(bf16[64,768]{1,0:T(8,128)(2,1)S(1)} %get-tuple-element.47), channel_id=1, source_target_pairs={{0,4},{4,0},{8,12},{12,8},{16,20},{20,16},{24,28},{28,24},{1,5},{5... | collective-permute-start | bytes 294920 | tf_op jit(solution)/shard_map/ppermute | solution.py:492
  4.7 11.5 %collective-permute-start.1 = (bf16[64,768]{1,0:T(8,128)(2,1)S(1)}, bf16[64,768]{1,0:T(8,128)(2,1)S(1)}, u32[]{:S(2)}, u32[]{:S(2)}) collective-permute-start(bf16[64,768]{1,0:T(8,128)(2,1)S(1)} %get-tuple-element.47), channel_id=1, source_target_pairs={{0,8},{4,12},{8,0},{12,4},{16,24},{20,28},{24,16},{28,20},{1,9},{5... | collective-permute-start | bytes 294920 | tf_op jit(solution)/shard_map/ppermute | solution.py:492
  6.2 10.0 %collective-permute-start.2 = (bf16[64,768]{1,0:T(8,128)(2,1)S(1)}, bf16[64,768]{1,0:T(8,128)(2,1)S(1)}, u32[]{:S(2)}, u32[]{:S(2)}) collective-permute-start(bf16[64,768]{1,0:T(8,128)(2,1)S(1)} %get-tuple-element.47), channel_id=1, source_target_pairs={{0,12},{4,8},{8,4},{12,0},{16,28},{20,24},{24,20},{28,16},{1,13},{... | collective-permute-start | bytes 294920 | tf_op jit(solution)/shard_map/ppermute | solution.py:492
  6.2 11.7 %collective-permute-start.3 = (bf16[64,768]{1,0:T(8,128)(2,1)S(1)}, bf16[64,768]{1,0:T(8,128)(2,1)S(1)}, u32[]{:S(2)}, u32[]{:S(2)}) collective-permute-start(bf16[64,768]{1,0:T(8,128)(2,1)S(1)} %get-tuple-element.47), channel_id=1, source_target_pairs={{0,16},{4,20},{8,24},{12,28},{16,0},{20,4},{24,8},{28,12},{1,17},{... | collective-permute-start | bytes 294920 | tf_op jit(solution)/shard_map/ppermute | solution.py:492
  9.2 15.2 %collective-permute-start.4 = (bf16[64,768]{1,0:T(8,128)(2,1)S(1)}, bf16[64,768]{1,0:T(8,128)(2,1)S(1)}, u32[]{:S(2)}, u32[]{:S(2)}) collective-permute-start(bf16[64,768]{1,0:T(8,128)(2,1)S(1)} %get-tuple-element.47), channel_id=1, source_target_pairs={{0,20},{4,16},{8,28},{12,24},{16,4},{20,0},{24,12},{28,8},{1,21},{... | collective-permute-start | bytes 294920 | tf_op jit(solution)/shard_map/ppermute | solution.py:492
  10.5 43.5 %copy-start = (bf16[192,768]{1,0:T(8,128)(2,1)S(1)}, bf16[192,768]{1,0:T(8,128)(2,1)}, u32[]{:S(2)}) copy-start(bf16[192,768]{1,0:T(8,128)(2,1)} %attn_weight.1) | copy-start | bytes 884740
  12.5 13.4 %collective-permute-start.5 = (bf16[64,768]{1,0:T(8,128)(2,1)S(1)}, bf16[64,768]{1,0:T(8,128)(2,1)S(1)}, u32[]{:S(2)}, u32[]{:S(2)}) collective-permute-start(bf16[64,768]{1,0:T(8,128)(2,1)S(1)} %get-tuple-element.47), channel_id=1, source_target_pairs={{0,24},{4,28},{8,16},{12,20},{16,8},{20,12},{24,0},{28,4},{1,25},{... | collective-permute-start | bytes 294920 | tf_op jit(solution)/shard_map/ppermute | solution.py:492
  16.1 9.8 %collective-permute-start.6 = (bf16[64,768]{1,0:T(8,128)(2,1)S(1)}, bf16[64,768]{1,0:T(8,128)(2,1)S(1)}, u32[]{:S(2)}, u32[]{:S(2)}) collective-permute-start(bf16[64,768]{1,0:T(8,128)(2,1)S(1)} %get-tuple-element.47), channel_id=1, source_target_pairs={{0,28},{4,24},{8,20},{12,16},{16,12},{20,8},{24,4},{28,0},{1,29},{... | collective-permute-start | bytes 294920 | tf_op jit(solution)/shard_map/ppermute | solution.py:492
  16.2 37.8 %collective-permute-start.10 = (bf16[192,768]{1,0:T(8,128)(2,1)}, bf16[192,768]{1,0:T(8,128)(2,1)S(1)}, u32[]{:S(2)}, u32[]{:S(2)}) collective-permute-start(bf16[192,768]{1,0:T(8,128)(2,1)} %attn_weight.1), channel_id=1, source_target_pairs={{0,2},{1,3},{2,0},{3,1},{4,6},{5,7},{6,4},{7,5},{8,10},{9,11},{10,... | collective-permute-start | bytes 884744 | tf_op jit(solution)/shard_map/ppermute | solution.py:499
  17.9 55.0 %collective-permute-start.12 = (bf16[576,768]{1,0:T(8,128)(2,1)}, bf16[576,768]{1,0:T(8,128)(2,1)S(1)}, u32[]{:S(2)}, u32[]{:S(2)}) collective-permute-start(bf16[576,768]{1,0:T(8,128)(2,1)} %bitcast.108), channel_id=1, source_target_pairs={{0,2},{1,3},{2,0},{3,1},{4,6},{5,7},{6,4},{7,5},{8,10},{9,11},{10,... | collective-permute-start | bytes 2654216 | tf_op jit(solution)/shard_map/ppermute | solution.py:499
  24.4 33.3 %collective-permute-start.13 = (bf16[288,768]{1,0:T(8,128)(2,1)}, bf16[288,768]{1,0:T(8,128)(2,1)S(1)}, u32[]{:S(2)}, u32[]{:S(2)}) collective-permute-start(bf16[288,768]{1,0:T(8,128)(2,1)} %param.14), channel_id=1, source_target_pairs={{0,2},{1,3},{2,0},{3,1},{4,6},{5,7},{6,4},{7,5},{8,10},{9,11},{10,... | collective-permute-start | bytes 1327112 | tf_op jit(solution)/shard_map/ppermute | solution.py:499
  25.9 31.8 %copy-start.15 = (bf16[288,768]{1,0:T(8,128)(2,1)S(1)}, bf16[288,768]{1,0:T(8,128)(2,1)}, u32[]{:S(2)}) copy-start(bf16[288,768]{1,0:T(8,128)(2,1)} %param.14) | copy-start | bytes 1327108
  26.0 4.7 %collective-permute-start.14 = (bf16[64,768]{1,0:T(8,128)(2,1)S(1)}, bf16[64,768]{1,0:T(8,128)(2,1)S(1)}, u32[]{:S(2)}, u32[]{:S(2)}) collective-permute-start(bf16[64,768]{1,0:T(8,128)(2,1)S(1)} %get-tuple-element.45), channel_id=1, source_target_pairs={{0,4},{4,0},{8,12},{12,8},{16,20},{20,16},{24,28},{28,24},{1,5},{5... | collective-permute-start | bytes 294920 | tf_op jit(solution)/shard_map/ppermute | solution.py:492
  27.0 6.2 %collective-permute-start.15 = (bf16[64,768]{1,0:T(8,128)(2,1)S(1)}, bf16[64,768]{1,0:T(8,128)(2,1)S(1)}, u32[]{:S(2)}, u32[]{:S(2)}) collective-permute-start(bf16[64,768]{1,0:T(8,128)(2,1)S(1)} %get-tuple-element.45), channel_id=1, source_target_pairs={{0,8},{4,12},{8,0},{12,4},{16,24},{20,28},{24,16},{28,20},{1,9},{5... | collective-permute-start | bytes 294920 | tf_op jit(solution)/shard_map/ppermute | solution.py:492
  30.7 6.5 %collective-permute-start.16 = (bf16[64,768]{1,0:T(8,128)(2,1)S(1)}, bf16[64,768]{1,0:T(8,128)(2,1)S(1)}, u32[]{:S(2)}, u32[]{:S(2)}) collective-permute-start(bf16[64,768]{1,0:T(8,128)(2,1)S(1)} %get-tuple-element.45), channel_id=1, source_target_pairs={{0,12},{4,8},{8,4},{12,0},{16,28},{20,24},{24,20},{28,16},{1,13},{... | collective-permute-start | bytes 294920 | tf_op jit(solution)/shard_map/ppermute | solution.py:492
  33.1 10.6 %collective-permute-start.17 = (bf16[64,768]{1,0:T(8,128)(2,1)S(1)}, bf16[64,768]{1,0:T(8,128)(2,1)S(1)}, u32[]{:S(2)}, u32[]{:S(2)}) collective-permute-start(bf16[64,768]{1,0:T(8,128)(2,1)S(1)} %get-tuple-element.45), channel_id=1, source_target_pairs={{0,16},{4,20},{8,24},{12,28},{16,0},{20,4},{24,8},{28,12},{1,17},{... | collective-permute-start | bytes 294920 | tf_op jit(solution)/shard_map/ppermute | solution.py:492
  37.2 9.5 %collective-permute-start.18 = (bf16[64,768]{1,0:T(8,128)(2,1)S(1)}, bf16[64,768]{1,0:T(8,128)(2,1)S(1)}, u32[]{:S(2)}, u32[]{:S(2)}) collective-permute-start(bf16[64,768]{1,0:T(8,128)(2,1)S(1)} %get-tuple-element.45), channel_id=1, source_target_pairs={{0,20},{4,16},{8,28},{12,24},{16,4},{20,0},{24,12},{28,8},{1,21},{... | collective-permute-start | bytes 294920 | tf_op jit(solution)/shard_map/ppermute | solution.py:492
  43.8 6.5 %collective-permute-start.19 = (bf16[64,768]{1,0:T(8,128)(2,1)S(1)}, bf16[64,768]{1,0:T(8,128)(2,1)S(1)}, u32[]{:S(2)}, u32[]{:S(2)}) collective-permute-start(bf16[64,768]{1,0:T(8,128)(2,1)S(1)} %get-tuple-element.45), channel_id=1, source_target_pairs={{0,24},{4,28},{8,16},{12,20},{16,8},{20,12},{24,0},{28,4},{1,25},{... | collective-permute-start | bytes 294920 | tf_op jit(solution)/shard_map/ppermute | solution.py:492
  46.6 11.2 %collective-permute-start.7 = (bf16[8,64,768]{2,1,0:T(8,128)(2,1)S(1)}, bf16[8,64,768]{2,1,0:T(8,128)(2,1)S(1)}, u32[]{:S(2)}, u32[]{:S(2)}) collective-permute-start(bf16[8,64,768]{2,1,0:T(8,128)(2,1)S(1)} %bitcast_dynamic-update-slice_fusion.16.mine), channel_id=1, source_target_pairs={{0,1},{1,0},{2,3},{3,2},{4,5},{5,4},{6,7},{7,6},{8,9},{9,8},{10,11... | collective-permute-start | bytes 2359304 | tf_op jit(solution)/shard_map/ppermute | solution.py:499
  50.3 7.3 %collective-permute-start.20 = (bf16[64,768]{1,0:T(8,128)(2,1)S(1)}, bf16[64,768]{1,0:T(8,128)(2,1)S(1)}, u32[]{:S(2)}, u32[]{:S(2)}) collective-permute-start(bf16[64,768]{1,0:T(8,128)(2,1)S(1)} %get-tuple-element.45), channel_id=1, source_target_pairs={{0,28},{4,24},{8,20},{12,16},{16,12},{20,8},{24,4},{28,0},{1,29},{... | collective-permute-start | bytes 294920 | tf_op jit(solution)/shard_map/ppermute | solution.py:492
  54.1 18.6 %collective-permute-start.11 = (bf16[2,192,768]{2,1,0:T(8,128)(2,1)S(1)}, bf16[2,192,768]{2,1,0:T(8,128)(2,1)S(1)}, u32[]{:S(2)}, u32[]{:S(2)}) collective-permute-start(bf16[2,192,768]{2,1,0:T(8,128)(2,1)S(1)} %pad_maximum_fusion.6), channel_id=1, source_target_pairs={{0,1},{1,0},{2,3},{3,2},{4,5},{5,4},{6,7},{7,6},{8,9},{9,8},{10,11... | collective-permute-start | bytes 1769480 | tf_op jit(solution)/shard_map/ppermute | solution.py:499
  57.6 15.5 %collective-permute-start.21 = (bf16[8,64,768]{2,1,0:T(8,128)(2,1)S(1)}, bf16[8,64,768]{2,1,0:T(8,128)(2,1)S(1)}, u32[]{:S(2)}, u32[]{:S(2)}) collective-permute-start(bf16[8,64,768]{2,1,0:T(8,128)(2,1)S(1)} %bitcast_dynamic-update-slice_fusion.8), channel_id=1, source_target_pairs={{0,1},{1,0},{2,3},{3,2},{4,5},{5,4},{6,7},{7,6},{8,9},{9,8},{10,11... | collective-permute-start | bytes 2359304 | tf_op jit(solution)/shard_map/ppermute | solution.py:499
  71.2 11.5 %collective-permute-start.8 = (bf16[192,1024]{1,0:T(8,128)(2,1)S(1)}, bf16[192,1024]{1,0:T(8,128)(2,1)S(1)}, u32[]{:S(2)}, u32[]{:S(2)}) collective-permute-start(bf16[192,1024]{1,0:T(8,128)(2,1)S(1)} %get-tuple-element.26), channel_id=1, source_target_pairs={{0,2},{1,3},{2,0},{3,1},{4,6},{5,7},{6,4},{7,5},{8,10},{9,11},{10,... | collective-permute-start | bytes 1179656 | tf_op jit(solution)/shard_map/ppermute | solution.py:499
  82.8 2.4 %collective-permute-start.9 = (bf16[2,192,1024]{2,1,0:T(8,128)(2,1)S(1)}, bf16[2,192,1024]{2,1,0:T(8,128)(2,1)S(1)}, u32[]{:S(2)}, u32[]{:S(2)}) collective-permute-start(bf16[2,192,1024]{2,1,0:T(8,128)(2,1)S(1)} %pad_maximum_fusion.5), channel_id=1, source_target_pairs={{0,1},{1,0},{2,3},{3,2},{4,5},{5,4},{6,7},{7,6},{8,9},{9,8},{10,11... | collective-permute-start | bytes 2359304 | tf_op jit(solution)/shard_map/ppermute | solution.py:499
  85.4 16.4 %copy-start.13 = (bf16[128,768]{1,0:T(8,128)(2,1)S(1)}, bf16[128,768]{1,0:T(8,128)(2,1)}, u32[]{:S(2)}) copy-start(bf16[128,768]{1,0:T(8,128)(2,1)} %param.8) | copy-start | bytes 589828
  101.1 7.3 %collective-permute-start.23 = (bf16[1024,768]{1,0:T(8,128)(2,1)}, bf16[1024,768]{1,0:T(8,128)(2,1)}, u32[]{:S(2)}, u32[]{:S(2)}) collective-permute-start(bf16[1024,768]{1,0:T(8,128)(2,1)} %get-tuple-element.30.part_a), channel_id=1, source_target_pairs={{0,1},{1,0},{2,3},{3,2},{4,5},{5,4},{6,7},{7,6},{8,9},{9,8},{10,11... | collective-permute-start | bytes 4718600 | tf_op jit(solution)/shard_map/ppermute | solution.py:499
  104.1 25.4 %collective-permute-start.22 = (bf16[128,768]{1,0:T(8,128)(2,1)S(1)}, bf16[128,768]{1,0:T(8,128)(2,1)S(1)}, u32[]{:S(2)}, u32[]{:S(2)}) collective-permute-start(bf16[128,768]{1,0:T(8,128)(2,1)S(1)} %get-tuple-element.29), channel_id=1, source_target_pairs={{0,1},{1,0},{2,3},{3,2},{4,5},{5,4},{6,7},{7,6},{8,9},{9,8},{10,11... | collective-permute-start | bytes 589832 | tf_op jit(solution)/shard_map/ppermute | solution.py:499
  109.4 17.4 %copy-start.8 = (bf16[1024,768]{1,0:T(8,128)(2,1)S(1)}, bf16[1024,768]{1,0:T(8,128)(2,1)}, u32[]{:S(2)}) copy-start(bf16[1024,768]{1,0:T(8,128)(2,1)} %copy-done.7) | copy-start | bytes 4718596
  129.3 1.6 %collective-permute-start.24 = (bf16[144,768]{1,0:T(8,128)(2,1)S(1)}, bf16[144,768]{1,0:T(8,128)(2,1)S(1)}, u32[]{:S(2)}, u32[]{:S(2)}) collective-permute-start(bf16[144,768]{1,0:T(8,128)(2,1)S(1)} %maximum_maximum_fusion), channel_id=1, source_target_pairs={{0,1},{1,0},{2,3},{3,2},{4,5},{5,4},{6,7},{7,6},{8,9},{9,8},{10,11... | collective-permute-start | bytes 663560 | tf_op jit(solution)/shard_map/ppermute | solution.py:499
  131.1 7.8 %collective-permute-start.25 = (bf16[144,768]{1,0:T(8,128)(2,1)S(1)}, bf16[144,768]{1,0:T(8,128)(2,1)S(1)}, u32[]{:S(2)}, u32[]{:S(2)}) collective-permute-start(bf16[144,768]{1,0:T(8,128)(2,1)S(1)} %pad_maximum_fusion.7), channel_id=1, source_target_pairs={{0,2},{1,3},{2,0},{3,1},{4,6},{5,7},{6,4},{7,5},{8,10},{9,11},{10,... | collective-permute-start | bytes 663560 | tf_op jit(solution)/shard_map/ppermute | solution.py:499
  132.6 6.9 %copy-start.18 = (f32[128]{0:T(128)S(1)}, f32[128]{0:T(128)}, u32[]{:S(2)}) copy-start(f32[128]{0:T(128)} %add_rsqrt_fusion) | copy-start | bytes 1540
  (14 other events, 34.0 us)

commit v2 on v0

--- a/solution.py
+++ b/solution.py
@@ -1,6 +1,10 @@
+import functools
+
 import jax
 import jax.numpy as jnp
 from jax import lax
+from jax.experimental import pallas as pl
+from jax.experimental.pallas import tpu as pltpu
 from jax.sharding import PartitionSpec as P
 
 HEAD = 64
@@ -54,7 +58,7 @@
     return (chances.astype(jnp.bfloat16), score_grad)
 
 
-def body(
+def split_body(
     tokens, first_gain, qkv_weight, attn_weight, second_gain, in_weight, mlp_weight, cotangent
 ):
     row_count = tokens.shape[0]
@@ -218,9 +222,612 @@
     return (output, tokens_grad, summed[0], summed[1], summed[2], summed[3], summed[4], summed[5])
 
 
+F32 = jnp.float32
+BF16 = jnp.bfloat16
+NT = (((1,), (1,)), ((), ()))
+TN = (((0,), (0,)), ((), ()))
+REPLICATED_TOKENS = 2048
+
+
+def mm(a, b, dims=(((1,), (0,)), ((), ()))):
+    return lax.dot_general(a, b, dims, preferred_element_type=F32)
+
+
+def norm_parts(values):
+    center = values - jnp.mean(values, axis=-1, keepdims=True)
+    scale = lax.rsqrt(jnp.mean(center * center, axis=-1, keepdims=True) + norm_epsilon)
+    return center * scale, scale
+
+
+def norm_back(grad, normed, scale):
+    mean_grad = jnp.mean(grad, axis=-1, keepdims=True)
+    mean_both = jnp.mean(grad * normed, axis=-1, keepdims=True)
+    return scale * (grad - mean_grad - normed * mean_both)
+
+
+def fast(shape, dtype):
+    return pltpu.VMEM(shape, dtype)
+
+
+class Away:
+    def __init__(self, value):
+        self.value = value
+
+
+def call(kernel, outs, args, scratch=(), copies=0, flops=0, cells=0, room=16):
+    in_specs, values = [], []
+    for arg in args:
+        value = arg.value if isinstance(arg, Away) else arg
+        if value.dtype == jnp.int32:
+            in_specs.append(pl.BlockSpec(memory_space=pltpu.SMEM))
+            values.append(value)
+            continue
+        space = pltpu.HBM if isinstance(arg, Away) else pltpu.VMEM
+        in_specs.append(pl.BlockSpec(memory_space=space))
+        values.append(pltpu.with_memory_space_constraint(value, space))
+    out_specs = [
+        pl.BlockSpec(memory_space=pltpu.HBM if isinstance(o, Away) else pltpu.VMEM) for o in outs
+    ]
+    moved = sum(a.size * a.dtype.itemsize for a in values)
+    return pl.pallas_call(
+        kernel,
+        out_shape=[o.value if isinstance(o, Away) else o for o in outs],
+        in_specs=in_specs,
+        out_specs=out_specs,
+        scratch_shapes=[pltpu.VMEM(shape, dtype) for shape, dtype in scratch]
+        + ([pltpu.SemaphoreType.DMA((copies,))] if copies else []),
+        compiler_params=pltpu.CompilerParams(vmem_limit_bytes=room * 1024 * 1024),
+        cost_estimate=pl.CostEstimate(
+            flops=flops, bytes_accessed=moved if flops else 0, transcendentals=cells
+        ),
+    )(*values)
+
+
+class Mover:
+    def __init__(self, sems):
+        self.sems, self.count, self.results = sems, 0, []
+
+    def load(self, source, target):
+        copy = pltpu.make_async_copy(source, target, self.sems.at[self.count])
+        self.count += 1
+        copy.start()
+        return copy
+
+    def store(self, source, target):
+        self.results.append(self.load(source, target))
+
+    def finish(self):
+        for copy in self.results:
+            copy.wait()
+
+
+def wait_all(copies):
+    for copy in copies:
+        copy.wait()
+
+
+def load_pieces(move, place, target, own, near, far, ids):
+    here, core = place[0], place[1]
+    rows = own.shape[0]
+    half = rows // 2
+    copies = [move.load(own, target.at[pl.ds(pl.multiple_of(here * rows, rows), rows), :])]
+    for pieces, side in ((near, core), (far, 1 - core)):
+        for ref, steps in zip(pieces, ids):
+            for i, step in enumerate(steps):
+                if step:
+                    spot = jnp.bitwise_xor(here, step) * rows + side * half
+                    copies.append(
+                        move.load(ref.at[i], target.at[pl.ds(pl.multiple_of(spot, half), half), :])
+                    )
+    return copies
+
+
+def loop(count, step, unroll=1):
+    def some(i, carry):
+        for j in range(unroll):
+            step(i * unroll + j)
+        return carry
+
+    if unroll == count:
+        some(0, 0)
+    else:
+        lax.fori_loop(0, count // unroll, some, 0)
+
+
+def part_of(i, size):
+    if isinstance(i, int):
+        return slice(i * size, (i + 1) * size)
+    return pl.ds(pl.multiple_of(i * size, size), size)
+
+
+def attend(heads, first, qkv, att, lse, keys, chunk=256):
+    def one_head(head):
+        keys[...] = qkv[part_of(heads + head, HEAD), :].T
+        rows = part_of(head, HEAD)
+
+        def one_chunk(i):
+            at = part_of(i, chunk)
+            scores = mm(keys[...], qkv[rows, part_of(i + first // chunk, chunk)])
+            top = jnp.max(scores, axis=0, keepdims=True)
+            exponent = jnp.exp(scores - top)
+            total = jnp.sum(exponent, axis=0, keepdims=True)
+            weighted = mm(qkv[part_of(2 * heads + head, HEAD), :], exponent.astype(BF16))
+            att[rows, at] = (weighted / total).astype(BF16)
+            lse[pl.ds(head, 1), at] = top + jnp.log(total)
+
+        loop(att.shape[1] // chunk, one_chunk, att.shape[1] // chunk)
+
+    lse[...] = jnp.zeros_like(lse)
+    loop(heads, one_head)
+
+
+def project_kernel(heads, ids, place, own, *refs):
+    count = len(ids)
+    near, far, refs = refs[:count], refs[count : 2 * count], refs[2 * count :]
+    gain, weight_in, cosine, sine, tok_out, first, qkv, att, lse, tok, weight, keys, sems = refs
+    move = Mover(sems)
+    local = heads * HEAD
+    tokens = tok.shape[0]
+    pieces = load_pieces(move, place, tok, own, near, far, ids)
+    weight_load = move.load(weight_in, weight)
+    wait_all(pieces)
+    move.store(tok, tok_out)
+    weight_load.wait()
+    chunk = 256
+
+    def one_chunk(i):
+        at = part_of(i, chunk)
+        normed, _ = norm_parts(tok[at, :].astype(F32))
+        rounded = (normed * gain[...]).astype(BF16)
+        first[at, :] = rounded
+        raw = mm(weight[...], rounded, NT)
+        cos, sin = cosine[:, at], sine[:, at]
+        for part in range(2):
+            for head in range(heads):
+                base = part * local + head * HEAD
+                lower = raw[base : base + HEAD // 2]
+                upper = raw[base + HEAD // 2 : base + HEAD]
+                turned = jnp.concatenate(
+                    [lower * cos - upper * sin, upper * cos + lower * sin], axis=0
+                ).astype(BF16)
+                if part == 0:
+                    turned = turned * jnp.asarray(HEAD ** (-0.5), BF16)
+                qkv[base : base + HEAD, at] = turned
+        qkv[2 * local :, at] = raw[2 * local :].astype(BF16)
+
+    loop(tokens // chunk, one_chunk, 2)
+    attend(heads, 0, qkv, att, lse, keys)
+    move.finish()
+
+
+def queries_kernel(heads, qkv, att, lse, keys):
+    attend(heads, qkv.shape[1] - att.shape[1], qkv, att, lse, keys)
+
+
+def cdf_terms(gate):
+    half = 0.5 * (1.0 + lax.erf(gate * (0.5**0.5)))
+    slope = half + gate * (jnp.exp(-0.5 * gate * gate) * 0.3989422804014327)
+    return half, slope
+
+
+def mlp_kernel(turn, ids, place, tok_in, *refs):
+    count = len(ids)
+    if turn == 0:
+        cot_own, near, far = refs[0], refs[1 : 1 + count], refs[1 + count : 1 + 2 * count]
+        refs = refs[1 + 2 * count :]
+        atts, attns, mlp_own, mlp_far = refs[:4], refs[4:8], refs[8], refs[9]
+        gain, cot, attn, w_in, w_mlp, tok_next = refs[10:16]
+        refs = refs[16:]
+    else:
+        cot, atts, (gain, attn, w_in, w_mlp), refs = refs[0], refs[1:5], refs[5:9], refs[9:]
+    middle_ref, second_ref, hidden_ref, gate_ref, part_ref, out_ref = refs[:6]
+    tokens = middle_ref.shape[0]
+    sems = refs[-1]
+    move = Mover(sems)
+    here, quarter, side = place[0], place[2], place[3]
+    local = atts[0].shape[0]
+    units = hidden_ref.shape[0]
+    begin = turn * tokens
+    first_loads = []
+    if turn == 0:
+        tok, refs = refs[6], refs[:6] + refs[7:]
+        first_loads.append(move.load(tok_in.at[:tokens, :], tok))
+    else:
+        tok = tok_in
+    att, hidden_v, gate_v = refs[6:9]
+    for p in range(4):
+        spot = pl.ds(pl.multiple_of(jnp.bitwise_xor(quarter, p) * local, local), local)
+        first_loads.append(move.load(atts[p], att.at[spot, :]))
+        if turn == 0:
+            first_loads.append(move.load(attns[p], attn.at[spot, :]))
+    in_loads, mlp_loads = [], []
+    if turn == 0:
+        for source, r in ((mlp_own, side), (mlp_far, 1 - side)):
+            for part, target in ((0, w_in), (1, w_in), (2, w_mlp)):
+                spot = pl.ds(pl.multiple_of((r + 2 * (part % 2)) * units, units), units)
+                rows = source.at[part * units : (part + 1) * units, :]
+                (mlp_loads if part == 2 else in_loads).append(move.load(rows, target.at[spot, :]))
+        mlp_loads += load_pieces(move, place, cot, cot_own, near, far, ids)
+        mlp_loads.append(move.load(tok_in.at[tokens:, :], tok_next))
+    wait_all(first_loads)
+    chunk = 256
+
+    def one_chunk(i):
+        at = part_of(i, chunk)
+        middle = tok[at, :].astype(F32) + mm(att[:, at].T, attn[...])
+        middle_ref[at, :] = middle
+        normed, _ = norm_parts(middle)
+        second = (normed * gain[...]).astype(BF16)
+        second_ref[at, :] = second
+
+        if i == 0:
+            wait_all(in_loads)
+
+        gate_up = mm(w_in[...], second, NT)
+        gate, up = gate_up[: 2 * units], gate_up[2 * units :]
+        half, slope = cdf_terms(gate)
+        active = gate * half
+        hidden_v[:, at] = (active * up).astype(BF16)
+
+        if i == 0:
+            wait_all(mlp_loads)
+
+        back = mm(w_mlp[...], cot[part_of(i + begin // chunk, chunk), :], NT)
+        grads = jnp.concatenate([slope * up * back, active * back], axis=0).astype(BF16)
+        gate_v[:, at] = grads
+        part_ref[at, :] = mm(grads.T, w_in[...]).astype(BF16)
+
+    loop(tokens // chunk, one_chunk, tokens // chunk)
+    mine = pl.ds(pl.multiple_of(side * units, units), units)
+    mine_up = pl.ds(pl.multiple_of(side * units + 2 * units, units), units)
+    hidden_ref[...] = hidden_v[mine, :]
+    gate_ref[:units, :] = gate_v[mine, :]
+    gate_ref[units:, :] = gate_v[mine_up, :]
+    rows = out_ref.shape[0]
+    spots = tokens // rows
+    out_ref[...] = jnp.zeros_like(out_ref)
+
+    @pl.when(here // spots == turn)
+    def _():
+        own = pl.ds(pl.multiple_of((here - turn * spots) * rows, rows), rows)
+        out_ref[...] = mm(hidden_v[:, own].T, w_mlp[...]).astype(BF16)
+
+
+def back_kernel(heads, place, *refs):
+    middles, parts, fars, refs = refs[:2], refs[2:4], refs[4:6], refs[6:]
+    cot, gain, attn, qkv, refs = refs[0], refs[1], refs[2], refs[3], refs[4:]
+    lses, weight, cosine, sine, refs = refs[:2], refs[2], refs[3], refs[4], refs[5:]
+    gain_v, branch, own_v, grad_v, first_v, back_rows, lse, keys, values, key_grad, value_grad = refs
+    here = place[0]
+    turns = middles[0].shape[0]
+    tokens = 2 * turns
+    rows = own_v.shape[0]
+    local = heads * HEAD
+    spots = turns // rows
+    gain_v[...] = jnp.zeros_like(gain_v)
+
+    def norm_block(turn, b, carry):
+        here_at = pl.ds(pl.multiple_of(b * rows, rows), rows)
+        at = pl.ds(pl.multiple_of((b + turn * spots) * rows, rows), rows)
+        second = parts[turn][here_at, :].astype(F32) + fars[turn][here_at, :].astype(F32)
+        normed, scale = norm_parts(middles[turn][here_at, :])
+        gain_v[...] += jnp.sum(second * normed, axis=0, keepdims=True)
+        grad = cot[at, :].astype(F32) + norm_back(second * gain[...], normed, scale)
+        branch[at, :] = grad.astype(BF16)
+
+        @pl.when(b + turn * spots == here)
+        def _():
+            own_v[...] = grad
+
+        return carry
+
+    for turn in range(2):
+        lax.fori_loop(0, spots, functools.partial(norm_block, turn), 0)
+    chunk = 256
+
+    def grad_chunk(i):
+        at = part_of(i, chunk)
+        back_rows[:, at] = mm(attn[...], branch[at, :], NT).astype(BF16)
+
+    loop(tokens // chunk, grad_chunk, 2)
+    for turn in range(2):
+        lse[:, turn * turns : (turn + 1) * turns] = lses[turn][...]
+    scale = HEAD ** (-0.5)
+
+    def turn_back(grad, cos, sin):
+        lower, upper = grad[: HEAD // 2], grad[HEAD // 2 :]
+        return jnp.concatenate(
+            [lower * cos + upper * sin, upper * cos - lower * sin], axis=0
+        ).astype(BF16)
+
+    def one_head(head):
+        rows_q, rows_k, rows_v = [part_of(p * heads + head, HEAD) for p in range(3)]
+        keys[...] = qkv[rows_k, :].T
+        values[...] = qkv[rows_v, :].T
+        key_grad[...] = jnp.zeros_like(key_grad)
+        value_grad[...] = jnp.zeros_like(value_grad)
+
+        def one_chunk(i):
+            at = part_of(i, chunk)
+            query = qkv[rows_q, at]
+            out_grad = back_rows[rows_q, at]
+            chances = jnp.exp(mm(keys[...], query) - lse[pl.ds(head, 1), at])
+            chance_grad = mm(values[...], out_grad)
+            delta = jnp.sum(chances * chance_grad, axis=0, keepdims=True)
+            score_grad = (chances * (chance_grad - delta)).astype(BF16)
+            query_grad = mm(qkv[rows_k, :], score_grad) * scale
+            key_grad[...] += mm(score_grad, query.T)
+            value_grad[...] += mm(chances.astype(BF16), out_grad.T)
+            grad_v[rows_q, at] = turn_back(query_grad, cosine[:, at], sine[:, at])
+
+        loop(tokens // chunk, one_chunk, tokens // chunk)
+        grad_v[rows_k, :] = turn_back(key_grad[...].T, cosine[...], sine[...])
+        grad_v[rows_v, :] = value_grad[...].T.astype(BF16)
+
+    loop(heads, one_head)
+    own = pl.ds(pl.multiple_of(here * rows, rows), rows)
+    first_v[...] = mm(grad_v[:, own].T, weight[...]).astype(BF16)
+
+
+def over_ctx(value, step, spots):
+    return lax.ppermute(value, "ctx", [(spot, spot ^ step) for spot in range(spots)])
+
+
+def swap(value, mask):
+    return lax.ppermute(value, "wt", [(spot, spot ^ mask) for spot in range(4)])
+
+
+def half_of(block, core):
+    half = block.shape[0] // 2
+    return lax.dynamic_slice_in_dim(block, core * half, half, axis=0)
+
+
+def gather_tokens(block, core, spots):
+    half = half_of(block, core)
+    steps = [over_ctx(half, step, spots) for step in range(2, spots, 2)]
+    first = jnp.stack([half, steps[0]])
+    rest = jnp.stack(steps[1:])
+    first_y = over_ctx(first, 1, spots)
+    rest_y = over_ctx(rest, 1, spots)
+    near = [first, first_y, rest, rest_y]
+    later = list(range(4, spots, 2))
+    ids = ((0, 2), (1, 3), tuple(later), tuple(step + 1 for step in later))
+    return near, [swap(piece, 1) for piece in near], ids, steps
+
+
+def gather_cotangent(block, core, spots, after, gate):
+    half = half_of(block, core)
+    pair = jnp.stack([half, over_ctx(half, 1, spots)])
+    pair, _ = lax.optimization_barrier((pair, after))
+    near = [pair] + [over_ctx(pair, step, spots) for step in range(2, spots, 2)]
+    ids = tuple((step, step + 1) for step in range(0, spots, 2))
+    near, _ = lax.optimization_barrier((near, gate))
+    return near, [swap(piece, 1) for piece in near], ids
+
+
+def two_rows(row):
+    high = row.astype(BF16)
+    low = (row - high.astype(F32)).astype(BF16)
+    return jnp.concatenate([high[None], low[None], jnp.zeros((14, row.shape[0]), BF16)], 0)
+
+
+def sum_rows(pair):
+    return pair[0].astype(F32) + pair[1].astype(F32)
+
+
+def replicated_body(
+    spots,
+    tokens,
+    first_gain,
+    qkv_weight,
+    attn_weight,
+    second_gain,
+    in_weight,
+    mlp_weight,
+    cotangent,
+):
+    rows, width = tokens.shape
+    total_rows = rows * spots
+    local = qkv_weight.shape[2]
+    heads = local // HEAD
+    units = mlp_weight.shape[0]
+    here, quarter = lax.axis_index("ctx"), lax.axis_index("wt")
+    core, side = quarter % 2, quarter // 2
+    place = jnp.stack([here, core, quarter, side]).astype(jnp.int32)
+    frequency = rope_base ** (-(jnp.arange(HEAD // 2).astype(F32) * 2.0 / HEAD))
+    angles = frequency[:, None] * jnp.arange(total_rows).astype(F32)[None, :]
+    cosine, sine = jnp.cos(angles), jnp.sin(angles)
+    qkv_t = jnp.transpose(qkv_weight, (1, 2, 0)).reshape(3 * local, width)
+    in_t = jnp.transpose(in_weight, (1, 2, 0)).reshape(2 * units, width)
+
+    near, far, ids, steps = gather_tokens(tokens, core, spots)
+    attn_core = swap(attn_weight, 1)
+    attn_side = swap(attn_weight, 2)
+    attn_both = swap(attn_side, 1)
+    mlp_weights = jnp.concatenate([in_t, mlp_weight], axis=0)
+    mlp_weights, _ = lax.optimization_barrier((mlp_weights, attn_side))
+    mlp_side = swap(mlp_weights, 2)
+    half_rows = total_rows // 2
+    tall, wide = (total_rows, width), (half_rows, width)
+    cells = heads * total_rows * half_rows
+    tok_all, first_input, qkv, att_a, lse_a = call(
+        functools.partial(project_kernel, heads, ids),
+        [
+            Away(pltpu.HBM(tall, BF16)),
+            fast(tall, BF16),
+            fast((3 * local, total_rows), BF16),
+            fast((local, half_rows), BF16),
+            fast((8, half_rows), F32),
+        ],
+        [
+            place,
+            Away(tokens),
+            *map(Away, near),
+            *map(Away, far),
+            first_gain[None, :],
+            Away(qkv_t),
+            cosine,
+            sine,
+        ],
+        scratch=[(tall, BF16), ((3 * local, width), BF16), ((total_rows, HEAD), BF16)],
+        copies=20,
+    )
+    side_a = swap(att_a, 2)
+    att_b, lse_b = call(
+        functools.partial(queries_kernel, heads),
+        [fast((local, half_rows), BF16), fast((8, half_rows), F32)],
+        [qkv],
+        scratch=[((total_rows, HEAD), BF16)],
+    )
+    cot_near, cot_far, cot_ids = gather_cotangent(cotangent, core, spots, steps[-1], att_b)
+    side_a, _ = lax.optimization_barrier((side_a, att_b))
+    atts_a = [att_a, swap(att_a, 1), side_a, swap(side_a, 1)]
+    halves = [
+        fast(wide, F32),
+        fast(wide, BF16),
+        fast((units, half_rows), BF16),
+        fast((2 * units, half_rows), BF16),
+        fast(wide, BF16),
+        fast((rows, width), BF16),
+    ]
+    room = [
+        ((4 * local, half_rows), BF16),
+        ((2 * units, half_rows), BF16),
+        ((4 * units, half_rows), BF16),
+    ]
+    second_row = second_gain[None, :]
+    cot_all, attn_all, in_all, mlp_all, tok_b, *results_a = call(
+        functools.partial(mlp_kernel, 0, cot_ids),
+        [
+            fast(tall, BF16),
+            fast((4 * local, width), BF16),
+            fast((4 * units, width), BF16),
+            fast((2 * units, width), BF16),
+            fast(wide, BF16),
+            *halves,
+        ],
+        [
+            place,
+            *map(Away, [tok_all, cotangent, *cot_near, *cot_far]),
+            att_a,
+            *map(Away, atts_a[1:]),
+            *map(Away, [attn_weight, attn_core, attn_side, attn_both]),
+            *map(Away, [mlp_weights, mlp_side]),
+            second_row,
+        ],
+        scratch=[(wide, BF16), *room],
+        copies=32,
+        flops=2 * half_rows * width * (4 * local + 10 * units),
+        cells=4 * units * half_rows,
+        room=20,
+    )
+    side_b, _ = lax.optimization_barrier((swap(att_b, 2), cot_all))
+    atts_b = [att_b, swap(att_b, 1), side_b, swap(side_b, 1)]
+    results_b = call(
+        functools.partial(mlp_kernel, 1, ()),
+        halves,
+        [
+            place,
+            tok_b,
+            cot_all,
+            att_b,
+            *map(Away, atts_b[1:]),
+            second_row,
+            attn_all,
+            in_all,
+            mlp_all,
+        ],
+        scratch=room,
+        copies=8,
+        flops=2 * half_rows * width * (4 * local + 10 * units),
+        cells=4 * units * half_rows,
+        room=20,
+    )
+    middles, seconds, hiddens, gates, parts, out_parts = zip(results_a, results_b)
+    fars = [swap(part, 1) for part in parts]
+    out_part = jnp.where(here < spots // 2, *out_parts)
+    out_far = swap(out_part, 1)
+
+    second_gain_grad, branch_grad, middle_grad, grad_t, first_part = call(
+        functools.partial(back_kernel, heads),
+        [
+            fast((1, width), F32),
+            fast(tall, BF16),
+            fast((rows, width), F32),
+            fast((3 * local, total_rows), BF16),
+            fast((rows, width), BF16),
+        ],
+        [
+            place,
+            *middles,
+            *parts,
+            *fars,
+            cot_all,
+            second_row,
+            attn_weight,
+            qkv,
+            lse_a,
+            lse_b,
+            qkv_t,
+            cosine,
+            sine,
+        ],
+        scratch=[
+            ((local, total_rows), BF16),
+            ((8, total_rows), F32),
+            ((total_rows, HEAD), BF16),
+            ((total_rows, HEAD), BF16),
+            ((total_rows, HEAD), F32),
+            ((total_rows, HEAD), F32),
+        ],
+        flops=2 * total_rows * local * (width + 20 * total_rows),
+        cells=heads * total_rows * total_rows,
+    )
+    pair = (first_part.astype(F32) + swap(first_part, 1).astype(F32)).astype(BF16)
+    qkv_grad = mm(grad_t, first_input)
+    gain_rows = two_rows(jnp.sum(qkv_t.astype(F32) * qkv_grad, axis=0) / first_gain)
+    across = jnp.concatenate([pair, gain_rows], 0)
+    far_rows = swap(across, 2)
+    first_grad = pair.astype(F32) + far_rows[:rows].astype(F32)
+    gain_rows = two_rows(sum_rows(gain_rows) + sum_rows(far_rows[rows:]))
+    first_gain_grad = sum_rows(gain_rows) + sum_rows(swap(gain_rows, 1))
+
+    hiddens, out_far, _ = lax.optimization_barrier((hiddens, out_far, pair))
+    attn_grad = mm(jnp.concatenate([att_a, att_b], 1), branch_grad)
+    in_grad = mm(gates[0], seconds[0]) + mm(gates[1], seconds[1])
+    mlp_grad = mm(hiddens[0], cot_all[:half_rows]) + mm(hiddens[1], cot_all[half_rows:])
+    own_row = (here % (spots // 2)) * rows
+    own_middle = jnp.where(
+        here < spots // 2,
+        *[lax.dynamic_slice_in_dim(middle, own_row, rows, axis=0) for middle in middles],
+    )
+    output = (own_middle + (out_part.astype(F32) + out_far.astype(F32))).astype(BF16)
+    normed, scale = norm_parts(tokens.astype(F32))
+    tokens_grad = (middle_grad + norm_back(first_grad * first_gain, normed, scale)).astype(BF16)
+    return (
+        output,
+        tokens_grad,
+        first_gain_grad,
+        jnp.transpose(qkv_grad.reshape(3, local, width), (2, 0, 1)),
+        attn_grad,
+        second_gain_grad[0],
+        jnp.transpose(in_grad.reshape(2, units, width), (2, 0, 1)),
+        mlp_grad,
+    )
+
+
+def body(sizes, tokens, *rest):
+    spots, lanes = sizes["ctx"], sizes["wt"]
+    rows = tokens.shape[0]
+    small = spots * rows <= REPLICATED_TOKENS and rows % 128 == 0 and (spots * rows) % 256 == 0
+    if small and lanes == 4 and spots == 8:
+        return replicated_body(spots, tokens, *rest)
+    return split_body(tokens, *rest)
+
+
 def solution(mesh):
     return jax.shard_map(
-        body,
+        functools.partial(body, dict(mesh.shape)),
         mesh=mesh,
         in_specs=(
             P("ctx", None),

time: 509 us -> 114 us (0.22)
  waiting for transfers between devices: 366 us -> 12.7 us
  blocking collectives: 78.9 us -> 0 us
  Pallas kernels: 0 us -> 48.3 us
  starting transfers between devices: 0.25 us -> 25.3 us
  matrix products: 23.1 us -> 7.77 us
  between operations: 14.6 us -> 1.45 us
  other arithmetic: 16.4 us -> 9.55 us
    psum x4 -> x0, waiting for transfers between devices: 246 us -> none  [the longest x1 157 us: body(): lax.psum((first_gain_grad, qkv_weight_grad, attn_weight_grad, second_gain...]
    reduce_scatter x2 -> x0, waiting for transfers between devices: 119 us -> none  [the longest x1 65.4 us: body(): lax.psum_scatter(value_total, 'ctx', scatter_dimension=0, tiled=True)]
    all_gather x2 -> x0, blocking collectives: 56.1 us -> none  [the longest x1 29 us: body(): value_piece = lax.all_gather(value_flat, 'ctx', axis=0, tiled=True)]
    pallas_call x0 -> x5, Pallas kernels: none -> 48.3 us  [call(): pl.pallas_call(kernel, out_shape=[o.value if isinstance(o, Away) else o f...]
    ppermute x0 -> x33, starting transfers between devices: none -> 25.3 us  [the longest x9 14.6 us: over_ctx(): lax.ppermute(value, 'ctx', [(spot, spot ^ step) for spot in range(spots)])]
    psum x1 -> x0, blocking collectives: 22.8 us -> none  [body(): lax.psum((first_gain_grad, qkv_weight_grad, attn_weight_grad, second_gain...]
    ppermute x0 -> x33, waiting for transfers between devices: none -> 12.7 us  [the longest x24 8.89 us: swap(): return lax.ppermute(value, 'wt', [(spot, spot ^ mask) for spot in range(4)])]
    dot_general x16 -> x6, matrix products: 20 us -> 7.77 us  [mm(): return lax.dot_general(a, b, dims, preferred_element_type=F32)]
  transfers between devices with their start and end apart: 6 -> 33, of which waited for: 6 -> 7; matrix products, arithmetic and copies ran while one was open for 4% -> 17% of each run, Pallas kernels for 0% -> 42%
where the time goes in v2:
time: 114 us
  Pallas kernels  48.3 us (42%)
  starting transfers between devices  25.3 us (22%)
  waiting for transfers between devices  12.7 us (11%)
  other arithmetic  9.55 us (8%)
  local copies, waits for them, and re-layouts  8.86 us (8%)
  matrix products  7.77 us (7%)
  between operations  1.45 us (1%)
    pallas_call x5, Pallas kernels, call(): pl.pallas_call(kernel, out_shape=[o.value if isinstance(o, Away) else o f...  48.3 us
    ppermute x9, starting transfers between devices, over_ctx(): lax.ppermute(value, 'ctx', [(spot, spot ^ step) for spot in range(spots)])  14.6 us
    ppermute x24, starting transfers between devices, swap(): return lax.ppermute(value, 'wt', [(spot, spot ^ mask) for spot in range(4)])  10.7 us
    ppermute x24, waiting for transfers between devices, swap(): return lax.ppermute(value, 'wt', [(spot, spot ^ mask) for spot in range(4)])  8.89 us
    dot_general x6, matrix products, mm(): return lax.dot_general(a, b, dims, preferred_element_type=F32)  7.77 us
    unnamed x104, local copies, waits for them, and re-layouts  4.94 us
    ppermute x9, waiting for transfers between devices, over_ctx(): lax.ppermute(value, 'ctx', [(spot, spot ^ step) for spot in range(spots)])  3.84 us
  transfers between devices with their start and end apart: 33, of which 7 were waited for; matrix products, arithmetic and copies ran while one was open for 17% of the time, Pallas kernels for 42%

profile of v2, /device:TPU:0, one launch (start us, length us, event | category | flops | bytes accessed | tf_op | source)
XLA Modules:
  0.0 113.9 jit_solution(5943730387949248828)
XLA Ops:
  0.7 0.9 constant_dynamic-slice_fusion.1
  1.6 4.0 %collective-permute-start.2 = (bf16[64,768]{1,0:T(8,128)(2,1)S(1)}, bf16[64,768]{1,0:T(8,128)(2,1)S(1)}, u32[]{:S(2)}, u32[]{:S(2)}) collective-permute-start(bf16[64,768]{1,0:T(8,128)(2,1)S(1)} %constant_dynamic-slice_fusion.1), channel_id=1, source_target_pairs={{0,16},{4,20},{8,24},{12,28},{16,0},{20,4},{24,8},{28,12},{1,17},{... | collective-permute-start | bytes 294920 | tf_op jit(solution)/shard_map/ppermute | solution.py:573
  5.6 1.3 %collective-permute-start.3 = (bf16[64,768]{1,0:T(8,128)(2,1)S(1)}, bf16[64,768]{1,0:T(8,128)(2,1)S(1)}, u32[]{:S(2)}, u32[]{:S(2)}) collective-permute-start(bf16[64,768]{1,0:T(8,128)(2,1)S(1)} %constant_dynamic-slice_fusion.1), channel_id=1, source_target_pairs={{0,24},{4,28},{8,16},{12,20},{16,8},{20,12},{24,0},{28,4},{1,25},{... | collective-permute-start | bytes 294920 | tf_op jit(solution)/shard_map/ppermute | solution.py:573
  7.2 0.9 constant_dynamic-slice_fusion
  8.1 1.5 %collective-permute-start.9 = (bf16[64,768]{1,0:T(8,128)(2,1)S(1)}, bf16[64,768]{1,0:T(8,128)(2,1)S(1)}, u32[]{:S(2)}, u32[]{:S(2)}) collective-permute-start(bf16[64,768]{1,0:T(8,128)(2,1)S(1)} %constant_dynamic-slice_fusion), channel_id=1, source_target_pairs={{0,4},{4,0},{8,12},{12,8},{16,20},{20,16},{24,28},{28,24},{1,5},{5... | collective-permute-start | bytes 294920 | tf_op jit(solution)/shard_map/ppermute | solution.py:573
  9.6 1.5 %collective-permute-start.21 = (bf16[192,768]{1,0:T(8,128)(2,1)}, bf16[192,768]{1,0:T(8,128)(2,1)S(1)}, u32[]{:S(2)}, u32[]{:S(2)}) collective-permute-start(bf16[192,768]{1,0:T(8,128)(2,1)} %refs_8_.1), channel_id=1, source_target_pairs={{0,2},{1,3},{2,0},{3,1},{4,6},{5,7},{6,4},{7,5},{8,10},{9,11},{10,... | collective-permute-start | bytes 884744 | tf_op jit(solution)/shard_map/ppermute | solution.py:577
  11.1 0.9 fusion.40
  12.0 1.4 %pad_maximum_fusion.refs_17_ = bf16[864,768]{1,0:T(8,128)(2,1)S(1)} fusion(bf16[288,768]{1,0:T(8,128)(2,1)} %param.14, bf16[576,768]{1,0:T(8,128)(2,1)} %bitcast.37), kind=kLoop, calls=%fused_computation.2 | loop fusion | flops 2654208 | bytes 2654208 | tf_op jit(solution)/shard_map/concatenate | solution.py:647
  13.5 1.8 %collective-permute-start.4 = (bf16[2,64,768]{2,1,0:T(8,128)(2,1)S(1)}, bf16[2,64,768]{2,1,0:T(8,128)(2,1)S(1)}, u32[]{:S(2)}, u32[]{:S(2)}) collective-permute-start(bf16[2,64,768]{2,1,0:T(8,128)(2,1)S(1)} %pad_maximum_fusion.3.refs_2_), channel_id=1, source_target_pairs={{0,4},{4,0},{8,12},{12,8},{16,20},{20,16},{24,28},{28,24},{1,5},{5... | collective-permute-start | bytes 589832 | tf_op jit(solution)/shard_map/ppermute | solution.py:573
  15.3 2.4 %collective-permute-done.21.refs_15_ = bf16[192,768]{1,0:T(8,128)(2,1)S(1)} collective-permute-done((bf16[192,768]{1,0:T(8,128)(2,1)}, bf16[192,768]{1,0:T(8,128)(2,1)S(1)}, u32[]{:S(2)}, u32[]{:S(2)}) %collective-permute-start.21) | collective-permute-done | bytes 294944 | tf_op jit(solution)/shard_map/ppermute | solution.py:577
  17.7 1.5 %collective-permute-start.23 = (bf16[864,768]{1,0:T(8,128)(2,1)S(1)}, bf16[864,768]{1,0:T(8,128)(2,1)}, u32[]{:S(2)}, u32[]{:S(2)}) collective-permute-start(bf16[864,768]{1,0:T(8,128)(2,1)S(1)} %pad_maximum_fusion.refs_17_), channel_id=1, source_target_pairs={{0,2},{1,3},{2,0},{3,1},{4,6},{5,7},{6,4},{7,5},{8,10},{9,11},{10,... | collective-permute-start | bytes 3981320 | tf_op jit(solution)/shard_map/ppermute | solution.py:577
  21.2 3.8 %collective-permute-done.1.refs_1_ = bf16[2,64,768]{2,1,0:T(8,128)(2,1)S(1)} collective-permute-done((bf16[2,64,768]{2,1,0:T(8,128)(2,1)S(1)}, bf16[2,64,768]{2,1,0:T(8,128)(2,1)S(1)}, u32[]{:S(2)}, u32[]{:S(2)}) %collective-permute-start.1) | collective-permute-done | bytes 196640 | tf_op jit(solution)/shard_map/ppermute | solution.py:573
  25.1 1.7 %collective-permute-start.10 = (bf16[2,64,768]{2,1,0:T(8,128)(2,1)S(1)}, bf16[2,64,768]{2,1,0:T(8,128)(2,1)S(1)}, u32[]{:S(2)}, u32[]{:S(2)}) collective-permute-start(bf16[2,64,768]{2,1,0:T(8,128)(2,1)S(1)} %pad_maximum_fusion.4.refs_1_), channel_id=1, source_target_pairs={{0,8},{4,12},{8,0},{12,4},{16,24},{20,28},{24,16},{28,20},{1,9},{5... | collective-permute-start | bytes 589832 | tf_op jit(solution)/shard_map/ppermute | solution.py:573
  26.8 2.0 %collective-permute-start.11 = (bf16[2,64,768]{2,1,0:T(8,128)(2,1)S(1)}, bf16[2,64,768]{2,1,0:T(8,128)(2,1)}, u32[]{:S(2)}, u32[]{:S(2)}) collective-permute-start(bf16[2,64,768]{2,1,0:T(8,128)(2,1)S(1)} %pad_maximum_fusion.4.refs_1_), channel_id=1, source_target_pairs={{0,16},{4,20},{8,24},{12,28},{16,0},{20,4},{24,8},{28,12},{1,17},{... | collective-permute-start | bytes 589832 | tf_op jit(solution)/shard_map/ppermute | solution.py:573
  28.9 1.4 %collective-permute-start.12 = (bf16[2,64,768]{2,1,0:T(8,128)(2,1)S(1)}, bf16[2,64,768]{2,1,0:T(8,128)(2,1)}, u32[]{:S(2)}, u32[]{:S(2)}) collective-permute-start(bf16[2,64,768]{2,1,0:T(8,128)(2,1)S(1)} %pad_maximum_fusion.4.refs_1_), channel_id=1, source_target_pairs={{0,24},{4,28},{8,16},{12,20},{16,8},{20,12},{24,0},{28,4},{1,25},{... | collective-permute-start | bytes 589832 | tf_op jit(solution)/shard_map/ppermute | solution.py:573
  31.0 9.3 %shard_map.143 = (bf16[1024,768]{1,0:T(8,128)(2,1)}, bf16[1024,768]{1,0:T(8,128)(2,1)S(1)}, bf16[576,1024]{1,0:T(8,128)(2,1)S(1)}, bf16[192,512]{1,0:T(8,128)(2,1)S(1)}, f32[8,512]{1,0:T(8,128)S(1)}) custom-call(s32[4]{0:T(128)S(1)} %pad_add_fusion.place, bf16[128,768]{1,0:T(8,128)(2,1)} %own.1, bf16[2,64,768]{2,1,0:T(8,128)(2,1)} %copy-done.23, ...), custom_call_target="tpu_custom_call" | custom-call | tf_op jit(solution)/shard_map/pallas_call | solution.py:272
  40.3 1.1 copy-done.15
  41.5 1.5 %collective-permute-start.18 = (bf16[192,512]{1,0:T(8,128)(2,1)S(1)}, bf16[192,512]{1,0:T(8,128)(2,1)S(1)}, u32[]{:S(2)}, u32[]{:S(2)}) collective-permute-start(bf16[192,512]{1,0:T(8,128)(2,1)S(1)} %get-tuple-element.56.refs_9_), channel_id=1, source_target_pairs={{0,2},{1,3},{2,0},{3,1},{4,6},{5,7},{6,4},{7,5},{8,10},{9,11},{10,... | collective-permute-start | bytes 589832 | tf_op jit(solution)/shard_map/ppermute | solution.py:577
  43.5 4.7 %shard_map.144 = (bf16[192,512]{1,0:T(8,128)(2,1)S(1)}, f32[8,512]{1,0:T(8,128)S(1)}) custom-call(bf16[576,1024]{1,0:T(8,128)(2,1)S(1)} %get-tuple-element.50.qkv.refs_9_), custom_call_target="tpu_custom_call" | custom-call | tf_op jit(solution)/shard_map/pallas_call | solution.py:272
  48.2 1.0 copy-done
  49.3 1.7 %collective-permute-done.18.refs_11_ = bf16[192,512]{1,0:T(8,128)(2,1)S(1)} collective-permute-done((bf16[192,512]{1,0:T(8,128)(2,1)S(1)}, bf16[192,512]{1,0:T(8,128)(2,1)S(1)}, u32[]{:S(2)}, u32[]{:S(2)}) %collective-permute-start.18) | collective-permute-done | bytes 196640 | tf_op jit(solution)/shard_map/ppermute | solution.py:577
  53.4 1.5 %collective-permute-start.25 = (bf16[192,512]{1,0:T(8,128)(2,1)S(1)}, bf16[192,512]{1,0:T(8,128)(2,1)S(1)}, u32[]{:S(2)}, u32[]{:S(2)}) collective-permute-start(bf16[192,512]{1,0:T(8,128)(2,1)S(1)} %get-tuple-element.51.refs_1_), channel_id=1, source_target_pairs={{0,2},{1,3},{2,0},{3,1},{4,6},{5,7},{6,4},{7,5},{8,10},{9,11},{10,... | collective-permute-start | bytes 589832 | tf_op jit(solution)/shard_map/ppermute | solution.py:577
  55.6 8.9 %shard_map.145 = (bf16[1024,768]{1,0:T(8,128)(2,1)S(1)}, bf16[768,768]{1,0:T(8,128)(2,1)S(1)}, bf16[1152,768]{1,0:T(8,128)(2,1)S(1)}, bf16[576,768]{1,0:T(8,128)...) custom-call(s32[4]{0:T(128)S(1)} %pad_add_fusion.place, ...), custom_call_target="tpu_custom_call" | custom-call | flops 2868903936 | bytes 7965712 | tf_op jit(solution)/shard_map/pallas_call | solution.py:272
  67.5 7.2 %shard_map.146 = (f32[512,768]{1,0:T(8,128)S(1)}, bf16[512,768]{1,0:T(8,128)(2,1)S(1)}, bf16[288,512]{1,0:T(8,128)(2,1)S(1)}, bf16[576,512]{1,0:T(8,128)(2,1)S(1...) custom-call(s32[4]{0:T(128)S(1)} %pad_add_fusion.place, bf16[512,768]{1,0:T(8,128)(2,1)S(1)} %get-tuple-element.60.tok_in, ...), custom_call_target="tpu_custom_call" | custom-call | flops 2868903936 | bytes 6982672 | tf_op jit(solution)/shard_map/pallas_call | solution.py:272
  76.9 1.8 %convolution_add_fusion = f32[576,768]{1,0:T(8,128)} fusion(f32[576,768]{1,0:T(8,128)S(1)} %fusion.29, bf16[576,512]{1,0:T(8,128)(2,1)S(1)} %get-tuple-element.82, bf16[512,768]{1,0:T(8,128)(2,1)S(1)} %get-tuple-element.83), kind=kOutput, calls=%fused_computation.1 | convolution fusion | flops 453427200 | bytes 4915200 | tf_op jit(solution)/shard_map/dot_general | solution.py:233
  78.8 18.1 %shard_map.147 = (f32[1,768]{1,0:T(1,128)S(1)}, bf16[1024,768]{1,0:T(8,128)(2,1)S(1)}, f32[128,768]{1,0:T(8,128)S(1)}, bf16[576,1024]{1,0:T(8,128)(2,1)S(1)}, bf16[128,768]{1,0:T(8,128)(2,1)}) custom-call(s32[4]{0:T(128)S(1)} %pad_add_fusion.place, f32[512,768]{1,0:T(8,128)S(1)} %get-tuple-element.59.refs_0_, f32[512,768]{1,0:T(8,128)S(1)} %get-tuple-element.66.refs_1_, ...), custom_call_target="tpu_custom_call" | custom-call | flops 8355053568 | bytes 10521616 | tf_op jit(solution)/shard_map/pallas_call | solution.py:272
  97.3 2.3 %multiply_reduce_fusion = (f32[768]{0:T(1024)S(1)}, f32[576,768]{1,0:T(8,128)}) fusion(bf16[768,3,192]{0,2,1:T(8,128)(2,1)S(1)} %copy-done.2, bf16[576,1024]{1,0:T(8,128)(2,1)S(1)} %get-tuple-element.78, bf16[1024,768]{1,0:T(8,128)(2,1)S(1)} %copy-done.16), kind=kOutput, calls=%fused_computation | convolution fusion | flops 907296000 | bytes 5409792 | tf_op jit(solution)/shard_map/dot_general | solution.py:233
  101.4 1.3 %fusion.13 = f32[192,768]{1,0:T(8,128)} fusion(bf16[1024,768]{1,0:T(8,128)(2,1)S(1)} %get-tuple-element.80, bf16[192,512]{1,0:T(8,128)(2,1)S(1)} %copy-done.12, bf16[192,512]{1,0:T(8,128)(2,1)S(1)} %copy-done.10), kind=kOutput, calls=%fused_computation.19 | convolution fusion | flops 302776320 | bytes 2555904 | tf_op jit(solution)/shard_map/dot_general | solution.py:233
  102.7 1.1 add_convert_fusion.1
  105.0 1.3 %convolution_add_fusion.1 = f32[288,768]{1,0:T(8,128)} fusion(f32[288,768]{1,0:T(8,128)S(1)} %fusion, bf16[288,512]{1,0:T(8,128)(2,1)S(1)} %copy-done.6, bf16[1024,768]{1,0:T(8,128)(2,1)S(1)} %get-tuple-element.61.refs_0_.refs_6_), kind=kOutput, calls=%fused_computation.3 | convolution fusion | flops 226713600 | bytes 2850816 | tf_op jit(solution)/shard_map/dot_general | solution.py:233
  106.3 2.1 %add_convert_fusion = bf16[128,768]{1,0:T(8,128)(2,1)} fusion(bf16[128,768]{1,0:T(8,128)(2,1)} %collective-permute-done.27, bf16[128,768]{1,0:T(8,128)(2,1)} %broadcast_select_fusion, f32[512,768]{1,0:T(8,128)} %copy-done.14, s32[]{:T(128)S(6)} %select_n.42, f32[512,768]{1,0:T(8,128)} %copy-done.13, pred[]{:T(512)S(6)} %lt.22), kind=kLoop, calls=%fused_computation.24 | loop fusion | flops 589824 | bytes 1376261 | tf_op jit(solution)/shard_map/convert_element_type | solution.py:804
  108.4 3.6 %collective-permute-done.31 = bf16[144,768]{1,0:T(8,128)(2,1)S(1)} collective-permute-done((bf16[144,768]{1,0:T(8,128)(2,1)S(1)}, bf16[144,768]{1,0:T(8,128)(2,1)S(1)}, u32[]{:S(2)}, u32[]{:S(2)}) %collective-permute-start.31) | collective-permute-done | bytes 221216 | tf_op jit(solution)/shard_map/ppermute | solution.py:577
  (186 shorter events, 16.7 us)
Async XLA Ops:
  1.6 11.9 %collective-permute-start.2 = (bf16[64,768]{1,0:T(8,128)(2,1)S(1)}, bf16[64,768]{1,0:T(8,128)(2,1)S(1)}, u32[]{:S(2)}, u32[]{:S(2)}) collective-permute-start(bf16[64,768]{1,0:T(8,128)(2,1)S(1)} %constant_dynamic-slice_fusion.1), channel_id=1, source_target_pairs={{0,16},{4,20},{8,24},{12,28},{16,0},{20,4},{24,8},{28,12},{1,17},{... | collective-permute-start | bytes 294920 | tf_op jit(solution)/shard_map/ppermute | solution.py:573
  5.6 7.9 %collective-permute-start.3 = (bf16[64,768]{1,0:T(8,128)(2,1)S(1)}, bf16[64,768]{1,0:T(8,128)(2,1)S(1)}, u32[]{:S(2)}, u32[]{:S(2)}) collective-permute-start(bf16[64,768]{1,0:T(8,128)(2,1)S(1)} %constant_dynamic-slice_fusion.1), channel_id=1, source_target_pairs={{0,24},{4,28},{8,16},{12,20},{16,8},{20,12},{24,0},{28,4},{1,25},{... | collective-permute-start | bytes 294920 | tf_op jit(solution)/shard_map/ppermute | solution.py:573
  6.9 12.3 %collective-permute-start = (bf16[64,768]{1,0:T(8,128)(2,1)S(1)}, bf16[64,768]{1,0:T(8,128)(2,1)S(1)}, u32[]{:S(2)}, u32[]{:S(2)}) collective-permute-start(bf16[64,768]{1,0:T(8,128)(2,1)S(1)} %constant_dynamic-slice_fusion.1), channel_id=1, source_target_pairs={{0,8},{4,12},{8,0},{12,4},{16,24},{20,28},{24,16},{28,20},{1,9},{5... | collective-permute-start | bytes 294920 | tf_op jit(solution)/shard_map/ppermute | solution.py:573
  8.1 12.4 %collective-permute-start.9 = (bf16[64,768]{1,0:T(8,128)(2,1)S(1)}, bf16[64,768]{1,0:T(8,128)(2,1)S(1)}, u32[]{:S(2)}, u32[]{:S(2)}) collective-permute-start(bf16[64,768]{1,0:T(8,128)(2,1)S(1)} %constant_dynamic-slice_fusion), channel_id=1, source_target_pairs={{0,4},{4,0},{8,12},{12,8},{16,20},{20,16},{24,28},{28,24},{1,5},{5... | collective-permute-start | bytes 294920 | tf_op jit(solution)/shard_map/ppermute | solution.py:573
  9.6 8.1 %collective-permute-start.21 = (bf16[192,768]{1,0:T(8,128)(2,1)}, bf16[192,768]{1,0:T(8,128)(2,1)S(1)}, u32[]{:S(2)}, u32[]{:S(2)}) collective-permute-start(bf16[192,768]{1,0:T(8,128)(2,1)} %refs_8_.1), channel_id=1, source_target_pairs={{0,2},{1,3},{2,0},{3,1},{4,6},{5,7},{6,4},{7,5},{8,10},{9,11},{10,... | collective-permute-start | bytes 884744 | tf_op jit(solution)/shard_map/ppermute | solution.py:577
  13.5 7.5 %collective-permute-start.4 = (bf16[2,64,768]{2,1,0:T(8,128)(2,1)S(1)}, bf16[2,64,768]{2,1,0:T(8,128)(2,1)S(1)}, u32[]{:S(2)}, u32[]{:S(2)}) collective-permute-start(bf16[2,64,768]{2,1,0:T(8,128)(2,1)S(1)} %pad_maximum_fusion.3.refs_2_), channel_id=1, source_target_pairs={{0,4},{4,0},{8,12},{12,8},{16,20},{20,16},{24,28},{28,24},{1,5},{5... | collective-permute-start | bytes 589832 | tf_op jit(solution)/shard_map/ppermute | solution.py:573
  17.7 37.2 %collective-permute-start.23 = (bf16[864,768]{1,0:T(8,128)(2,1)S(1)}, bf16[864,768]{1,0:T(8,128)(2,1)}, u32[]{:S(2)}, u32[]{:S(2)}) collective-permute-start(bf16[864,768]{1,0:T(8,128)(2,1)S(1)} %pad_maximum_fusion.refs_17_), channel_id=1, source_target_pairs={{0,2},{1,3},{2,0},{3,1},{4,6},{5,7},{6,4},{7,5},{8,10},{9,11},{10,... | collective-permute-start | bytes 3981320 | tf_op jit(solution)/shard_map/ppermute | solution.py:577
  19.3 5.7 %collective-permute-start.1 = (bf16[2,64,768]{2,1,0:T(8,128)(2,1)S(1)}, bf16[2,64,768]{2,1,0:T(8,128)(2,1)S(1)}, u32[]{:S(2)}, u32[]{:S(2)}) collective-permute-start(bf16[2,64,768]{2,1,0:T(8,128)(2,1)S(1)} %pad_maximum_fusion.2.refs_0_), channel_id=1, source_target_pairs={{0,4},{4,0},{8,12},{12,8},{16,20},{20,16},{24,28},{28,24},{1,5},{5... | collective-permute-start | bytes 589832 | tf_op jit(solution)/shard_map/ppermute | solution.py:573
  20.4 4.6 %collective-permute-start.7 = (bf16[2,64,768]{2,1,0:T(8,128)(2,1)S(1)}, bf16[2,64,768]{2,1,0:T(8,128)(2,1)S(1)}, u32[]{:S(2)}, u32[]{:S(2)}) collective-permute-start(bf16[2,64,768]{2,1,0:T(8,128)(2,1)S(1)} %pad_maximum_fusion.3.refs_2_), channel_id=1, source_target_pairs={{0,1},{1,0},{2,3},{3,2},{4,5},{5,4},{6,7},{7,6},{8,9},{9,8},{10,11... | collective-permute-start | bytes 589832 | tf_op jit(solution)/shard_map/ppermute | solution.py:577
  20.5 6.3 %collective-permute-start.5 = (bf16[2,64,768]{2,1,0:T(8,128)(2,1)S(1)}, bf16[2,64,768]{2,1,0:T(8,128)(2,1)S(1)}, u32[]{:S(2)}, u32[]{:S(2)}) collective-permute-start(bf16[2,64,768]{2,1,0:T(8,128)(2,1)S(1)} %pad_maximum_fusion.2.refs_0_), channel_id=1, source_target_pairs={{0,1},{1,0},{2,3},{3,2},{4,5},{5,4},{6,7},{7,6},{8,9},{9,8},{10,11... | collective-permute-start | bytes 589832 | tf_op jit(solution)/shard_map/ppermute | solution.py:577
  21.0 7.8 %collective-permute-start.8 = (bf16[2,64,768]{2,1,0:T(8,128)(2,1)S(1)}, bf16[2,64,768]{2,1,0:T(8,128)(2,1)S(1)}, u32[]{:S(2)}, u32[]{:S(2)}) collective-permute-start(bf16[2,64,768]{2,1,0:T(8,128)(2,1)S(1)} %collective-permute-done.4.refs_3_), channel_id=1, source_target_pairs={{0,1},{1,0},{2,3},{3,2},{4,5},{5,4},{6,7},{7,6},{8,9},{9,8},{10,11... | collective-permute-start | bytes 589832 | tf_op jit(solution)/shard_map/ppermute | solution.py:577
  25.0 5.3 %collective-permute-start.6 = (bf16[2,64,768]{2,1,0:T(8,128)(2,1)S(1)}, bf16[2,64,768]{2,1,0:T(8,128)(2,1)S(1)}, u32[]{:S(2)}, u32[]{:S(2)}) collective-permute-start(bf16[2,64,768]{2,1,0:T(8,128)(2,1)S(1)} %collective-permute-done.1.refs_1_), channel_id=1, source_target_pairs={{0,1},{1,0},{2,3},{3,2},{4,5},{5,4},{6,7},{7,6},{8,9},{9,8},{10,11... | collective-permute-start | bytes 589832 | tf_op jit(solution)/shard_map/ppermute | solution.py:577
  25.1 17.9 %collective-permute-start.10 = (bf16[2,64,768]{2,1,0:T(8,128)(2,1)S(1)}, bf16[2,64,768]{2,1,0:T(8,128)(2,1)S(1)}, u32[]{:S(2)}, u32[]{:S(2)}) collective-permute-start(bf16[2,64,768]{2,1,0:T(8,128)(2,1)S(1)} %pad_maximum_fusion.4.refs_1_), channel_id=1, source_target_pairs={{0,8},{4,12},{8,0},{12,4},{16,24},{20,28},{24,16},{28,20},{1,9},{5... | collective-permute-start | bytes 589832 | tf_op jit(solution)/shard_map/ppermute | solution.py:573
  26.8 16.3 %collective-permute-start.11 = (bf16[2,64,768]{2,1,0:T(8,128)(2,1)S(1)}, bf16[2,64,768]{2,1,0:T(8,128)(2,1)}, u32[]{:S(2)}, u32[]{:S(2)}) collective-permute-start(bf16[2,64,768]{2,1,0:T(8,128)(2,1)S(1)} %pad_maximum_fusion.4.refs_1_), channel_id=1, source_target_pairs={{0,16},{4,20},{8,24},{12,28},{16,0},{20,4},{24,8},{28,12},{1,17},{... | collective-permute-start | bytes 589832 | tf_op jit(solution)/shard_map/ppermute | solution.py:573
  28.9 20.4 %collective-permute-start.12 = (bf16[2,64,768]{2,1,0:T(8,128)(2,1)S(1)}, bf16[2,64,768]{2,1,0:T(8,128)(2,1)}, u32[]{:S(2)}, u32[]{:S(2)}) collective-permute-start(bf16[2,64,768]{2,1,0:T(8,128)(2,1)S(1)} %pad_maximum_fusion.4.refs_1_), channel_id=1, source_target_pairs={{0,24},{4,28},{8,16},{12,20},{16,8},{20,12},{24,0},{28,4},{1,25},{... | collective-permute-start | bytes 589832 | tf_op jit(solution)/shard_map/ppermute | solution.py:573
  41.5 9.6 %collective-permute-start.18 = (bf16[192,512]{1,0:T(8,128)(2,1)S(1)}, bf16[192,512]{1,0:T(8,128)(2,1)S(1)}, u32[]{:S(2)}, u32[]{:S(2)}) collective-permute-start(bf16[192,512]{1,0:T(8,128)(2,1)S(1)} %get-tuple-element.56.refs_9_), channel_id=1, source_target_pairs={{0,2},{1,3},{2,0},{3,1},{4,6},{5,7},{6,4},{7,5},{8,10},{9,11},{10,... | collective-permute-start | bytes 589832 | tf_op jit(solution)/shard_map/ppermute | solution.py:577
  43.0 8.2 %collective-permute-start.20 = (bf16[192,768]{1,0:T(8,128)(2,1)S(1)}, bf16[192,768]{1,0:T(8,128)(2,1)S(1)}, u32[]{:S(2)}, u32[]{:S(2)}) collective-permute-start(bf16[192,768]{1,0:T(8,128)(2,1)S(1)} %copy-done.17), channel_id=1, source_target_pairs={{0,1},{1,0},{2,3},{3,2},{4,5},{5,4},{6,7},{7,6},{8,9},{9,8},{10,11... | collective-permute-start | bytes 884744 | tf_op jit(solution)/shard_map/ppermute | solution.py:577
  43.1 8.7 %collective-permute-start.22 = (bf16[192,768]{1,0:T(8,128)(2,1)S(1)}, bf16[192,768]{1,0:T(8,128)(2,1)S(1)}, u32[]{:S(2)}, u32[]{:S(2)}) collective-permute-start(bf16[192,768]{1,0:T(8,128)(2,1)S(1)} %copy-done.40), channel_id=1, source_target_pairs={{0,1},{1,0},{2,3},{3,2},{4,5},{5,4},{6,7},{7,6},{8,9},{9,8},{10,11... | collective-permute-start | bytes 884744 | tf_op jit(solution)/shard_map/ppermute | solution.py:577
  49.2 2.6 %collective-permute-start.13 = (bf16[2,64,768]{2,1,0:T(8,128)(2,1)S(1)}, bf16[2,64,768]{2,1,0:T(8,128)(2,1)S(1)}, u32[]{:S(2)}, u32[]{:S(2)}) collective-permute-start(bf16[2,64,768]{2,1,0:T(8,128)(2,1)S(1)} %pad_maximum_fusion.4.refs_1_), channel_id=1, source_target_pairs={{0,1},{1,0},{2,3},{3,2},{4,5},{5,4},{6,7},{7,6},{8,9},{9,8},{10,11... | collective-permute-start | bytes 589832 | tf_op jit(solution)/shard_map/ppermute | solution.py:577
  51.0 1.4 %collective-permute-start.14 = (bf16[2,64,768]{2,1,0:T(8,128)(2,1)S(1)}, bf16[2,64,768]{2,1,0:T(8,128)(2,1)S(1)}, u32[]{:S(2)}, u32[]{:S(2)}) collective-permute-start(bf16[2,64,768]{2,1,0:T(8,128)(2,1)S(1)} %collective-permute-done.10.refs_2_), channel_id=1, source_target_pairs={{0,1},{1,0},{2,3},{3,2},{4,5},{5,4},{6,7},{7,6},{8,9},{9,8},{10,11... | collective-permute-start | bytes 589832 | tf_op jit(solution)/shard_map/ppermute | solution.py:577
  51.2 3.7 %collective-permute-start.17 = (bf16[192,512]{1,0:T(8,128)(2,1)S(1)}, bf16[192,512]{1,0:T(8,128)(2,1)S(1)}, u32[]{:S(2)}, u32[]{:S(2)}) collective-permute-start(bf16[192,512]{1,0:T(8,128)(2,1)S(1)} %get-tuple-element.56.refs_9_), channel_id=1, source_target_pairs={{0,1},{1,0},{2,3},{3,2},{4,5},{5,4},{6,7},{7,6},{8,9},{9,8},{10,11... | collective-permute-start | bytes 589832 | tf_op jit(solution)/shard_map/ppermute | solution.py:577
  51.8 1.7 %collective-permute-start.15 = (bf16[2,64,768]{2,1,0:T(8,128)(2,1)}, bf16[2,64,768]{2,1,0:T(8,128)(2,1)S(1)}, u32[]{:S(2)}, u32[]{:S(2)}) collective-permute-start(bf16[2,64,768]{2,1,0:T(8,128)(2,1)} %collective-permute-done.11.refs_3_), channel_id=1, source_target_pairs={{0,1},{1,0},{2,3},{3,2},{4,5},{5,4},{6,7},{7,6},{8,9},{9,8},{10,11... | collective-permute-start | bytes 589832 | tf_op jit(solution)/shard_map/ppermute | solution.py:577
  51.9 3.1 %collective-permute-start.16 = (bf16[2,64,768]{2,1,0:T(8,128)(2,1)}, bf16[2,64,768]{2,1,0:T(8,128)(2,1)}, u32[]{:S(2)}, u32[]{:S(2)}) collective-permute-start(bf16[2,64,768]{2,1,0:T(8,128)(2,1)} %collective-permute-done.12.refs_4_), channel_id=1, source_target_pairs={{0,1},{1,0},{2,3},{3,2},{4,5},{5,4},{6,7},{7,6},{8,9},{9,8},{10,11... | collective-permute-start | bytes 589832 | tf_op jit(solution)/shard_map/ppermute | solution.py:577
  52.5 2.5 %collective-permute-start.19 = (bf16[192,512]{1,0:T(8,128)(2,1)S(1)}, bf16[192,512]{1,0:T(8,128)(2,1)}, u32[]{:S(2)}, u32[]{:S(2)}) collective-permute-start(bf16[192,512]{1,0:T(8,128)(2,1)S(1)} %collective-permute-done.18.refs_11_), channel_id=1, source_target_pairs={{0,1},{1,0},{2,3},{3,2},{4,5},{5,4},{6,7},{7,6},{8,9},{9,8},{10,11... | collective-permute-start | bytes 589832 | tf_op jit(solution)/shard_map/ppermute | solution.py:577
  53.4 11.8 %collective-permute-start.25 = (bf16[192,512]{1,0:T(8,128)(2,1)S(1)}, bf16[192,512]{1,0:T(8,128)(2,1)S(1)}, u32[]{:S(2)}, u32[]{:S(2)}) collective-permute-start(bf16[192,512]{1,0:T(8,128)(2,1)S(1)} %get-tuple-element.51.refs_1_), channel_id=1, source_target_pairs={{0,2},{1,3},{2,0},{3,1},{4,6},{5,7},{6,4},{7,5},{8,10},{9,11},{10,... | collective-permute-start | bytes 589832 | tf_op jit(solution)/shard_map/ppermute | solution.py:577
  54.9 11.5 %collective-permute-start.24 = (bf16[192,512]{1,0:T(8,128)(2,1)S(1)}, bf16[192,512]{1,0:T(8,128)(2,1)S(1)}, u32[]{:S(2)}, u32[]{:S(2)}) collective-permute-start(bf16[192,512]{1,0:T(8,128)(2,1)S(1)} %get-tuple-element.51.refs_1_), channel_id=1, source_target_pairs={{0,1},{1,0},{2,3},{3,2},{4,5},{5,4},{6,7},{7,6},{8,9},{9,8},{10,11... | collective-permute-start | bytes 589832 | tf_op jit(solution)/shard_map/ppermute | solution.py:577
  65.2 1.6 %collective-permute-start.26 = (bf16[192,512]{1,0:T(8,128)(2,1)S(1)}, bf16[192,512]{1,0:T(8,128)(2,1)S(1)}, u32[]{:S(2)}, u32[]{:S(2)}) collective-permute-start(bf16[192,512]{1,0:T(8,128)(2,1)S(1)} %collective-permute-done.25.refs_3_), channel_id=1, source_target_pairs={{0,1},{1,0},{2,3},{3,2},{4,5},{5,4},{6,7},{7,6},{8,9},{9,8},{10,11... | collective-permute-start | bytes 589832 | tf_op jit(solution)/shard_map/ppermute | solution.py:577
  66.4 12.4 %collective-permute-start.28 = (bf16[512,768]{1,0:T(8,128)(2,1)S(1)}, bf16[512,768]{1,0:T(8,128)(2,1)S(1)}, u32[]{:S(2)}, u32[]{:S(2)}) collective-permute-start(bf16[512,768]{1,0:T(8,128)(2,1)S(1)} %get-tuple-element.71.refs_2_), channel_id=1, source_target_pairs={{0,1},{1,0},{2,3},{3,2},{4,5},{5,4},{6,7},{7,6},{8,9},{9,8},{10,11... | collective-permute-start | bytes 2359304 | tf_op jit(solution)/shard_map/ppermute | solution.py:577
  74.8 4.0 %collective-permute-start.29 = (bf16[512,768]{1,0:T(8,128)(2,1)S(1)}, bf16[512,768]{1,0:T(8,128)(2,1)S(1)}, u32[]{:S(2)}, u32[]{:S(2)}) collective-permute-start(bf16[512,768]{1,0:T(8,128)(2,1)S(1)} %get-tuple-element.72.refs_3_), channel_id=1, source_target_pairs={{0,1},{1,0},{2,3},{3,2},{4,5},{5,4},{6,7},{7,6},{8,9},{9,8},{10,11... | collective-permute-start | bytes 2359304 | tf_op jit(solution)/shard_map/ppermute | solution.py:577
  76.0 27.8 %collective-permute-start.27 = (bf16[128,768]{1,0:T(8,128)(2,1)}, bf16[128,768]{1,0:T(8,128)(2,1)}, u32[]{:S(2)}, u32[]{:S(2)}) collective-permute-start(bf16[128,768]{1,0:T(8,128)(2,1)} %broadcast_select_fusion), channel_id=1, source_target_pairs={{0,1},{1,0},{2,3},{3,2},{4,5},{5,4},{6,7},{7,6},{8,9},{9,8},{10,11... | collective-permute-start | bytes 589832 | tf_op jit(solution)/shard_map/ppermute | solution.py:577
  97.0 5.7 %collective-permute-start.30 = (bf16[128,768]{1,0:T(8,128)(2,1)}, bf16[128,768]{1,0:T(8,128)(2,1)}, u32[]{:S(2)}, u32[]{:S(2)}) collective-permute-start(bf16[128,768]{1,0:T(8,128)(2,1)} %get-tuple-element.75), channel_id=1, source_target_pairs={{0,1},{1,0},{2,3},{3,2},{4,5},{5,4},{6,7},{7,6},{8,9},{9,8},{10,11... | collective-permute-start | bytes 589832 | tf_op jit(solution)/shard_map/ppermute | solution.py:577
  104.3 7.6 %collective-permute-start.31 = (bf16[144,768]{1,0:T(8,128)(2,1)S(1)}, bf16[144,768]{1,0:T(8,128)(2,1)S(1)}, u32[]{:S(2)}, u32[]{:S(2)}) collective-permute-start(bf16[144,768]{1,0:T(8,128)(2,1)S(1)} %pad_maximum_fusion.1), channel_id=1, source_target_pairs={{0,2},{1,3},{2,0},{3,1},{4,6},{5,7},{6,4},{7,5},{8,10},{9,11},{10,... | collective-permute-start | bytes 663560 | tf_op jit(solution)/shard_map/ppermute | solution.py:577
  (53 other events, 378.4 us)

commit v3 on v2

--- a/solution.py
+++ b/solution.py
@@ -234,9 +234,14 @@
 
 
 def norm_parts(values):
-    center = values - jnp.mean(values, axis=-1, keepdims=True)
+    return norm_stats(values)[:2]
+
+
+def norm_stats(values):
+    mean = jnp.mean(values, axis=-1, keepdims=True)
+    center = values - mean
     scale = lax.rsqrt(jnp.mean(center * center, axis=-1, keepdims=True) + norm_epsilon)
-    return center * scale, scale
+    return center * scale, scale, mean
 
 
 def norm_back(grad, normed, scale):
@@ -340,7 +345,7 @@
     return pl.ds(pl.multiple_of(i * size, size), size)
 
 
-def attend(heads, first, qkv, att, lse, keys, chunk=256):
+def attend(heads, first, qkv, att, exact, lse, keys, chunk=256):
     def one_head(head):
         keys[...] = qkv[part_of(heads + head, HEAD), :].T
         rows = part_of(head, HEAD)
@@ -352,7 +357,9 @@
             exponent = jnp.exp(scores - top)
             total = jnp.sum(exponent, axis=0, keepdims=True)
             weighted = mm(qkv[part_of(2 * heads + head, HEAD), :], exponent.astype(BF16))
-            att[rows, at] = (weighted / total).astype(BF16)
+            weighted = weighted / total
+            exact[rows, at] = weighted
+            att[rows, at] = weighted.astype(BF16)
             lse[pl.ds(head, 1), at] = top + jnp.log(total)
 
         loop(att.shape[1] // chunk, one_chunk, att.shape[1] // chunk)
@@ -364,7 +371,7 @@
 def project_kernel(heads, ids, place, own, *refs):
     count = len(ids)
     near, far, refs = refs[:count], refs[count : 2 * count], refs[2 * count :]
-    gain, weight_in, cosine, sine, tok_out, first, qkv, att, lse, tok, weight, keys, sems = refs
+    gain, weight_in, cosine, sine, tok_out, first, qkv, att, exact, lse, tok, weight, keys, sems = refs
     move = Mover(sems)
     local = heads * HEAD
     tokens = tok.shape[0]
@@ -396,12 +403,12 @@
         qkv[2 * local :, at] = raw[2 * local :].astype(BF16)
 
     loop(tokens // chunk, one_chunk, 2)
-    attend(heads, 0, qkv, att, lse, keys)
+    attend(heads, 0, qkv, att, exact, lse, keys)
     move.finish()
 
 
-def queries_kernel(heads, qkv, att, lse, keys):
-    attend(heads, qkv.shape[1] - att.shape[1], qkv, att, lse, keys)
+def queries_kernel(heads, qkv, att, exact, lse, keys):
+    attend(heads, qkv.shape[1] - att.shape[1], qkv, att, exact, lse, keys)
 
 
 def cdf_terms(gate):
@@ -415,12 +422,15 @@
     if turn == 0:
         cot_own, near, far = refs[0], refs[1 : 1 + count], refs[1 + count : 1 + 2 * count]
         refs = refs[1 + 2 * count :]
-        atts, attns, mlp_own, mlp_far = refs[:4], refs[4:8], refs[8], refs[9]
-        gain, cot, attn, w_in, w_mlp, tok_next = refs[10:16]
-        refs = refs[16:]
+        atts, attns, (in_own, in_far, mlp_own, rest_far) = refs[:4], refs[4:7], refs[7:11]
+        attns = [*attns[:2], rest_far.at[mlp_own.shape[0] :, :], attns[2]]
+        gain, cot, attn, w_in, w_mlp, tok_next = refs[11:17]
+        refs = refs[17:]
     else:
         cot, atts, (gain, attn, w_in, w_mlp), refs = refs[0], refs[1:5], refs[5:9], refs[9:]
-    middle_ref, second_ref, hidden_ref, gate_ref, part_ref, out_ref = refs[:6]
+        (mid_before, out_before), refs = refs[:2], refs[2:]
+    middle_ref, second_ref, hidden_ref, gate_ref, part_ref, mean_ref, scale_ref = refs[:7]
+    mid_ref, out_ref, refs = refs[7], refs[8], refs[9:]
     tokens = middle_ref.shape[0]
     sems = refs[-1]
     move = Mover(sems)
@@ -430,11 +440,11 @@
     begin = turn * tokens
     first_loads = []
     if turn == 0:
-        tok, refs = refs[6], refs[:6] + refs[7:]
+        tok, refs = refs[0], refs[1:]
         first_loads.append(move.load(tok_in.at[:tokens, :], tok))
     else:
         tok = tok_in
-    att, hidden_v, gate_v = refs[6:9]
+    att, hidden_v, gate_v = refs[:3]
     for p in range(4):
         spot = pl.ds(pl.multiple_of(jnp.bitwise_xor(quarter, p) * local, local), local)
         first_loads.append(move.load(atts[p], att.at[spot, :]))
@@ -442,11 +452,14 @@
             first_loads.append(move.load(attns[p], attn.at[spot, :]))
     in_loads, mlp_loads = [], []
     if turn == 0:
-        for source, r in ((mlp_own, side), (mlp_far, 1 - side)):
-            for part, target in ((0, w_in), (1, w_in), (2, w_mlp)):
-                spot = pl.ds(pl.multiple_of((r + 2 * (part % 2)) * units, units), units)
+        for source, r in ((in_own, side), (in_far, 1 - side)):
+            for part in range(2):
+                spot = pl.ds(pl.multiple_of((r + 2 * part) * units, units), units)
                 rows = source.at[part * units : (part + 1) * units, :]
-                (mlp_loads if part == 2 else in_loads).append(move.load(rows, target.at[spot, :]))
+                in_loads.append(move.load(rows, w_in.at[spot, :]))
+        for source, r in ((mlp_own, side), (rest_far, 1 - side)):
+            spot = pl.ds(pl.multiple_of(r * units, units), units)
+            mlp_loads.append(move.load(source.at[:units, :], w_mlp.at[spot, :]))
         mlp_loads += load_pieces(move, place, cot, cot_own, near, far, ids)
         mlp_loads.append(move.load(tok_in.at[tokens:, :], tok_next))
     wait_all(first_loads)
@@ -456,7 +469,7 @@
         at = part_of(i, chunk)
         middle = tok[at, :].astype(F32) + mm(att[:, at].T, attn[...])
         middle_ref[at, :] = middle
-        normed, _ = norm_parts(middle)
+        normed, scale_ref[at, :], mean_ref[at, :] = norm_stats(middle)
         second = (normed * gain[...]).astype(BF16)
         second_ref[at, :] = second
 
@@ -485,19 +498,36 @@
     gate_ref[units:, :] = gate_v[mine_up, :]
     rows = out_ref.shape[0]
     spots = tokens // rows
-    out_ref[...] = jnp.zeros_like(out_ref)
+    mid_ref[...] = mid_before[...] if turn else jnp.zeros_like(mid_ref)
+    out_ref[...] = out_before[...] if turn else jnp.zeros_like(out_ref)
 
     @pl.when(here // spots == turn)
     def _():
         own = pl.ds(pl.multiple_of((here - turn * spots) * rows, rows), rows)
+        mid_ref[...] = middle_ref[own, :]
         out_ref[...] = mm(hidden_v[:, own].T, w_mlp[...]).astype(BF16)
 
 
+def two_rows(row):
+    high = row.astype(BF16).astype(F32)
+    spots = lax.broadcasted_iota(jnp.int32, (16, row.shape[1]), 0)
+    rows = jnp.where(spots == 0, high, jnp.where(spots == 1, row - high, 0.0))
+    return rows.astype(BF16)
+
+
+def sum_rows(rows):
+    return jnp.sum(rows.astype(F32), axis=0, keepdims=True)
+
+
 def back_kernel(heads, place, *refs):
-    middles, parts, fars, refs = refs[:2], refs[2:4], refs[4:6], refs[6:]
+    middles, means, scales, refs = refs[:2], refs[2:4], refs[4:6], refs[6:]
+    parts, fars, refs = refs[:2], refs[2:4], refs[4:]
     cot, gain, attn, qkv, refs = refs[0], refs[1], refs[2], refs[3], refs[4:]
-    lses, weight, cosine, sine, refs = refs[:2], refs[2], refs[3], refs[4], refs[5:]
-    gain_v, branch, own_v, grad_v, first_v, back_rows, lse, keys, values, key_grad, value_grad = refs
+    exacts, lses, refs = refs[:2], refs[2:4], refs[4:]
+    weight, cosine, sine, refs = refs[0], refs[1], refs[2], refs[3:]
+    first_in, first_gain, gain_v, branch, own_v, message, qkv_out, refs = *refs[:7], refs[7:]
+    grad_v, back_rows, lse, keys, values, key_grad, value_grad, qkv_grad, sems = refs
+    move = Mover(sems)
     here = place[0]
     turns = middles[0].shape[0]
     tokens = 2 * turns
@@ -510,7 +540,8 @@
         here_at = pl.ds(pl.multiple_of(b * rows, rows), rows)
         at = pl.ds(pl.multiple_of((b + turn * spots) * rows, rows), rows)
         second = parts[turn][here_at, :].astype(F32) + fars[turn][here_at, :].astype(F32)
-        normed, scale = norm_parts(middles[turn][here_at, :])
+        scale = scales[turn][here_at, :]
+        normed = (middles[turn][here_at, :] - means[turn][here_at, :]) * scale
         gain_v[...] += jnp.sum(second * normed, axis=0, keepdims=True)
         grad = cot[at, :].astype(F32) + norm_back(second * gain[...], normed, scale)
         branch[at, :] = grad.astype(BF16)
@@ -553,7 +584,8 @@
             out_grad = back_rows[rows_q, at]
             chances = jnp.exp(mm(keys[...], query) - lse[pl.ds(head, 1), at])
             chance_grad = mm(values[...], out_grad)
-            delta = jnp.sum(chances * chance_grad, axis=0, keepdims=True)
+            exact = exacts[i * chunk // turns][rows_q, part_of(i % (turns // chunk), chunk)]
+            delta = jnp.sum(out_grad.astype(F32) * exact, axis=0, keepdims=True)
             score_grad = (chances * (chance_grad - delta)).astype(BF16)
             query_grad = mm(qkv[rows_k, :], score_grad) * scale
             key_grad[...] += mm(score_grad, query.T)
@@ -566,7 +598,55 @@
 
     loop(heads, one_head)
     own = pl.ds(pl.multiple_of(here * rows, rows), rows)
-    first_v[...] = mm(grad_v[:, own].T, weight[...]).astype(BF16)
+    message[:rows, :] = mm(grad_v[:, own].T, weight[...]).astype(BF16)
+    gain_row = jnp.zeros_like(gain_v)
+    for part in range(3):
+        at = part_of(part, local)
+        product = mm(grad_v[at, :], first_in[...])
+        qkv_grad[at, :] = product
+        move.store(qkv_grad.at[at, :], qkv_out.at[at, :])
+        gain_row += jnp.sum(weight[at, :].astype(F32) * product, axis=0, keepdims=True)
+    message[rows:, :] = two_rows(gain_row / first_gain[...])
+    move.finish()
+
+
+def sum_kernel(message, far, out):
+    rows = out.shape[0] - 16
+    out[:rows, :] = (message[:rows, :].astype(F32) + far[:rows, :].astype(F32)).astype(BF16)
+    out[rows:, :] = two_rows(sum_rows(message[rows:, :]) + sum_rows(far[rows:, :]))
+
+
+def last_kernel(mine, far, tokens, gain, middle_grad, tokens_grad, gain_grad):
+    rows = tokens.shape[0]
+    gain_grad[...] = sum_rows(mine[rows:, :]) + sum_rows(far[rows:, :])
+    first_grad = mine[:rows, :].astype(F32) + far[:rows, :].astype(F32)
+    normed, scale = norm_parts(tokens[...].astype(F32))
+    back = norm_back(first_grad * gain[...], normed, scale)
+    tokens_grad[...] = (middle_grad[...] + back).astype(BF16)
+
+
+def products_kernel(gate_a, gate_b, hidden_a, hidden_b, second_a, second_b, cot, *refs):
+    in_out, mlp_out, in_grad, mlp_grad, sems = refs
+    move = Mover(sems)
+    tokens = second_a.shape[0]
+    units = hidden_a.shape[0]
+    for part in range(2):
+        at = part_of(part, units)
+        in_grad[at, :] = mm(gate_a[at, :], second_a[...]) + mm(gate_b[at, :], second_b[...])
+        move.store(in_grad.at[at, :], in_out.at[at, :])
+    mlp_grad[...] = mm(hidden_a[...], cot[:tokens, :]) + mm(hidden_b[...], cot[tokens:, :])
+    move.store(mlp_grad, mlp_out)
+    move.finish()
+
+
+def output_kernel(att_a, att_b, branch, middle, part, far, attn_out, output, attn_grad, sems):
+    move = Mover(sems)
+    tokens = att_a.shape[1]
+    attn_grad[...] = mm(att_a[...], branch[:tokens, :]) + mm(att_b[...], branch[tokens:, :])
+    move.store(attn_grad, attn_out)
+    branch_sum = part[...].astype(F32) + far[...].astype(F32)
+    output[...] = (middle[...] + branch_sum).astype(BF16)
+    move.finish()
 
 
 def over_ctx(value, step, spots):
@@ -603,16 +683,6 @@
     ids = tuple((step, step + 1) for step in range(0, spots, 2))
     near, _ = lax.optimization_barrier((near, gate))
     return near, [swap(piece, 1) for piece in near], ids
-
-
-def two_rows(row):
-    high = row.astype(BF16)
-    low = (row - high.astype(F32)).astype(BF16)
-    return jnp.concatenate([high[None], low[None], jnp.zeros((14, row.shape[0]), BF16)], 0)
-
-
-def sum_rows(pair):
-    return pair[0].astype(F32) + pair[1].astype(F32)
 
 
 def replicated_body(
@@ -642,21 +712,21 @@
 
     near, far, ids, steps = gather_tokens(tokens, core, spots)
     attn_core = swap(attn_weight, 1)
-    attn_side = swap(attn_weight, 2)
-    attn_both = swap(attn_side, 1)
-    mlp_weights = jnp.concatenate([in_t, mlp_weight], axis=0)
-    mlp_weights, _ = lax.optimization_barrier((mlp_weights, attn_side))
-    mlp_side = swap(mlp_weights, 2)
+    in_side = swap(in_t, 2)
+    rest = jnp.concatenate([mlp_weight, attn_weight], axis=0)
+    rest_side = swap(rest, 2)
+    attn_both = swap(rest_side[units:], 1)
     half_rows = total_rows // 2
     tall, wide = (total_rows, width), (half_rows, width)
     cells = heads * total_rows * half_rows
-    tok_all, first_input, qkv, att_a, lse_a = call(
+    tok_all, first_input, qkv, att_a, exact_a, lse_a = call(
         functools.partial(project_kernel, heads, ids),
         [
             Away(pltpu.HBM(tall, BF16)),
             fast(tall, BF16),
             fast((3 * local, total_rows), BF16),
             fast((local, half_rows), BF16),
+            fast((local, half_rows), F32),
             fast((8, half_rows), F32),
         ],
         [
@@ -673,9 +743,13 @@
         copies=20,
     )
     side_a = swap(att_a, 2)
-    att_b, lse_b = call(
+    att_b, exact_b, lse_b = call(
         functools.partial(queries_kernel, heads),
-        [fast((local, half_rows), BF16), fast((8, half_rows), F32)],
+        [
+            fast((local, half_rows), BF16),
+            fast((local, half_rows), F32),
+            fast((8, half_rows), F32),
+        ],
         [qkv],
         scratch=[((total_rows, HEAD), BF16)],
     )
@@ -688,6 +762,9 @@
         fast((units, half_rows), BF16),
         fast((2 * units, half_rows), BF16),
         fast(wide, BF16),
+        fast((half_rows, 1), F32),
+        fast((half_rows, 1), F32),
+        fast((rows, width), F32),
         fast((rows, width), BF16),
     ]
     room = [
@@ -711,8 +788,8 @@
             *map(Away, [tok_all, cotangent, *cot_near, *cot_far]),
             att_a,
             *map(Away, atts_a[1:]),
-            *map(Away, [attn_weight, attn_core, attn_side, attn_both]),
-            *map(Away, [mlp_weights, mlp_side]),
+            *map(Away, [attn_weight, attn_core, attn_both]),
+            *map(Away, [in_t, in_side, mlp_weight, rest_side]),
             second_row,
         ],
         scratch=[(wide, BF16), *room],
@@ -721,8 +798,8 @@
         cells=4 * units * half_rows,
         room=20,
     )
-    side_b, _ = lax.optimization_barrier((swap(att_b, 2), cot_all))
-    atts_b = [att_b, swap(att_b, 1), side_b, swap(side_b, 1)]
+    atts_b = [att_b, *[swap(att_b, mask) for mask in (1, 2, 3)]]
+    atts_b, _ = lax.optimization_barrier((atts_b, cot_all))
     results_b = call(
         functools.partial(mlp_kernel, 1, ()),
         halves,
@@ -736,6 +813,7 @@
             attn_all,
             in_all,
             mlp_all,
+            *results_a[7:],
         ],
         scratch=room,
         copies=8,
@@ -743,71 +821,86 @@
         cells=4 * units * half_rows,
         room=20,
     )
-    middles, seconds, hiddens, gates, parts, out_parts = zip(results_a, results_b)
+    middles, seconds, hiddens, gates, parts, means, scales = zip(results_a[:7], results_b[:7])
+    own_middle, out_part = results_b[7:]
     fars = [swap(part, 1) for part in parts]
-    out_part = jnp.where(here < spots // 2, *out_parts)
     out_far = swap(out_part, 1)
-
-    second_gain_grad, branch_grad, middle_grad, grad_t, first_part = call(
+    in_grad, mlp_grad = call(
+        products_kernel,
+        [Away(pltpu.HBM((2 * units, width), F32)), Away(pltpu.HBM((units, width), F32))],
+        [*gates, *hiddens, *seconds, cot_all],
+        scratch=[((2 * units, width), F32), ((units, width), F32)],
+        copies=4,
+        flops=6 * total_rows * width * units,
+    )
+    fars, in_grad, mlp_grad = lax.optimization_barrier((fars, in_grad, mlp_grad))
+    second_gain_grad, branch_grad, middle_grad, message, qkv_grad = call(
         functools.partial(back_kernel, heads),
         [
             fast((1, width), F32),
             fast(tall, BF16),
             fast((rows, width), F32),
-            fast((3 * local, total_rows), BF16),
-            fast((rows, width), BF16),
+            fast((rows + 16, width), BF16),
+            Away(pltpu.HBM((3 * local, width), F32)),
         ],
         [
             place,
             *middles,
+            *means,
+            *scales,
             *parts,
             *fars,
             cot_all,
             second_row,
             attn_weight,
             qkv,
+            exact_a,
+            exact_b,
             lse_a,
             lse_b,
             qkv_t,
             cosine,
             sine,
+            first_input,
+            first_gain[None, :],
         ],
         scratch=[
+            ((3 * local, total_rows), BF16),
             ((local, total_rows), BF16),
             ((8, total_rows), F32),
             ((total_rows, HEAD), BF16),
             ((total_rows, HEAD), BF16),
             ((total_rows, HEAD), F32),
             ((total_rows, HEAD), F32),
+            ((3 * local, width), F32),
         ],
-        flops=2 * total_rows * local * (width + 20 * total_rows),
+        copies=4,
+        flops=2 * total_rows * local * (4 * width + 20 * total_rows),
         cells=heads * total_rows * total_rows,
     )
-    pair = (first_part.astype(F32) + swap(first_part, 1).astype(F32)).astype(BF16)
-    qkv_grad = mm(grad_t, first_input)
-    gain_rows = two_rows(jnp.sum(qkv_t.astype(F32) * qkv_grad, axis=0) / first_gain)
-    across = jnp.concatenate([pair, gain_rows], 0)
-    far_rows = swap(across, 2)
-    first_grad = pair.astype(F32) + far_rows[:rows].astype(F32)
-    gain_rows = two_rows(sum_rows(gain_rows) + sum_rows(far_rows[rows:]))
-    first_gain_grad = sum_rows(gain_rows) + sum_rows(swap(gain_rows, 1))
-
-    hiddens, out_far, _ = lax.optimization_barrier((hiddens, out_far, pair))
-    attn_grad = mm(jnp.concatenate([att_a, att_b], 1), branch_grad)
-    in_grad = mm(gates[0], seconds[0]) + mm(gates[1], seconds[1])
-    mlp_grad = mm(hiddens[0], cot_all[:half_rows]) + mm(hiddens[1], cot_all[half_rows:])
-    own_row = (here % (spots // 2)) * rows
-    own_middle = jnp.where(
-        here < spots // 2,
-        *[lax.dynamic_slice_in_dim(middle, own_row, rows, axis=0) for middle in middles],
-    )
-    output = (own_middle + (out_part.astype(F32) + out_far.astype(F32))).astype(BF16)
-    normed, scale = norm_parts(tokens.astype(F32))
-    tokens_grad = (middle_grad + norm_back(first_grad * first_gain, normed, scale)).astype(BF16)
+    (mine,) = call(
+        sum_kernel, [fast((rows + 16, width), BF16)], [message, swap(message, 1)], flops=rows * width
+    )
+    far = swap(mine, 2)
+    out_far, att_b, _ = lax.optimization_barrier((out_far, att_b, mine))
+    attn_grad, output = call(
+        output_kernel,
+        [Away(pltpu.HBM((local, width), F32)), jax.ShapeDtypeStruct((rows, width), BF16)],
+        [att_a, att_b, branch_grad, own_middle, out_part, out_far],
+        scratch=[((local, width), F32)],
+        copies=2,
+        flops=2 * total_rows * width * local,
+    )
+    tokens_grad, first_gain_grad = call(
+        last_kernel,
+        [jax.ShapeDtypeStruct((rows, width), BF16), jax.ShapeDtypeStruct((1, width), F32)],
+        [mine, far, tokens, first_gain[None, :], middle_grad],
+        flops=16 * rows * width,
+    )
     return (
         output,
         tokens_grad,
-        first_gain_grad,
+        first_gain_grad[0],
         jnp.transpose(qkv_grad.reshape(3, local, width), (2, 0, 1)),
         attn_grad,
         second_gain_grad[0],

time: 114 us -> 105 us (0.921)
  matrix products: 7.77 us -> 0 us
  other arithmetic: 9.55 us -> 3.04 us
  Pallas kernels: 48.3 us -> 53.3 us
  local copies, waits for them, and re-layouts: 8.86 us -> 4.5 us
  starting transfers between devices: 25.3 us -> 28 us
  waiting for transfers between devices: 12.7 us -> 14.4 us
    dot_general x6 -> x0, matrix products: 7.77 us -> none  [mm(): return lax.dot_general(a, b, dims, preferred_element_type=F32)]
    pallas_call x5 -> x9, Pallas kernels: 48.3 us -> 53.3 us  [call(): pl.pallas_call(kernel, out_shape=[o.value if isinstance(o, Away) else o f...]
    ppermute x9, waiting for transfers between devices: 3.84 us -> 8.75 us  [over_ctx(): lax.ppermute(value, 'ctx', [(spot, spot ^ step) for spot in range(spots)])]
    convert_element_type x5 -> x0, other arithmetic: 4.12 us -> none  [the longest x1 2.1 us: replicated_body(): (own_middle + (out_part.astype(F32) + out_far.astype(F32))).astype(BF16)]
    unnamed x104 -> x62, local copies, waits for them, and re-layouts: 4.94 us -> 1.63 us
    ppermute x24 -> x23, waiting for transfers between devices: 8.89 us -> 5.65 us  [swap(): return lax.ppermute(value, 'wt', [(spot, spot ^ mask) for spot in range(4)])]
    ppermute x9, starting transfers between devices: 14.6 us -> 16.9 us  [over_ctx(): lax.ppermute(value, 'ctx', [(spot, spot ^ step) for spot in range(spots)])]
    broadcast_in_dim x4 -> x0, local copies, waits for them, and re-layouts: 1.2 us -> none  [the longest x2 0.61 us: two_rows(): high[None]]
  transfers between devices with their start and end apart: 33 -> 32, of which waited for: 7 -> 9; matrix products, arithmetic and copies ran while one was open for 17% -> 4% of each run, Pallas kernels for 42% -> 27%
where the time goes in v3:
time: 105 us; the launch traced here: 104 us
  Pallas kernels  53.3 us (51%)
  starting transfers between devices  28 us (27%)
  waiting for transfers between devices  14.4 us (14%)
  local copies, waits for them, and re-layouts  4.5 us (4%)
  other arithmetic  3.04 us (3%)
  between operations  1.16 us (1%)
    pallas_call x9, Pallas kernels, call(): pl.pallas_call(kernel, out_shape=[o.value if isinstance(o, Away) else o f...  53.3 us
    ppermute x9, starting transfers between devices, over_ctx(): lax.ppermute(value, 'ctx', [(spot, spot ^ step) for spot in range(spots)])  16.9 us
    ppermute x23, starting transfers between devices, swap(): return lax.ppermute(value, 'wt', [(spot, spot ^ mask) for spot in range(4)])  11.1 us
    ppermute x9, waiting for transfers between devices, over_ctx(): lax.ppermute(value, 'ctx', [(spot, spot ^ step) for spot in range(spots)])  8.75 us
    ppermute x23, waiting for transfers between devices, swap(): return lax.ppermute(value, 'wt', [(spot, spot ^ mask) for spot in range(4)])  5.65 us
  transfers between devices with their start and end apart: 32, of which 9 were waited for; matrix products, arithmetic and copies ran while one was open for 4% of the time, Pallas kernels for 27%

profile of v3, /device:TPU:0, one launch (start us, length us, event | category | flops | bytes accessed | tf_op | source)
XLA Modules:
  0.0 104.4 jit_solution(2562111148784045749)
XLA Ops:
  0.7 1.0 constant_dynamic-slice_fusion.1
  1.6 4.0 %collective-permute-start.2 = (bf16[64,768]{1,0:T(8,128)(2,1)S(1)}, bf16[64,768]{1,0:T(8,128)(2,1)S(1)}, u32[]{:S(2)}, u32[]{:S(2)}) collective-permute-start(bf16[64,768]{1,0:T(8,128)(2,1)S(1)} %constant_dynamic-slice_fusion.1), channel_id=1, source_target_pairs={{0,16},{4,20},{8,24},{12,28},{16,0},{20,4},{24,8},{28,12},{1,17},{... | collective-permute-start | bytes 294920 | tf_op jit(solution)/shard_map/ppermute | solution.py:653
  5.7 1.3 %collective-permute-start.3 = (bf16[64,768]{1,0:T(8,128)(2,1)S(1)}, bf16[64,768]{1,0:T(8,128)(2,1)S(1)}, u32[]{:S(2)}, u32[]{:S(2)}) collective-permute-start(bf16[64,768]{1,0:T(8,128)(2,1)S(1)} %constant_dynamic-slice_fusion.1), channel_id=1, source_target_pairs={{0,24},{4,28},{8,16},{12,20},{16,8},{20,12},{24,0},{28,4},{1,25},{... | collective-permute-start | bytes 294920 | tf_op jit(solution)/shard_map/ppermute | solution.py:653
  7.3 0.9 constant_dynamic-slice_fusion
  8.2 1.6 %collective-permute-start.9 = (bf16[64,768]{1,0:T(8,128)(2,1)S(1)}, bf16[64,768]{1,0:T(8,128)(2,1)S(1)}, u32[]{:S(2)}, u32[]{:S(2)}) collective-permute-start(bf16[64,768]{1,0:T(8,128)(2,1)S(1)} %constant_dynamic-slice_fusion), channel_id=1, source_target_pairs={{0,4},{4,0},{8,12},{12,8},{16,20},{20,16},{24,28},{28,24},{1,5},{5... | collective-permute-start | bytes 294920 | tf_op jit(solution)/shard_map/ppermute | solution.py:653
  9.8 1.2 %pad_maximum_fusion = bf16[480,768]{1,0:T(8,128)(2,1)S(1)} fusion(bf16[192,768]{1,0:T(8,128)(2,1)} %refs_12_.1, bf16[288,768]{1,0:T(8,128)(2,1)} %refs_18_.1), kind=kLoop, calls=%fused_computation | loop fusion | flops 1474560 | bytes 1474560 | tf_op jit(solution)/shard_map/concatenate | solution.py:716
  10.9 1.6 %collective-permute-start.21 = (bf16[480,768]{1,0:T(8,128)(2,1)S(1)}, bf16[480,768]{1,0:T(8,128)(2,1)}, u32[]{:S(2)}, u32[]{:S(2)}) collective-permute-start(bf16[480,768]{1,0:T(8,128)(2,1)S(1)} %pad_maximum_fusion), channel_id=1, source_target_pairs={{0,2},{1,3},{2,0},{3,1},{4,6},{5,7},{6,4},{7,5},{8,10},{9,11},{10,... | collective-permute-start | bytes 2211848 | tf_op jit(solution)/shard_map/ppermute | solution.py:657
  12.5 1.1 %collective-permute-done.2 = bf16[64,768]{1,0:T(8,128)(2,1)S(1)} collective-permute-done((bf16[64,768]{1,0:T(8,128)(2,1)S(1)}, bf16[64,768]{1,0:T(8,128)(2,1)S(1)}, u32[]{:S(2)}, u32[]{:S(2)}) %collective-permute-start.2) | collective-permute-done | bytes 98336 | tf_op jit(solution)/shard_map/ppermute | solution.py:653
  13.6 1.8 %collective-permute-start.4 = (bf16[2,64,768]{2,1,0:T(8,128)(2,1)S(1)}, bf16[2,64,768]{2,1,0:T(8,128)(2,1)S(1)}, u32[]{:S(2)}, u32[]{:S(2)}) collective-permute-start(bf16[2,64,768]{2,1,0:T(8,128)(2,1)S(1)} %pad_maximum_fusion.2.refs_2_), channel_id=1, source_target_pairs={{0,4},{4,0},{8,12},{12,8},{16,20},{20,16},{24,28},{28,24},{1,5},{5... | collective-permute-start | bytes 589832 | tf_op jit(solution)/shard_map/ppermute | solution.py:653
  16.4 3.8 %collective-permute-done.4.refs_3_ = bf16[2,64,768]{2,1,0:T(8,128)(2,1)S(1)} collective-permute-done((bf16[2,64,768]{2,1,0:T(8,128)(2,1)S(1)}, bf16[2,64,768]{2,1,0:T(8,128)(2,1)S(1)}, u32[]{:S(2)}, u32[]{:S(2)}) %collective-permute-start.4) | collective-permute-done | bytes 196640 | tf_op jit(solution)/shard_map/ppermute | solution.py:653
  20.2 3.2 %collective-permute-start.10 = (bf16[2,64,768]{2,1,0:T(8,128)(2,1)S(1)}, bf16[2,64,768]{2,1,0:T(8,128)(2,1)S(1)}, u32[]{:S(2)}, u32[]{:S(2)}) collective-permute-start(bf16[2,64,768]{2,1,0:T(8,128)(2,1)S(1)} %pad_maximum_fusion.3.refs_1_), channel_id=1, source_target_pairs={{0,8},{4,12},{8,0},{12,4},{16,24},{20,28},{24,16},{28,20},{1,9},{5... | collective-permute-start | bytes 589832 | tf_op jit(solution)/shard_map/ppermute | solution.py:653
  23.5 1.6 %collective-permute-start.23 = (bf16[576,768]{1,0:T(8,128)(2,1)}, bf16[576,768]{1,0:T(8,128)(2,1)}, u32[]{:S(2)}, u32[]{:S(2)}) collective-permute-start(bf16[576,768]{1,0:T(8,128)(2,1)} %bitcast.13.refs_16_), channel_id=1, source_target_pairs={{0,2},{1,3},{2,0},{3,1},{4,6},{5,7},{6,4},{7,5},{8,10},{9,11},{10,... | collective-permute-start | bytes 2654216 | tf_op jit(solution)/shard_map/ppermute | solution.py:657
  25.3 1.8 %collective-permute-done.10.refs_2_ = bf16[2,64,768]{2,1,0:T(8,128)(2,1)S(1)} collective-permute-done((bf16[2,64,768]{2,1,0:T(8,128)(2,1)S(1)}, bf16[2,64,768]{2,1,0:T(8,128)(2,1)S(1)}, u32[]{:S(2)}, u32[]{:S(2)}) %collective-permute-start.10) | collective-permute-done | bytes 196640 | tf_op jit(solution)/shard_map/ppermute | solution.py:653
  27.1 3.9 %collective-permute-start.11 = (bf16[2,64,768]{2,1,0:T(8,128)(2,1)S(1)}, bf16[2,64,768]{2,1,0:T(8,128)(2,1)}, u32[]{:S(2)}, u32[]{:S(2)}) collective-permute-start(bf16[2,64,768]{2,1,0:T(8,128)(2,1)S(1)} %pad_maximum_fusion.3.refs_1_), channel_id=1, source_target_pairs={{0,16},{4,20},{8,24},{12,28},{16,0},{20,4},{24,8},{28,12},{1,17},{... | collective-permute-start | bytes 589832 | tf_op jit(solution)/shard_map/ppermute | solution.py:653
  31.7 0.8 collective-permute-done.6.refs_5_
  33.2 9.3 %shard_map.143 = (bf16[1024,768]{1,0:T(8,128)(2,1)}, bf16[1024,768]{1,0:T(8,128)(2,1)S(1)}, bf16[576,1024]{1,0:T(8,128)(2,1)S(1)}, bf16[192,512]{1,0:T(8,128)(2,...) custom-call(s32[4]{0:T(128)S(1)} %pad_add_fusion.place, bf16[128,768]{1,0:T(8,128)(2,1)} %tokens.1, ...), custom_call_target="tpu_custom_call" | custom-call | tf_op jit(solution)/shard_map/pallas_call | solution.py:277
  42.6 2.1 %collective-permute-done.11.refs_3_ = bf16[2,64,768]{2,1,0:T(8,128)(2,1)} collective-permute-done((bf16[2,64,768]{2,1,0:T(8,128)(2,1)S(1)}, bf16[2,64,768]{2,1,0:T(8,128)(2,1)}, u32[]{:S(2)}, u32[]{:S(2)}) %collective-permute-start.11) | collective-permute-done | bytes 196640 | tf_op jit(solution)/shard_map/ppermute | solution.py:653
  45.2 4.7 %shard_map.144 = (bf16[192,512]{1,0:T(8,128)(2,1)S(1)}, f32[192,512]{1,0:T(8,128)S(1)}, f32[8,512]{1,0:T(8,128)S(1)}) custom-call(bf16[576,1024]{1,0:T(8,128)(2,1)S(1)} %get-tuple-element.69.qkv.refs_13_), custom_call_target="tpu_custom_call" | custom-call | tf_op jit(solution)/shard_map/pallas_call | solution.py:277
  50.6 1.0 slice.4
  52.7 0.9 collective-permute-done.16.refs_8_
  54.0 1.5 %collective-permute-start.25 = (bf16[192,512]{1,0:T(8,128)(2,1)S(1)}, bf16[192,512]{1,0:T(8,128)(2,1)S(1)}, u32[]{:S(2)}, u32[]{:S(2)}) collective-permute-start(bf16[192,512]{1,0:T(8,128)(2,1)S(1)} %get-tuple-element.111.refs_1_.att_b), channel_id=1, source_target_pairs={{0,2},{1,3},{2,0},{3,1},{4,6},{5,7},{6,4},{7,5},{8,10},{9,11},{10,... | collective-permute-start | bytes 589832 | tf_op jit(solution)/shard_map/ppermute | solution.py:657
  56.3 9.0 %shard_map.145 = (bf16[1024,768]{1,0:T(8,128)(2,1)S(1)}, bf16[768,768]{1,0:T(8,128)(2,1)S(1)}, bf16[1152,768]{1,0:T(8,128)(2,1)S(1)}, bf16[576,768]{1,0:T(8,128)...) custom-call(s32[4]{0:T(128)S(1)} %pad_add_fusion.place, ...), custom_call_target="tpu_custom_call" | custom-call | flops 2868903936 | bytes 7965712 | tf_op jit(solution)/shard_map/pallas_call | solution.py:277
  65.4 0.6 copy-done.26
  66.2 8.0 %shard_map.146 = (f32[512,768]{1,0:T(8,128)S(1)}, bf16[512,768]{1,0:T(8,128)(2,1)S(1)}, bf16[288,512]{1,0:T(8,128)(2,1)S(1)}, bf16[576,512]{1,0:T(8,128)(2,1)S(1...) custom-call(s32[4]{0:T(128)S(1)} %pad_add_fusion.place, ...), custom_call_target="tpu_custom_call" | custom-call | flops 2868903936 | bytes 7572496 | tf_op jit(solution)/shard_map/pallas_call | solution.py:277
  74.8 2.5 %shard_map.147 = (f32[576,768]{1,0:T(8,128)}, f32[288,768]{1,0:T(8,128)}) custom-call(bf16[576,512]{1,0:T(8,128)(2,1)S(1)} %get-tuple-element.95.gate_a, bf16[576,512]{1,0:T(8,128)(2,1)S(1)} %get-tuple-element.96.gate_b, bf16[288,512]{1,0:T(8,128)(2,1)S(1)} %get-tuple-element.97.hidden_a, bf16[288,512]{1,0:T(8,128)(2,1)S(1)} %get-tuple-element.98.hidden_b, ...), custom_call_target="tpu_custom_call" | custom-call | flops 1358954496 | bytes 4915200 | tf_op jit(solution)/shard_map/pallas_call | solution.py:277
  77.8 15.6 %shard_map.148 = (f32[1,768]{1,0:T(1,128)S(1)}, bf16[1024,768]{1,0:T(8,128)(2,1)S(1)}, f32[128,768]{1,0:T(8,128)S(1)}, bf16[144,768]{1,0:T(8,128)(2,1)S(1)}, f32[576,768]{1,0:T(8,128)}) custom-call(s32[4]{0:T(128)S(1)} %pad_add_fusion.place, f32[512,768]{1,0:T(8,128)S(1)} %get-tuple-element.87.refs_0_, f32[512,768]{1,0:T(8,128)S(1)} %get-tuple-element.88.refs_1_, ...), custom_call_target="tpu_custom_call" | custom-call | flops 9261023232 | bytes 12892176 | tf_op jit(solution)/shard_map/pallas_call | solution.py:277
  94.0 1.0 collective-permute-done.30.far
  95.0 1.6 %collective-permute-start.31 = (bf16[144,768]{1,0:T(8,128)(2,1)S(1)}, bf16[144,768]{1,0:T(8,128)(2,1)S(1)}, u32[]{:S(2)}, u32[]{:S(2)}) collective-permute-start(bf16[144,768]{1,0:T(8,128)(2,1)S(1)} %shard_map.149.mine), channel_id=1, source_target_pairs={{0,2},{1,3},{2,0},{3,1},{4,6},{5,7},{6,4},{7,5},{8,10},{9,11},{10,... | collective-permute-start | bytes 663560 | tf_op jit(solution)/shard_map/ppermute | solution.py:657
  96.6 0.6 reduce.1
  97.2 3.1 %shard_map.150 = (f32[192,768]{1,0:T(8,128)}, bf16[128,768]{1,0:T(8,128)(2,1)}) custom-call(bf16[192,512]{1,0:T(8,128)(2,1)S(1)} %get-tuple-element.66.refs_9_.att_a, bf16[192,512]{1,0:T(8,128)(2,1)S(1)} %get-tuple-element.111.refs_1_.att_b, bf16[1024,768]{1,0:T(8,128)(2,1)S(1)} %get-tuple-element.112.branch, f32[128,768]{1,0:T(8,128)S(1)} %get-tuple-element.113.middle, ...), custom_call_target="tpu_custom_call" | custom-call | flops 301989888 | bytes 2752512 | tf_op jit(solution)/shard_map/pallas_call | solution.py:277
  100.3 2.5 %collective-permute-done.31.far = bf16[144,768]{1,0:T(8,128)(2,1)S(1)} collective-permute-done((bf16[144,768]{1,0:T(8,128)(2,1)S(1)}, bf16[144,768]{1,0:T(8,128)(2,1)S(1)}, u32[]{:S(2)}, u32[]{:S(2)}) %collective-permute-start.31) | collective-permute-done | bytes 221216 | tf_op jit(solution)/shard_map/ppermute | solution.py:657
  102.8 1.0 shard_map.151
  (120 shorter events, 8.8 us)
Async XLA Ops:
  1.6 11.9 %collective-permute-start.2 = (bf16[64,768]{1,0:T(8,128)(2,1)S(1)}, bf16[64,768]{1,0:T(8,128)(2,1)S(1)}, u32[]{:S(2)}, u32[]{:S(2)}) collective-permute-start(bf16[64,768]{1,0:T(8,128)(2,1)S(1)} %constant_dynamic-slice_fusion.1), channel_id=1, source_target_pairs={{0,16},{4,20},{8,24},{12,28},{16,0},{20,4},{24,8},{28,12},{1,17},{... | collective-permute-start | bytes 294920 | tf_op jit(solution)/shard_map/ppermute | solution.py:653
  5.7 7.9 %collective-permute-start.3 = (bf16[64,768]{1,0:T(8,128)(2,1)S(1)}, bf16[64,768]{1,0:T(8,128)(2,1)S(1)}, u32[]{:S(2)}, u32[]{:S(2)}) collective-permute-start(bf16[64,768]{1,0:T(8,128)(2,1)S(1)} %constant_dynamic-slice_fusion.1), channel_id=1, source_target_pairs={{0,24},{4,28},{8,16},{12,20},{16,8},{20,12},{24,0},{28,4},{1,25},{... | collective-permute-start | bytes 294920 | tf_op jit(solution)/shard_map/ppermute | solution.py:653
  7.0 8.4 %collective-permute-start = (bf16[64,768]{1,0:T(8,128)(2,1)S(1)}, bf16[64,768]{1,0:T(8,128)(2,1)S(1)}, u32[]{:S(2)}, u32[]{:S(2)}) collective-permute-start(bf16[64,768]{1,0:T(8,128)(2,1)S(1)} %constant_dynamic-slice_fusion.1), channel_id=1, source_target_pairs={{0,8},{4,12},{8,0},{12,4},{16,24},{20,28},{24,16},{28,20},{1,9},{5... | collective-permute-start | bytes 294920 | tf_op jit(solution)/shard_map/ppermute | solution.py:653
  8.2 7.7 %collective-permute-start.9 = (bf16[64,768]{1,0:T(8,128)(2,1)S(1)}, bf16[64,768]{1,0:T(8,128)(2,1)S(1)}, u32[]{:S(2)}, u32[]{:S(2)}) collective-permute-start(bf16[64,768]{1,0:T(8,128)(2,1)S(1)} %constant_dynamic-slice_fusion), channel_id=1, source_target_pairs={{0,4},{4,0},{8,12},{12,8},{16,20},{20,16},{24,28},{28,24},{1,5},{5... | collective-permute-start | bytes 294920 | tf_op jit(solution)/shard_map/ppermute | solution.py:653
  10.9 39.6 %collective-permute-start.21 = (bf16[480,768]{1,0:T(8,128)(2,1)S(1)}, bf16[480,768]{1,0:T(8,128)(2,1)}, u32[]{:S(2)}, u32[]{:S(2)}) collective-permute-start(bf16[480,768]{1,0:T(8,128)(2,1)S(1)} %pad_maximum_fusion), channel_id=1, source_target_pairs={{0,2},{1,3},{2,0},{3,1},{4,6},{5,7},{6,4},{7,5},{8,10},{9,11},{10,... | collective-permute-start | bytes 2211848 | tf_op jit(solution)/shard_map/ppermute | solution.py:657
  13.6 6.6 %collective-permute-start.4 = (bf16[2,64,768]{2,1,0:T(8,128)(2,1)S(1)}, bf16[2,64,768]{2,1,0:T(8,128)(2,1)S(1)}, u32[]{:S(2)}, u32[]{:S(2)}) collective-permute-start(bf16[2,64,768]{2,1,0:T(8,128)(2,1)S(1)} %pad_maximum_fusion.2.refs_2_), channel_id=1, source_target_pairs={{0,4},{4,0},{8,12},{12,8},{16,20},{20,16},{24,28},{28,24},{1,5},{5... | collective-permute-start | bytes 589832 | tf_op jit(solution)/shard_map/ppermute | solution.py:653
  15.4 8.0 %collective-permute-start.1 = (bf16[2,64,768]{2,1,0:T(8,128)(2,1)S(1)}, bf16[2,64,768]{2,1,0:T(8,128)(2,1)S(1)}, u32[]{:S(2)}, u32[]{:S(2)}) collective-permute-start(bf16[2,64,768]{2,1,0:T(8,128)(2,1)S(1)} %pad_maximum_fusion.1.refs_0_), channel_id=1, source_target_pairs={{0,4},{4,0},{8,12},{12,8},{16,20},{20,16},{24,28},{28,24},{1,5},{5... | collective-permute-start | bytes 589832 | tf_op jit(solution)/shard_map/ppermute | solution.py:653
  15.8 7.6 %collective-permute-start.7 = (bf16[2,64,768]{2,1,0:T(8,128)(2,1)S(1)}, bf16[2,64,768]{2,1,0:T(8,128)(2,1)S(1)}, u32[]{:S(2)}, u32[]{:S(2)}) collective-permute-start(bf16[2,64,768]{2,1,0:T(8,128)(2,1)S(1)} %pad_maximum_fusion.2.refs_2_), channel_id=1, source_target_pairs={{0,1},{1,0},{2,3},{3,2},{4,5},{5,4},{6,7},{7,6},{8,9},{9,8},{10,11... | collective-permute-start | bytes 589832 | tf_op jit(solution)/shard_map/ppermute | solution.py:657
  15.9 9.1 %collective-permute-start.5 = (bf16[2,64,768]{2,1,0:T(8,128)(2,1)S(1)}, bf16[2,64,768]{2,1,0:T(8,128)(2,1)S(1)}, u32[]{:S(2)}, u32[]{:S(2)}) collective-permute-start(bf16[2,64,768]{2,1,0:T(8,128)(2,1)S(1)} %pad_maximum_fusion.1.refs_0_), channel_id=1, source_target_pairs={{0,1},{1,0},{2,3},{3,2},{4,5},{5,4},{6,7},{7,6},{8,9},{9,8},{10,11... | collective-permute-start | bytes 589832 | tf_op jit(solution)/shard_map/ppermute | solution.py:657
  20.2 6.8 %collective-permute-start.10 = (bf16[2,64,768]{2,1,0:T(8,128)(2,1)S(1)}, bf16[2,64,768]{2,1,0:T(8,128)(2,1)S(1)}, u32[]{:S(2)}, u32[]{:S(2)}) collective-permute-start(bf16[2,64,768]{2,1,0:T(8,128)(2,1)S(1)} %pad_maximum_fusion.3.refs_1_), channel_id=1, source_target_pairs={{0,8},{4,12},{8,0},{12,4},{16,24},{20,28},{24,16},{28,20},{1,9},{5... | collective-permute-start | bytes 589832 | tf_op jit(solution)/shard_map/ppermute | solution.py:653
  23.4 7.6 %collective-permute-start.8 = (bf16[2,64,768]{2,1,0:T(8,128)(2,1)S(1)}, bf16[2,64,768]{2,1,0:T(8,128)(2,1)S(1)}, u32[]{:S(2)}, u32[]{:S(2)}) collective-permute-start(bf16[2,64,768]{2,1,0:T(8,128)(2,1)S(1)} %collective-permute-done.4.refs_3_), channel_id=1, source_target_pairs={{0,1},{1,0},{2,3},{3,2},{4,5},{5,4},{6,7},{7,6},{8,9},{9,8},{10,11... | collective-permute-start | bytes 589832 | tf_op jit(solution)/shard_map/ppermute | solution.py:657
  23.5 32.2 %collective-permute-start.23 = (bf16[576,768]{1,0:T(8,128)(2,1)}, bf16[576,768]{1,0:T(8,128)(2,1)}, u32[]{:S(2)}, u32[]{:S(2)}) collective-permute-start(bf16[576,768]{1,0:T(8,128)(2,1)} %bitcast.13.refs_16_), channel_id=1, source_target_pairs={{0,2},{1,3},{2,0},{3,1},{4,6},{5,7},{6,4},{7,5},{8,10},{9,11},{10,... | collective-permute-start | bytes 2654216 | tf_op jit(solution)/shard_map/ppermute | solution.py:657
  25.1 24.9 %collective-permute-start.20 = (bf16[192,768]{1,0:T(8,128)(2,1)S(1)}, bf16[192,768]{1,0:T(8,128)(2,1)}, u32[]{:S(2)}, u32[]{:S(2)}) collective-permute-start(bf16[192,768]{1,0:T(8,128)(2,1)S(1)} %copy-done.3), channel_id=1, source_target_pairs={{0,1},{1,0},{2,3},{3,2},{4,5},{5,4},{6,7},{7,6},{8,9},{9,8},{10,11... | collective-permute-start | bytes 884744 | tf_op jit(solution)/shard_map/ppermute | solution.py:657
  27.1 17.6 %collective-permute-start.11 = (bf16[2,64,768]{2,1,0:T(8,128)(2,1)S(1)}, bf16[2,64,768]{2,1,0:T(8,128)(2,1)}, u32[]{:S(2)}, u32[]{:S(2)}) collective-permute-start(bf16[2,64,768]{2,1,0:T(8,128)(2,1)S(1)} %pad_maximum_fusion.3.refs_1_), channel_id=1, source_target_pairs={{0,16},{4,20},{8,24},{12,28},{16,0},{20,4},{24,8},{28,12},{1,17},{... | collective-permute-start | bytes 589832 | tf_op jit(solution)/shard_map/ppermute | solution.py:653
  31.0 1.5 %collective-permute-start.6 = (bf16[2,64,768]{2,1,0:T(8,128)(2,1)S(1)}, bf16[2,64,768]{2,1,0:T(8,128)(2,1)S(1)}, u32[]{:S(2)}, u32[]{:S(2)}) collective-permute-start(bf16[2,64,768]{2,1,0:T(8,128)(2,1)S(1)} %collective-permute-done.1.refs_1_), channel_id=1, source_target_pairs={{0,1},{1,0},{2,3},{3,2},{4,5},{5,4},{6,7},{7,6},{8,9},{9,8},{10,11... | collective-permute-start | bytes 589832 | tf_op jit(solution)/shard_map/ppermute | solution.py:657
  32.5 17.4 %collective-permute-start.12 = (bf16[2,64,768]{2,1,0:T(8,128)(2,1)S(1)}, bf16[2,64,768]{2,1,0:T(8,128)(2,1)S(1)}, u32[]{:S(2)}, u32[]{:S(2)}) collective-permute-start(bf16[2,64,768]{2,1,0:T(8,128)(2,1)S(1)} %pad_maximum_fusion.3.refs_1_), channel_id=1, source_target_pairs={{0,24},{4,28},{8,16},{12,20},{16,8},{20,12},{24,0},{28,4},{1,25},{... | collective-permute-start | bytes 589832 | tf_op jit(solution)/shard_map/ppermute | solution.py:653
  44.7 6.9 %collective-permute-start.18 = (bf16[192,512]{1,0:T(8,128)(2,1)S(1)}, bf16[192,512]{1,0:T(8,128)(2,1)S(1)}, u32[]{:S(2)}, u32[]{:S(2)}) collective-permute-start(bf16[192,512]{1,0:T(8,128)(2,1)S(1)} %get-tuple-element.66.refs_9_.att_a), channel_id=1, source_target_pairs={{0,2},{1,3},{2,0},{3,1},{4,6},{5,7},{6,4},{7,5},{8,10},{9,11},{10,... | collective-permute-start | bytes 589832 | tf_op jit(solution)/shard_map/ppermute | solution.py:657
  49.9 2.2 %collective-permute-start.13 = (bf16[2,64,768]{2,1,0:T(8,128)(2,1)S(1)}, bf16[2,64,768]{2,1,0:T(8,128)(2,1)S(1)}, u32[]{:S(2)}, u32[]{:S(2)}) collective-permute-start(bf16[2,64,768]{2,1,0:T(8,128)(2,1)S(1)} %pad_maximum_fusion.3.refs_1_), channel_id=1, source_target_pairs={{0,1},{1,0},{2,3},{3,2},{4,5},{5,4},{6,7},{7,6},{8,9},{9,8},{10,11... | collective-permute-start | bytes 589832 | tf_op jit(solution)/shard_map/ppermute | solution.py:657
  50.0 2.2 %collective-permute-start.14 = (bf16[2,64,768]{2,1,0:T(8,128)(2,1)S(1)}, bf16[2,64,768]{2,1,0:T(8,128)(2,1)S(1)}, u32[]{:S(2)}, u32[]{:S(2)}) collective-permute-start(bf16[2,64,768]{2,1,0:T(8,128)(2,1)S(1)} %copy-done.19), channel_id=1, source_target_pairs={{0,1},{1,0},{2,3},{3,2},{4,5},{5,4},{6,7},{7,6},{8,9},{9,8},{10,11... | collective-permute-start | bytes 589832 | tf_op jit(solution)/shard_map/ppermute | solution.py:657
  50.5 2.1 %collective-permute-start.15 = (bf16[2,64,768]{2,1,0:T(8,128)(2,1)}, bf16[2,64,768]{2,1,0:T(8,128)(2,1)S(1)}, u32[]{:S(2)}, u32[]{:S(2)}) collective-permute-start(bf16[2,64,768]{2,1,0:T(8,128)(2,1)} %collective-permute-done.11.refs_3_), channel_id=1, source_target_pairs={{0,1},{1,0},{2,3},{3,2},{4,5},{5,4},{6,7},{7,6},{8,9},{9,8},{10,11... | collective-permute-start | bytes 589832 | tf_op jit(solution)/shard_map/ppermute | solution.py:657
  51.6 4.0 %collective-permute-start.22 = (bf16[192,768]{1,0:T(8,128)(2,1)S(1)}, bf16[192,768]{1,0:T(8,128)(2,1)S(1)}, u32[]{:S(2)}, u32[]{:S(2)}) collective-permute-start(bf16[192,768]{1,0:T(8,128)(2,1)S(1)} %slice.4), channel_id=1, source_target_pairs={{0,1},{1,0},{2,3},{3,2},{4,5},{5,4},{6,7},{7,6},{8,9},{9,8},{10,11... | collective-permute-start | bytes 884744 | tf_op jit(solution)/shard_map/ppermute | solution.py:657
  52.1 1.5 %collective-permute-start.16 = (bf16[2,64,768]{2,1,0:T(8,128)(2,1)S(1)}, bf16[2,64,768]{2,1,0:T(8,128)(2,1)S(1)}, u32[]{:S(2)}, u32[]{:S(2)}) collective-permute-start(bf16[2,64,768]{2,1,0:T(8,128)(2,1)S(1)} %collective-permute-done.12.refs_4_), channel_id=1, source_target_pairs={{0,1},{1,0},{2,3},{3,2},{4,5},{5,4},{6,7},{7,6},{8,9},{9,8},{10,11... | collective-permute-start | bytes 589832 | tf_op jit(solution)/shard_map/ppermute | solution.py:657
  52.2 1.8 %collective-permute-start.17 = (bf16[192,512]{1,0:T(8,128)(2,1)S(1)}, bf16[192,512]{1,0:T(8,128)(2,1)S(1)}, u32[]{:S(2)}, u32[]{:S(2)}) collective-permute-start(bf16[192,512]{1,0:T(8,128)(2,1)S(1)} %get-tuple-element.66.refs_9_.att_a), channel_id=1, source_target_pairs={{0,1},{1,0},{2,3},{3,2},{4,5},{5,4},{6,7},{7,6},{8,9},{9,8},{10,11... | collective-permute-start | bytes 589832 | tf_op jit(solution)/shard_map/ppermute | solution.py:657
  52.6 2.8 %collective-permute-start.19 = (bf16[192,512]{1,0:T(8,128)(2,1)S(1)}, bf16[192,512]{1,0:T(8,128)(2,1)S(1)}, u32[]{:S(2)}, u32[]{:S(2)}) collective-permute-start(bf16[192,512]{1,0:T(8,128)(2,1)S(1)} %collective-permute-done.18.refs_11_), channel_id=1, source_target_pairs={{0,1},{1,0},{2,3},{3,2},{4,5},{5,4},{6,7},{7,6},{8,9},{9,8},{10,11... | collective-permute-start | bytes 589832 | tf_op jit(solution)/shard_map/ppermute | solution.py:657
  53.6 11.8 %collective-permute-start.24 = (bf16[192,512]{1,0:T(8,128)(2,1)S(1)}, bf16[192,512]{1,0:T(8,128)(2,1)S(1)}, u32[]{:S(2)}, u32[]{:S(2)}) collective-permute-start(bf16[192,512]{1,0:T(8,128)(2,1)S(1)} %get-tuple-element.111.refs_1_.att_b), channel_id=1, source_target_pairs={{0,1},{1,0},{2,3},{3,2},{4,5},{5,4},{6,7},{7,6},{8,9},{9,8},{10,11... | collective-permute-start | bytes 589832 | tf_op jit(solution)/shard_map/ppermute | solution.py:657
  54.0 11.4 %collective-permute-start.25 = (bf16[192,512]{1,0:T(8,128)(2,1)S(1)}, bf16[192,512]{1,0:T(8,128)(2,1)S(1)}, u32[]{:S(2)}, u32[]{:S(2)}) collective-permute-start(bf16[192,512]{1,0:T(8,128)(2,1)S(1)} %get-tuple-element.111.refs_1_.att_b), channel_id=1, source_target_pairs={{0,2},{1,3},{2,0},{3,1},{4,6},{5,7},{6,4},{7,5},{8,10},{9,11},{10,... | collective-permute-start | bytes 589832 | tf_op jit(solution)/shard_map/ppermute | solution.py:657
  55.5 9.9 %collective-permute-start.26 = (bf16[192,512]{1,0:T(8,128)(2,1)S(1)}, bf16[192,512]{1,0:T(8,128)(2,1)S(1)}, u32[]{:S(2)}, u32[]{:S(2)}) collective-permute-start(bf16[192,512]{1,0:T(8,128)(2,1)S(1)} %get-tuple-element.111.refs_1_.att_b), channel_id=1, source_target_pairs={{0,3},{1,2},{2,1},{3,0},{4,7},{5,6},{6,5},{7,4},{8,11},{9,10},{10,... | collective-permute-start | bytes 589832 | tf_op jit(solution)/shard_map/ppermute | solution.py:657
  74.2 3.1 %collective-permute-start.29 = (bf16[512,768]{1,0:T(8,128)(2,1)S(1)}, bf16[512,768]{1,0:T(8,128)(2,1)S(1)}, u32[]{:S(2)}, u32[]{:S(2)}) collective-permute-start(bf16[512,768]{1,0:T(8,128)(2,1)S(1)} %get-tuple-element.94.refs_7_), channel_id=1, source_target_pairs={{0,1},{1,0},{2,3},{3,2},{4,5},{5,4},{6,7},{7,6},{8,9},{9,8},{10,11... | collective-permute-start | bytes 2359304 | tf_op jit(solution)/shard_map/ppermute | solution.py:657
  74.7 3.0 %collective-permute-start.28 = (bf16[512,768]{1,0:T(8,128)(2,1)S(1)}, bf16[512,768]{1,0:T(8,128)(2,1)S(1)}, u32[]{:S(2)}, u32[]{:S(2)}) collective-permute-start(bf16[512,768]{1,0:T(8,128)(2,1)S(1)} %get-tuple-element.93.refs_6_), channel_id=1, source_target_pairs={{0,1},{1,0},{2,3},{3,2},{4,5},{5,4},{6,7},{7,6},{8,9},{9,8},{10,11... | collective-permute-start | bytes 2359304 | tf_op jit(solution)/shard_map/ppermute | solution.py:657
  93.4 1.6 %collective-permute-start.30 = (bf16[144,768]{1,0:T(8,128)(2,1)S(1)}, bf16[144,768]{1,0:T(8,128)(2,1)S(1)}, u32[]{:S(2)}, u32[]{:S(2)}) collective-permute-start(bf16[144,768]{1,0:T(8,128)(2,1)S(1)} %get-tuple-element.110.message), channel_id=1, source_target_pairs={{0,1},{1,0},{2,3},{3,2},{4,5},{5,4},{6,7},{7,6},{8,9},{9,8},{10,11... | collective-permute-start | bytes 663560 | tf_op jit(solution)/shard_map/ppermute | solution.py:657
  93.8 3.4 %collective-permute-start.27 = (bf16[128,768]{1,0:T(8,128)(2,1)}, bf16[128,768]{1,0:T(8,128)(2,1)}, u32[]{:S(2)}, u32[]{:S(2)}) collective-permute-start(bf16[128,768]{1,0:T(8,128)(2,1)} %get-tuple-element.86.part), channel_id=1, source_target_pairs={{0,1},{1,0},{2,3},{3,2},{4,5},{5,4},{6,7},{7,6},{8,9},{9,8},{10,11... | collective-permute-start | bytes 589832 | tf_op jit(solution)/shard_map/ppermute | solution.py:657
  95.0 7.8 %collective-permute-start.31 = (bf16[144,768]{1,0:T(8,128)(2,1)S(1)}, bf16[144,768]{1,0:T(8,128)(2,1)S(1)}, u32[]{:S(2)}, u32[]{:S(2)}) collective-permute-start(bf16[144,768]{1,0:T(8,128)(2,1)S(1)} %shard_map.149.mine), channel_id=1, source_target_pairs={{0,2},{1,3},{2,0},{3,1},{4,6},{5,7},{6,4},{7,5},{8,10},{9,11},{10,... | collective-permute-start | bytes 663560 | tf_op jit(solution)/shard_map/ppermute | solution.py:657
  (31 other events, 259.6 us)

commit v4 on v3

--- a/solution.py
+++ b/solution.py
@@ -365,7 +365,7 @@
         loop(att.shape[1] // chunk, one_chunk, att.shape[1] // chunk)
 
     lse[...] = jnp.zeros_like(lse)
-    loop(heads, one_head)
+    loop(heads, one_head, heads)
 
 
 def project_kernel(heads, ids, place, own, *refs):
@@ -422,10 +422,11 @@
     if turn == 0:
         cot_own, near, far = refs[0], refs[1 : 1 + count], refs[1 + count : 1 + 2 * count]
         refs = refs[1 + 2 * count :]
-        atts, attns, (in_own, in_far, mlp_own, rest_far) = refs[:4], refs[4:7], refs[7:11]
-        attns = [*attns[:2], rest_far.at[mlp_own.shape[0] :, :], attns[2]]
-        gain, cot, attn, w_in, w_mlp, tok_next = refs[11:17]
-        refs = refs[17:]
+        atts, attns, (in_own, in_side, in_rest, mlp_own, rest_far) = refs[:4], refs[4:7], refs[7:12]
+        units_here = mlp_own.shape[0]
+        attns = [*attns[:2], rest_far.at[units_here:, :], attns[2].at[units_here:, :]]
+        gain, cot, attn, w_in, w_mlp, tok_next = refs[12:18]
+        refs = refs[18:]
     else:
         cot, atts, (gain, attn, w_in, w_mlp), refs = refs[0], refs[1:5], refs[5:9], refs[9:]
         (mid_before, out_before), refs = refs[:2], refs[2:]
@@ -452,18 +453,21 @@
             first_loads.append(move.load(attns[p], attn.at[spot, :]))
     in_loads, mlp_loads = [], []
     if turn == 0:
-        for source, r in ((in_own, side), (in_far, 1 - side)):
-            for part in range(2):
-                spot = pl.ds(pl.multiple_of((r + 2 * part) * units, units), units)
-                rows = source.at[part * units : (part + 1) * units, :]
-                in_loads.append(move.load(rows, w_in.at[spot, :]))
+        row = here % 2
+        for part in range(2):
+            spot = pl.ds(pl.multiple_of((side + 2 * part) * units, units), units)
+            rows = in_own.at[part * units : (part + 1) * units, :]
+            in_loads.append(move.load(rows, w_in.at[spot, :]))
+        for part, source in ((row, in_side), (1 - row, in_rest)):
+            spot = pl.ds(pl.multiple_of((1 - side + 2 * part) * units, units), units)
+            in_loads.append(move.load(source, w_in.at[spot, :]))
         for source, r in ((mlp_own, side), (rest_far, 1 - side)):
             spot = pl.ds(pl.multiple_of(r * units, units), units)
             mlp_loads.append(move.load(source.at[:units, :], w_mlp.at[spot, :]))
         mlp_loads += load_pieces(move, place, cot, cot_own, near, far, ids)
         mlp_loads.append(move.load(tok_in.at[tokens:, :], tok_next))
     wait_all(first_loads)
-    chunk = 256
+    chunk = 512
 
     def one_chunk(i):
         at = part_of(i, chunk)
@@ -536,7 +540,7 @@
     spots = turns // rows
     gain_v[...] = jnp.zeros_like(gain_v)
 
-    def norm_block(turn, b, carry):
+    def norm_block(turn, b):
         here_at = pl.ds(pl.multiple_of(b * rows, rows), rows)
         at = pl.ds(pl.multiple_of((b + turn * spots) * rows, rows), rows)
         second = parts[turn][here_at, :].astype(F32) + fars[turn][here_at, :].astype(F32)
@@ -550,10 +554,8 @@
         def _():
             own_v[...] = grad
 
-        return carry
-
     for turn in range(2):
-        lax.fori_loop(0, spots, functools.partial(norm_block, turn), 0)
+        loop(spots, functools.partial(norm_block, turn), 2)
     chunk = 256
 
     def grad_chunk(i):
@@ -588,15 +590,15 @@
             delta = jnp.sum(out_grad.astype(F32) * exact, axis=0, keepdims=True)
             score_grad = (chances * (chance_grad - delta)).astype(BF16)
             query_grad = mm(qkv[rows_k, :], score_grad) * scale
-            key_grad[...] += mm(score_grad, query.T)
-            value_grad[...] += mm(chances.astype(BF16), out_grad.T)
+            key_grad[...] += mm(query, score_grad, NT)
+            value_grad[...] += mm(out_grad, chances.astype(BF16), NT)
             grad_v[rows_q, at] = turn_back(query_grad, cosine[:, at], sine[:, at])
 
         loop(tokens // chunk, one_chunk, tokens // chunk)
-        grad_v[rows_k, :] = turn_back(key_grad[...].T, cosine[...], sine[...])
-        grad_v[rows_v, :] = value_grad[...].T.astype(BF16)
-
-    loop(heads, one_head)
+        grad_v[rows_k, :] = turn_back(key_grad[...], cosine[...], sine[...])
+        grad_v[rows_v, :] = value_grad[...].astype(BF16)
+
+    loop(heads, one_head, heads)
     own = pl.ds(pl.multiple_of(here * rows, rows), rows)
     message[:rows, :] = mm(grad_v[:, own].T, weight[...]).astype(BF16)
     gain_row = jnp.zeros_like(gain_v)
@@ -618,7 +620,7 @@
 
 def last_kernel(mine, far, tokens, gain, middle_grad, tokens_grad, gain_grad):
     rows = tokens.shape[0]
-    gain_grad[...] = sum_rows(mine[rows:, :]) + sum_rows(far[rows:, :])
+    gain_grad[...] = (sum_rows(mine[rows:, :]) + sum_rows(far[rows:, :]))[0]
     first_grad = mine[:rows, :].astype(F32) + far[:rows, :].astype(F32)
     normed, scale = norm_parts(tokens[...].astype(F32))
     back = norm_back(first_grad * gain[...], normed, scale)
@@ -676,13 +678,16 @@
 
 
 def gather_cotangent(block, core, spots, after, gate):
-    half = half_of(block, core)
-    pair = jnp.stack([half, over_ctx(half, 1, spots)])
-    pair, _ = lax.optimization_barrier((pair, after))
-    near = [pair] + [over_ctx(pair, step, spots) for step in range(2, spots, 2)]
-    ids = tuple((step, step + 1) for step in range(0, spots, 2))
+    near = half_of(block, core)[None]
+    ids, step = (0,), 1
+    while step < spots:
+        if step == 2:
+            near, _ = lax.optimization_barrier((near, after))
+        near = jnp.concatenate([near, over_ctx(near, step, spots)], axis=0)
+        ids += tuple(i + step for i in ids)
+        step *= 2
     near, _ = lax.optimization_barrier((near, gate))
-    return near, [swap(piece, 1) for piece in near], ids
+    return [near], [swap(near, 1)], (ids,)
 
 
 def replicated_body(
@@ -712,10 +717,12 @@
 
     near, far, ids, steps = gather_tokens(tokens, core, spots)
     attn_core = swap(attn_weight, 1)
-    in_side = swap(in_t, 2)
+    in_part = lax.dynamic_index_in_dim(in_t.reshape(2, units, width), here % 2, 0, keepdims=False)
+    in_side = swap(in_part, 2)
+    in_rest = over_ctx(in_side, 1, spots)
     rest = jnp.concatenate([mlp_weight, attn_weight], axis=0)
     rest_side = swap(rest, 2)
-    attn_both = swap(rest_side[units:], 1)
+    rest_both = swap(rest_side, 1)
     half_rows = total_rows // 2
     tall, wide = (total_rows, width), (half_rows, width)
     cells = heads * total_rows * half_rows
@@ -753,7 +760,7 @@
         [qkv],
         scratch=[((total_rows, HEAD), BF16)],
     )
-    cot_near, cot_far, cot_ids = gather_cotangent(cotangent, core, spots, steps[-1], att_b)
+    cot_near, cot_far, cot_ids = gather_cotangent(cotangent, core, spots, steps[-1], att_a)
     side_a, _ = lax.optimization_barrier((side_a, att_b))
     atts_a = [att_a, swap(att_a, 1), side_a, swap(side_a, 1)]
     halves = [
@@ -788,8 +795,8 @@
             *map(Away, [tok_all, cotangent, *cot_near, *cot_far]),
             att_a,
             *map(Away, atts_a[1:]),
-            *map(Away, [attn_weight, attn_core, attn_both]),
-            *map(Away, [in_t, in_side, mlp_weight, rest_side]),
+            *map(Away, [attn_weight, attn_core, rest_both]),
+            *map(Away, [in_t, in_side, in_rest, mlp_weight, rest_side]),
             second_row,
         ],
         scratch=[(wide, BF16), *room],
@@ -798,8 +805,9 @@
         cells=4 * units * half_rows,
         room=20,
     )
-    atts_b = [att_b, *[swap(att_b, mask) for mask in (1, 2, 3)]]
-    atts_b, _ = lax.optimization_barrier((atts_b, cot_all))
+    att_core_b = swap(att_b, 1)
+    side_b, _ = lax.optimization_barrier((swap(att_b, 2), cot_all))
+    atts_b = [att_b, att_core_b, side_b, swap(side_b, 1)]
     results_b = call(
         functools.partial(mlp_kernel, 1, ()),
         halves,
@@ -870,8 +878,8 @@
             ((8, total_rows), F32),
             ((total_rows, HEAD), BF16),
             ((total_rows, HEAD), BF16),
-            ((total_rows, HEAD), F32),
-            ((total_rows, HEAD), F32),
+            ((HEAD, total_rows), F32),
+            ((HEAD, total_rows), F32),
             ((3 * local, width), F32),
         ],
         copies=4,
@@ -893,14 +901,14 @@
     )
     tokens_grad, first_gain_grad = call(
         last_kernel,
-        [jax.ShapeDtypeStruct((rows, width), BF16), jax.ShapeDtypeStruct((1, width), F32)],
+        [jax.ShapeDtypeStruct((rows, width), BF16), jax.ShapeDtypeStruct((width,), F32)],
         [mine, far, tokens, first_gain[None, :], middle_grad],
         flops=16 * rows * width,
     )
     return (
         output,
         tokens_grad,
-        first_gain_grad[0],
+        first_gain_grad,
         jnp.transpose(qkv_grad.reshape(3, local, width), (2, 0, 1)),
         attn_grad,
         second_gain_grad[0],

time: 105 us -> 103 us (0.981)
  Pallas kernels: 53.3 us -> 51.5 us
    pallas_call x9, Pallas kernels: 53.3 us -> 51.5 us  [call(): pl.pallas_call(kernel, out_shape=[o.value if isinstance(o, Away) else o f...]
    unnamed x62 -> x52, local copies, waits for them, and re-layouts: 1.63 us -> 2.65 us
    ppermute x23 -> x20, waiting for transfers between devices: 5.65 us -> 6.41 us  [swap(): return lax.ppermute(value, 'wt', [(spot, spot ^ mask) for spot in range(4)])]
    ppermute x23 -> x20, starting transfers between devices: 11.1 us -> 10.8 us  [swap(): return lax.ppermute(value, 'wt', [(spot, spot ^ mask) for spot in range(4)])]
  transfers between devices with their start and end apart: 32 -> 29, of which waited for: 9 -> 10; matrix products, arithmetic and copies ran while one was open for 4% -> 3% of each run, Pallas kernels for 27% -> 34%
where the time goes in v4:
time: 103 us
  Pallas kernels  51.5 us (50%)
  starting transfers between devices  28.2 us (27%)
  waiting for transfers between devices  14.8 us (14%)
  local copies, waits for them, and re-layouts  4.56 us (4%)
  other arithmetic  2.55 us (2%)
  between operations  1.11 us (1%)
    pallas_call x9, Pallas kernels, call(): pl.pallas_call(kernel, out_shape=[o.value if isinstance(o, Away) else o f...  51.5 us
    ppermute x9, starting transfers between devices, over_ctx(): lax.ppermute(value, 'ctx', [(spot, spot ^ step) for spot in range(spots)])  17.5 us
    ppermute x20, starting transfers between devices, swap(): return lax.ppermute(value, 'wt', [(spot, spot ^ mask) for spot in range(4)])  10.8 us
    ppermute x9, waiting for transfers between devices, over_ctx(): lax.ppermute(value, 'ctx', [(spot, spot ^ step) for spot in range(spots)])  8.35 us
    ppermute x20, waiting for transfers between devices, swap(): return lax.ppermute(value, 'wt', [(spot, spot ^ mask) for spot in range(4)])  6.41 us
    unnamed x52, local copies, waits for them, and re-layouts  2.65 us
  transfers between devices with their start and end apart: 29, of which 10 were waited for; matrix products, arithmetic and copies ran while one was open for 3% of the time, Pallas kernels for 34%

profile of v4, /device:TPU:0, one launch (start us, length us, event | category | flops | bytes accessed | tf_op | source)
XLA Modules:
  0.0 102.7 jit_solution(5967670731450045665)
XLA Ops:
  0.7 1.0 constant_dynamic-slice_fusion
  1.6 4.0 %collective-permute-start.2 = (bf16[64,768]{1,0:T(8,128)(2,1)S(1)}, bf16[64,768]{1,0:T(8,128)(2,1)S(1)}, u32[]{:S(2)}, u32[]{:S(2)}) collective-permute-start(bf16[64,768]{1,0:T(8,128)(2,1)S(1)} %constant_dynamic-slice_fusion), channel_id=1, source_target_pairs={{0,16},{4,20},{8,24},{12,28},{16,0},{20,4},{24,8},{28,12},{1,17},{... | collective-permute-start | bytes 294920 | tf_op jit(solution)/shard_map/ppermute | solution.py:655
  5.7 1.3 %collective-permute-start.3 = (bf16[64,768]{1,0:T(8,128)(2,1)S(1)}, bf16[64,768]{1,0:T(8,128)(2,1)S(1)}, u32[]{:S(2)}, u32[]{:S(2)}) collective-permute-start(bf16[64,768]{1,0:T(8,128)(2,1)S(1)} %constant_dynamic-slice_fusion), channel_id=1, source_target_pairs={{0,24},{4,28},{8,16},{12,20},{16,8},{20,12},{24,0},{28,4},{1,25},{... | collective-permute-start | bytes 294920 | tf_op jit(solution)/shard_map/ppermute | solution.py:655
  7.2 0.9 dynamic-slice_bitcast_fusion.1
  8.2 1.6 %collective-permute-start.9 = (bf16[1,64,768]{2,1,0:T(8,128)(2,1)S(1)}, bf16[1,64,768]{2,1,0:T(8,128)(2,1)S(1)}, u32[]{:S(2)}, u32[]{:S(2)}) collective-permute-start(bf16[1,64,768]{2,1,0:T(8,128)(2,1)S(1)} %dynamic-slice_bitcast_fusion.1), channel_id=1, source_target_pairs={{0,4},{4,0},{8,12},{12,8},{16,20},{20,16},{24,28},{28,24},{1,5},{5... | collective-permute-start | bytes 294920 | tf_op jit(solution)/shard_map/ppermute | solution.py:655
  9.7 1.2 %pad_maximum_fusion.1 = bf16[480,768]{1,0:T(8,128)(2,1)S(1)} fusion(bf16[192,768]{1,0:T(8,128)(2,1)} %refs_12_.1, bf16[288,768]{1,0:T(8,128)(2,1)} %refs_13_.1), kind=kLoop, calls=%fused_computation.1 | loop fusion | flops 1474560 | bytes 1474560 | tf_op jit(solution)/shard_map/concatenate | solution.py:723
  10.9 1.6 %collective-permute-start.17 = (bf16[480,768]{1,0:T(8,128)(2,1)S(1)}, bf16[480,768]{1,0:T(8,128)(2,1)}, u32[]{:S(2)}, u32[]{:S(2)}) collective-permute-start(bf16[480,768]{1,0:T(8,128)(2,1)S(1)} %pad_maximum_fusion.1), channel_id=1, source_target_pairs={{0,2},{1,3},{2,0},{3,1},{4,6},{5,7},{6,4},{7,5},{8,10},{9,11},{10,... | collective-permute-start | bytes 2211848 | tf_op jit(solution)/shard_map/ppermute | solution.py:659
  12.9 2.7 %collective-permute-start.10 = (bf16[2,64,768]{2,1,0:T(8,128)(2,1)S(1)}, bf16[2,64,768]{2,1,0:T(8,128)(2,1)S(1)}, u32[]{:S(2)}, u32[]{:S(2)}) collective-permute-start(bf16[2,64,768]{2,1,0:T(8,128)(2,1)S(1)} %pad_maximum_fusion.5), channel_id=1, source_target_pairs={{0,8},{4,12},{8,0},{12,4},{16,24},{20,28},{24,16},{28,20},{1,9},{5... | collective-permute-start | bytes 589832 | tf_op jit(solution)/shard_map/ppermute | solution.py:655
  15.6 1.6 %collective-permute-start.4 = (bf16[2,64,768]{2,1,0:T(8,128)(2,1)S(1)}, bf16[2,64,768]{2,1,0:T(8,128)(2,1)S(1)}, u32[]{:S(2)}, u32[]{:S(2)}) collective-permute-start(bf16[2,64,768]{2,1,0:T(8,128)(2,1)S(1)} %pad_maximum_fusion.4.refs_2_), channel_id=1, source_target_pairs={{0,4},{4,0},{8,12},{12,8},{16,20},{20,16},{24,28},{28,24},{1,5},{5... | collective-permute-start | bytes 589832 | tf_op jit(solution)/shard_map/ppermute | solution.py:655
  17.8 2.8 %collective-permute-done.10 = bf16[2,64,768]{2,1,0:T(8,128)(2,1)S(1)} collective-permute-done((bf16[2,64,768]{2,1,0:T(8,128)(2,1)S(1)}, bf16[2,64,768]{2,1,0:T(8,128)(2,1)S(1)}, u32[]{:S(2)}, u32[]{:S(2)}) %collective-permute-start.10) | collective-permute-done | bytes 196640 | tf_op jit(solution)/shard_map/ppermute | solution.py:655
  20.7 3.7 %collective-permute-start.11 = (bf16[4,64,768]{2,1,0:T(8,128)(2,1)S(1)}, bf16[4,64,768]{2,1,0:T(8,128)(2,1)S(1)}, u32[]{:S(2)}, u32[]{:S(2)}) collective-permute-start(bf16[4,64,768]{2,1,0:T(8,128)(2,1)S(1)} %pad_maximum_fusion.2), channel_id=1, source_target_pairs={{0,16},{4,20},{8,24},{12,28},{16,0},{20,4},{24,8},{28,12},{1,17},{... | collective-permute-start | bytes 1179656 | tf_op jit(solution)/shard_map/ppermute | solution.py:655
  24.6 1.9 %collective-permute-done.1.refs_1_ = bf16[2,64,768]{2,1,0:T(8,128)(2,1)} collective-permute-done((bf16[2,64,768]{2,1,0:T(8,128)(2,1)S(1)}, bf16[2,64,768]{2,1,0:T(8,128)(2,1)}, u32[]{:S(2)}, u32[]{:S(2)}) %collective-permute-start.1) | collective-permute-done | bytes 196640 | tf_op jit(solution)/shard_map/ppermute | solution.py:655
  27.6 1.6 %collective-permute-start.19 = (bf16[288,768]{1,0:T(8,128)(2,1)S(1)}, bf16[288,768]{1,0:T(8,128)(2,1)S(1)}, u32[]{:S(2)}, u32[]{:S(2)}) collective-permute-start(bf16[288,768]{1,0:T(8,128)(2,1)S(1)} %dynamic-slice_bitcast_fusion), channel_id=1, source_target_pairs={{0,2},{1,3},{2,0},{3,1},{4,6},{5,7},{6,4},{7,5},{8,10},{9,11},{10,... | collective-permute-start | bytes 1327112 | tf_op jit(solution)/shard_map/ppermute | solution.py:659
  29.9 9.0 %shard_map.143 = (bf16[1024,768]{1,0:T(8,128)(2,1)}, bf16[1024,768]{1,0:T(8,128)(2,1)S(1)}, bf16[576,1024]{1,0:T(8,128)(2,1)S(1)}, bf16[192,512]{1,0:T(8,128)(2,...) custom-call(s32[4]{0:T(128)S(1)} %pad_add_fusion.place, bf16[128,768]{1,0:T(8,128)(2,1)} %tokens.1, ...), custom_call_target="tpu_custom_call" | custom-call | tf_op jit(solution)/shard_map/pallas_call | solution.py:277
  38.9 2.4 %collective-permute-done.11 = bf16[4,64,768]{2,1,0:T(8,128)(2,1)S(1)} collective-permute-done((bf16[4,64,768]{2,1,0:T(8,128)(2,1)S(1)}, bf16[4,64,768]{2,1,0:T(8,128)(2,1)S(1)}, u32[]{:S(2)}, u32[]{:S(2)}) %collective-permute-start.11) | collective-permute-done | bytes 393248 | tf_op jit(solution)/shard_map/ppermute | solution.py:655
  42.1 1.7 %collective-permute-start.20 = (bf16[288,768]{1,0:T(8,128)(2,1)S(1)}, bf16[288,768]{1,0:T(8,128)(2,1)S(1)}, u32[]{:S(2)}, u32[]{:S(2)}) collective-permute-start(bf16[288,768]{1,0:T(8,128)(2,1)S(1)} %collective-permute-done.19.refs_11_), channel_id=1, source_target_pairs={{0,4},{4,0},{8,12},{12,8},{16,20},{20,16},{24,28},{28,24},{1,5},{5... | collective-permute-start | bytes 1327112 | tf_op jit(solution)/shard_map/ppermute | solution.py:655
  43.9 1.5 %collective-permute-start.14 = (bf16[192,512]{1,0:T(8,128)(2,1)S(1)}, bf16[192,512]{1,0:T(8,128)(2,1)S(1)}, u32[]{:S(2)}, u32[]{:S(2)}) collective-permute-start(bf16[192,512]{1,0:T(8,128)(2,1)S(1)} %get-tuple-element.61.refs_3_.att_a), channel_id=1, source_target_pairs={{0,2},{1,3},{2,0},{3,1},{4,6},{5,7},{6,4},{7,5},{8,10},{9,11},{10,... | collective-permute-start | bytes 589832 | tf_op jit(solution)/shard_map/ppermute | solution.py:659
  45.4 4.4 %shard_map.144 = (bf16[192,512]{1,0:T(8,128)(2,1)S(1)}, f32[192,512]{1,0:T(8,128)S(1)}, f32[8,512]{1,0:T(8,128)S(1)}) custom-call(bf16[576,1024]{1,0:T(8,128)(2,1)S(1)} %get-tuple-element.65.qkv.refs_13_), custom_call_target="tpu_custom_call" | custom-call | tf_op jit(solution)/shard_map/pallas_call | solution.py:277
  49.7 1.1 %collective-permute-done.14.refs_5_ = bf16[192,512]{1,0:T(8,128)(2,1)S(1)} collective-permute-done((bf16[192,512]{1,0:T(8,128)(2,1)S(1)}, bf16[192,512]{1,0:T(8,128)(2,1)S(1)}, u32[]{:S(2)}, u32[]{:S(2)}) %collective-permute-start.14) | collective-permute-done | bytes 196640 | tf_op jit(solution)/shard_map/ppermute | solution.py:659
  51.4 0.9 collective-permute-done.13.refs_4_
  52.3 1.5 %collective-permute-start.22 = (bf16[192,512]{1,0:T(8,128)(2,1)S(1)}, bf16[192,512]{1,0:T(8,128)(2,1)S(1)}, u32[]{:S(2)}, u32[]{:S(2)}) collective-permute-start(bf16[192,512]{1,0:T(8,128)(2,1)S(1)} %get-tuple-element.101.refs_1_.att_b), channel_id=1, source_target_pairs={{0,2},{1,3},{2,0},{3,1},{4,6},{5,7},{6,4},{7,5},{8,10},{9,11},{10,... | collective-permute-start | bytes 589832 | tf_op jit(solution)/shard_map/ppermute | solution.py:659
  53.8 0.9 collective-permute-done.20.refs_12_
  55.9 8.4 %shard_map.145 = (bf16[1024,768]{1,0:T(8,128)(2,1)S(1)}, bf16[768,768]{1,0:T(8,128)(2,1)S(1)}, bf16[1152,768]{1,0:T(8,128)(2,1)S(1)}, bf16[576,768]{1,0:T(8,128)...) custom-call(s32[4]{0:T(128)S(1)} %pad_add_fusion.place, ...), custom_call_target="tpu_custom_call" | custom-call | flops 2868903936 | bytes 8408080 | tf_op jit(solution)/shard_map/pallas_call | solution.py:277
  65.0 0.9 collective-permute-done.23.refs_4_
  66.6 7.7 %shard_map.146 = (f32[512,768]{1,0:T(8,128)S(1)}, bf16[512,768]{1,0:T(8,128)(2,1)S(1)}, bf16[288,512]{1,0:T(8,128)(2,1)S(1)}, bf16[576,512]{1,0:T(8,128)(2,1)S(1...) custom-call(s32[4]{0:T(128)S(1)} %pad_add_fusion.place, ...), custom_call_target="tpu_custom_call" | custom-call | flops 2868903936 | bytes 7572496 | tf_op jit(solution)/shard_map/pallas_call | solution.py:277
  74.4 2.5 %shard_map.147 = (f32[576,768]{1,0:T(8,128)}, f32[288,768]{1,0:T(8,128)}) custom-call(bf16[576,512]{1,0:T(8,128)(2,1)S(1)} %get-tuple-element.85.gate_a, bf16[576,512]{1,0:T(8,128)(2,1)S(1)} %get-tuple-element.86.gate_b, bf16[288,512]{1,0:T(8,128)(2,1)S(1)} %get-tuple-element.87.hidden_a, bf16[288,512]{1,0:T(8,128)(2,1)S(1)} %get-tuple-element.88.hidden_b, ...), custom_call_target="tpu_custom_call" | custom-call | flops 1358954496 | bytes 4915200 | tf_op jit(solution)/shard_map/pallas_call | solution.py:277
  77.0 15.3 %shard_map.148 = (f32[1,768]{1,0:T(1,128)S(1)}, bf16[1024,768]{1,0:T(8,128)(2,1)S(1)}, f32[128,768]{1,0:T(8,128)S(1)}, bf16[144,768]{1,0:T(8,128)(2,1)S(1)}, f32[576,768]{1,0:T(8,128)}) custom-call(s32[4]{0:T(128)S(1)} %pad_add_fusion.place, f32[512,768]{1,0:T(8,128)S(1)} %get-tuple-element.77.refs_0_, f32[512,768]{1,0:T(8,128)S(1)} %get-tuple-element.78.refs_1_, ...), custom_call_target="tpu_custom_call" | custom-call | flops 9261023232 | bytes 12892176 | tf_op jit(solution)/shard_map/pallas_call | solution.py:277
  92.9 1.0 collective-permute-done.27.far
  93.9 1.6 %collective-permute-start.28 = (bf16[144,768]{1,0:T(8,128)(2,1)S(1)}, bf16[144,768]{1,0:T(8,128)(2,1)S(1)}, u32[]{:S(2)}, u32[]{:S(2)}) collective-permute-start(bf16[144,768]{1,0:T(8,128)(2,1)S(1)} %shard_map.149.mine), channel_id=1, source_target_pairs={{0,2},{1,3},{2,0},{3,1},{4,6},{5,7},{6,4},{7,5},{8,10},{9,11},{10,... | collective-permute-start | bytes 663560 | tf_op jit(solution)/shard_map/ppermute | solution.py:659
  96.1 3.1 %shard_map.150 = (f32[192,768]{1,0:T(8,128)}, bf16[128,768]{1,0:T(8,128)(2,1)}) custom-call(bf16[192,512]{1,0:T(8,128)(2,1)S(1)} %get-tuple-element.61.refs_3_.att_a, bf16[192,512]{1,0:T(8,128)(2,1)S(1)} %get-tuple-element.101.refs_1_.att_b, bf16[1024,768]{1,0:T(8,128)(2,1)S(1)} %get-tuple-element.102.branch, f32[128,768]{1,0:T(8,128)S(1)} %get-tuple-element.103.middle, ...), custom_call_target="tpu_custom_call" | custom-call | flops 301989888 | bytes 2752512 | tf_op jit(solution)/shard_map/pallas_call | solution.py:277
  99.2 2.5 %collective-permute-done.28.far = bf16[144,768]{1,0:T(8,128)(2,1)S(1)} collective-permute-done((bf16[144,768]{1,0:T(8,128)(2,1)S(1)}, bf16[144,768]{1,0:T(8,128)(2,1)S(1)}, u32[]{:S(2)}, u32[]{:S(2)}) %collective-permute-start.28) | collective-permute-done | bytes 221216 | tf_op jit(solution)/shard_map/ppermute | solution.py:659
  101.7 1.0 %shard_map.151 = (bf16[128,768]{1,0:T(8,128)(2,1)}, f32[768]{0:T(1024)}) custom-call(bf16[144,768]{1,0:T(8,128)(2,1)S(1)} %shard_map.149.mine, bf16[144,768]{1,0:T(8,128)(2,1)S(1)} %collective-permute-done.28.far, bf16[128,768]{1,0:T(8,128)(2,1)S(1)} %copy-done.1, f32[1,768]{1,0:T(1,128)S(1)} %broadcast_in_dim.6.refs_8_.refs_22_.gain, ...), custom_call_target="tpu_custom_call" | custom-call | flops 1572864 | bytes 1035264 | tf_op jit(solution)/shard_map/pallas_call | solution.py:277
  (104 shorter events, 8.4 us)
Async XLA Ops:
  1.6 13.9 %collective-permute-start.2 = (bf16[64,768]{1,0:T(8,128)(2,1)S(1)}, bf16[64,768]{1,0:T(8,128)(2,1)S(1)}, u32[]{:S(2)}, u32[]{:S(2)}) collective-permute-start(bf16[64,768]{1,0:T(8,128)(2,1)S(1)} %constant_dynamic-slice_fusion), channel_id=1, source_target_pairs={{0,16},{4,20},{8,24},{12,28},{16,0},{20,4},{24,8},{28,12},{1,17},{... | collective-permute-start | bytes 294920 | tf_op jit(solution)/shard_map/ppermute | solution.py:655
  5.7 7.2 %collective-permute-start.3 = (bf16[64,768]{1,0:T(8,128)(2,1)S(1)}, bf16[64,768]{1,0:T(8,128)(2,1)S(1)}, u32[]{:S(2)}, u32[]{:S(2)}) collective-permute-start(bf16[64,768]{1,0:T(8,128)(2,1)S(1)} %constant_dynamic-slice_fusion), channel_id=1, source_target_pairs={{0,24},{4,28},{8,16},{12,20},{16,8},{20,12},{24,0},{28,4},{1,25},{... | collective-permute-start | bytes 294920 | tf_op jit(solution)/shard_map/ppermute | solution.py:655
  7.0 10.2 %collective-permute-start = (bf16[64,768]{1,0:T(8,128)(2,1)S(1)}, bf16[64,768]{1,0:T(8,128)(2,1)S(1)}, u32[]{:S(2)}, u32[]{:S(2)}) collective-permute-start(bf16[64,768]{1,0:T(8,128)(2,1)S(1)} %constant_dynamic-slice_fusion), channel_id=1, source_target_pairs={{0,8},{4,12},{8,0},{12,4},{16,24},{20,28},{24,16},{28,20},{1,9},{5... | collective-permute-start | bytes 294920 | tf_op jit(solution)/shard_map/ppermute | solution.py:655
  8.1 16.3 %copy-start.13 = (f32[768]{0:T(1024)S(1)}, f32[768]{0:T(1024)}, u32[]{:S(2)}) copy-start(f32[768]{0:T(1024)} %param.9) | copy-start | bytes 9220
  8.1 16.3 %copy-start.8 = (bf16[768,2,288]{0,2,1:T(8,128)(2,1)S(1)}, bf16[768,2,288]{0,2,1:T(8,128)(2,1)}, u32[]{:S(2)}) copy-start(bf16[768,2,288]{0,2,1:T(8,128)(2,1)} %param.13) | copy-start | bytes 2654212
  8.2 4.7 %collective-permute-start.9 = (bf16[1,64,768]{2,1,0:T(8,128)(2,1)S(1)}, bf16[1,64,768]{2,1,0:T(8,128)(2,1)S(1)}, u32[]{:S(2)}, u32[]{:S(2)}) collective-permute-start(bf16[1,64,768]{2,1,0:T(8,128)(2,1)S(1)} %dynamic-slice_bitcast_fusion.1), channel_id=1, source_target_pairs={{0,4},{4,0},{8,12},{12,8},{16,20},{20,16},{24,28},{28,24},{1,5},{5... | collective-permute-start | bytes 294920 | tf_op jit(solution)/shard_map/ppermute | solution.py:655
  10.9 30.6 %collective-permute-start.17 = (bf16[480,768]{1,0:T(8,128)(2,1)S(1)}, bf16[480,768]{1,0:T(8,128)(2,1)}, u32[]{:S(2)}, u32[]{:S(2)}) collective-permute-start(bf16[480,768]{1,0:T(8,128)(2,1)S(1)} %pad_maximum_fusion.1), channel_id=1, source_target_pairs={{0,2},{1,3},{2,0},{3,1},{4,6},{5,7},{6,4},{7,5},{8,10},{9,11},{10,... | collective-permute-start | bytes 2211848 | tf_op jit(solution)/shard_map/ppermute | solution.py:659
  12.9 7.7 %collective-permute-start.10 = (bf16[2,64,768]{2,1,0:T(8,128)(2,1)S(1)}, bf16[2,64,768]{2,1,0:T(8,128)(2,1)S(1)}, u32[]{:S(2)}, u32[]{:S(2)}) collective-permute-start(bf16[2,64,768]{2,1,0:T(8,128)(2,1)S(1)} %pad_maximum_fusion.5), channel_id=1, source_target_pairs={{0,8},{4,12},{8,0},{12,4},{16,24},{20,28},{24,16},{28,20},{1,9},{5... | collective-permute-start | bytes 589832 | tf_op jit(solution)/shard_map/ppermute | solution.py:655
  15.6 13.6 %copy-start.5 = (bf16[2,64,768]{2,1,0:T(8,128)(2,1)}, bf16[2,64,768]{2,1,0:T(8,128)(2,1)S(1)}, u32[]{:S(2)}) copy-start(bf16[2,64,768]{2,1,0:T(8,128)(2,1)S(1)} %pad_maximum_fusion.4.refs_2_) | copy-start | bytes 589828
  15.6 8.9 %collective-permute-start.4 = (bf16[2,64,768]{2,1,0:T(8,128)(2,1)S(1)}, bf16[2,64,768]{2,1,0:T(8,128)(2,1)S(1)}, u32[]{:S(2)}, u32[]{:S(2)}) collective-permute-start(bf16[2,64,768]{2,1,0:T(8,128)(2,1)S(1)} %pad_maximum_fusion.4.refs_2_), channel_id=1, source_target_pairs={{0,4},{4,0},{8,12},{12,8},{16,20},{20,16},{24,28},{28,24},{1,5},{5... | collective-permute-start | bytes 589832 | tf_op jit(solution)/shard_map/ppermute | solution.py:655
  17.2 9.3 %collective-permute-start.7 = (bf16[2,64,768]{2,1,0:T(8,128)(2,1)S(1)}, bf16[2,64,768]{2,1,0:T(8,128)(2,1)}, u32[]{:S(2)}, u32[]{:S(2)}) collective-permute-start(bf16[2,64,768]{2,1,0:T(8,128)(2,1)S(1)} %pad_maximum_fusion.4.refs_2_), channel_id=1, source_target_pairs={{0,1},{1,0},{2,3},{3,2},{4,5},{5,4},{6,7},{7,6},{8,9},{9,8},{10,11... | collective-permute-start | bytes 589832 | tf_op jit(solution)/shard_map/ppermute | solution.py:659
  17.2 9.3 %collective-permute-start.1 = (bf16[2,64,768]{2,1,0:T(8,128)(2,1)S(1)}, bf16[2,64,768]{2,1,0:T(8,128)(2,1)}, u32[]{:S(2)}, u32[]{:S(2)}) collective-permute-start(bf16[2,64,768]{2,1,0:T(8,128)(2,1)S(1)} %pad_maximum_fusion.3.refs_0_), channel_id=1, source_target_pairs={{0,4},{4,0},{8,12},{12,8},{16,20},{20,16},{24,28},{28,24},{1,5},{5... | collective-permute-start | bytes 589832 | tf_op jit(solution)/shard_map/ppermute | solution.py:655
  20.7 20.7 %collective-permute-start.11 = (bf16[4,64,768]{2,1,0:T(8,128)(2,1)S(1)}, bf16[4,64,768]{2,1,0:T(8,128)(2,1)S(1)}, u32[]{:S(2)}, u32[]{:S(2)}) collective-permute-start(bf16[4,64,768]{2,1,0:T(8,128)(2,1)S(1)} %pad_maximum_fusion.2), channel_id=1, source_target_pairs={{0,16},{4,20},{8,24},{12,28},{16,0},{20,4},{24,8},{28,12},{1,17},{... | collective-permute-start | bytes 1179656 | tf_op jit(solution)/shard_map/ppermute | solution.py:655
  24.5 3.0 %collective-permute-start.5 = (bf16[2,64,768]{2,1,0:T(8,128)(2,1)S(1)}, bf16[2,64,768]{2,1,0:T(8,128)(2,1)S(1)}, u32[]{:S(2)}, u32[]{:S(2)}) collective-permute-start(bf16[2,64,768]{2,1,0:T(8,128)(2,1)S(1)} %pad_maximum_fusion.3.refs_0_), channel_id=1, source_target_pairs={{0,1},{1,0},{2,3},{3,2},{4,5},{5,4},{6,7},{7,6},{8,9},{9,8},{10,11... | collective-permute-start | bytes 589832 | tf_op jit(solution)/shard_map/ppermute | solution.py:659
  26.5 2.6 %collective-permute-start.8 = (bf16[2,64,768]{2,1,0:T(8,128)(2,1)S(1)}, bf16[2,64,768]{2,1,0:T(8,128)(2,1)S(1)}, u32[]{:S(2)}, u32[]{:S(2)}) collective-permute-start(bf16[2,64,768]{2,1,0:T(8,128)(2,1)S(1)} %collective-permute-done.4.refs_3_), channel_id=1, source_target_pairs={{0,1},{1,0},{2,3},{3,2},{4,5},{5,4},{6,7},{7,6},{8,9},{9,8},{10,11... | collective-permute-start | bytes 589832 | tf_op jit(solution)/shard_map/ppermute | solution.py:659
  26.5 2.6 %collective-permute-start.6 = (bf16[2,64,768]{2,1,0:T(8,128)(2,1)}, bf16[2,64,768]{2,1,0:T(8,128)(2,1)S(1)}, u32[]{:S(2)}, u32[]{:S(2)}) collective-permute-start(bf16[2,64,768]{2,1,0:T(8,128)(2,1)} %collective-permute-done.1.refs_1_), channel_id=1, source_target_pairs={{0,1},{1,0},{2,3},{3,2},{4,5},{5,4},{6,7},{7,6},{8,9},{9,8},{10,11... | collective-permute-start | bytes 589832 | tf_op jit(solution)/shard_map/ppermute | solution.py:659
  27.6 14.6 %collective-permute-start.19 = (bf16[288,768]{1,0:T(8,128)(2,1)S(1)}, bf16[288,768]{1,0:T(8,128)(2,1)S(1)}, u32[]{:S(2)}, u32[]{:S(2)}) collective-permute-start(bf16[288,768]{1,0:T(8,128)(2,1)S(1)} %dynamic-slice_bitcast_fusion), channel_id=1, source_target_pairs={{0,2},{1,3},{2,0},{3,1},{4,6},{5,7},{6,4},{7,5},{8,10},{9,11},{10,... | collective-permute-start | bytes 1327112 | tf_op jit(solution)/shard_map/ppermute | solution.py:659
  41.5 13.2 %collective-permute-start.12 = (bf16[8,64,768]{2,1,0:T(8,128)(2,1)S(1)}, bf16[8,64,768]{2,1,0:T(8,128)(2,1)S(1)}, u32[]{:S(2)}, u32[]{:S(2)}) collective-permute-start(bf16[8,64,768]{2,1,0:T(8,128)(2,1)S(1)} %pad_maximum_fusion.refs_1_), channel_id=1, source_target_pairs={{0,1},{1,0},{2,3},{3,2},{4,5},{5,4},{6,7},{7,6},{8,9},{9,8},{10,11... | collective-permute-start | bytes 2359304 | tf_op jit(solution)/shard_map/ppermute | solution.py:659
  41.6 13.1 %collective-permute-start.18 = (bf16[480,768]{1,0:T(8,128)(2,1)}, bf16[480,768]{1,0:T(8,128)(2,1)S(1)}, u32[]{:S(2)}, u32[]{:S(2)}) collective-permute-start(bf16[480,768]{1,0:T(8,128)(2,1)} %collective-permute-done.17.refs_14_), channel_id=1, source_target_pairs={{0,1},{1,0},{2,3},{3,2},{4,5},{5,4},{6,7},{7,6},{8,9},{9,8},{10,11... | collective-permute-start | bytes 2211848 | tf_op jit(solution)/shard_map/ppermute | solution.py:659
  42.0 8.8 %collective-permute-start.16 = (bf16[192,768]{1,0:T(8,128)(2,1)S(1)}, bf16[192,768]{1,0:T(8,128)(2,1)S(1)}, u32[]{:S(2)}, u32[]{:S(2)}) collective-permute-start(bf16[192,768]{1,0:T(8,128)(2,1)S(1)} %copy-done.3), channel_id=1, source_target_pairs={{0,1},{1,0},{2,3},{3,2},{4,5},{5,4},{6,7},{7,6},{8,9},{9,8},{10,11... | collective-permute-start | bytes 884744 | tf_op jit(solution)/shard_map/ppermute | solution.py:659
  42.1 12.5 %collective-permute-start.20 = (bf16[288,768]{1,0:T(8,128)(2,1)S(1)}, bf16[288,768]{1,0:T(8,128)(2,1)S(1)}, u32[]{:S(2)}, u32[]{:S(2)}) collective-permute-start(bf16[288,768]{1,0:T(8,128)(2,1)S(1)} %collective-permute-done.19.refs_11_), channel_id=1, source_target_pairs={{0,4},{4,0},{8,12},{12,8},{16,20},{20,16},{24,28},{28,24},{1,5},{5... | collective-permute-start | bytes 1327112 | tf_op jit(solution)/shard_map/ppermute | solution.py:655
  43.9 7.0 %collective-permute-start.14 = (bf16[192,512]{1,0:T(8,128)(2,1)S(1)}, bf16[192,512]{1,0:T(8,128)(2,1)S(1)}, u32[]{:S(2)}, u32[]{:S(2)}) collective-permute-start(bf16[192,512]{1,0:T(8,128)(2,1)S(1)} %get-tuple-element.61.refs_3_.att_a), channel_id=1, source_target_pairs={{0,2},{1,3},{2,0},{3,1},{4,6},{5,7},{6,4},{7,5},{8,10},{9,11},{10,... | collective-permute-start | bytes 589832 | tf_op jit(solution)/shard_map/ppermute | solution.py:659
  50.8 1.4 %collective-permute-start.13 = (bf16[192,512]{1,0:T(8,128)(2,1)S(1)}, bf16[192,512]{1,0:T(8,128)(2,1)S(1)}, u32[]{:S(2)}, u32[]{:S(2)}) collective-permute-start(bf16[192,512]{1,0:T(8,128)(2,1)S(1)} %get-tuple-element.61.refs_3_.att_a), channel_id=1, source_target_pairs={{0,1},{1,0},{2,3},{3,2},{4,5},{5,4},{6,7},{7,6},{8,9},{9,8},{10,11... | collective-permute-start | bytes 589832 | tf_op jit(solution)/shard_map/ppermute | solution.py:659
  50.9 2.9 %collective-permute-start.15 = (bf16[192,512]{1,0:T(8,128)(2,1)S(1)}, bf16[192,512]{1,0:T(8,128)(2,1)S(1)}, u32[]{:S(2)}, u32[]{:S(2)}) collective-permute-start(bf16[192,512]{1,0:T(8,128)(2,1)S(1)} %collective-permute-done.14.refs_5_), channel_id=1, source_target_pairs={{0,1},{1,0},{2,3},{3,2},{4,5},{5,4},{6,7},{7,6},{8,9},{9,8},{10,11... | collective-permute-start | bytes 589832 | tf_op jit(solution)/shard_map/ppermute | solution.py:659
  52.3 12.1 %collective-permute-start.22 = (bf16[192,512]{1,0:T(8,128)(2,1)S(1)}, bf16[192,512]{1,0:T(8,128)(2,1)S(1)}, u32[]{:S(2)}, u32[]{:S(2)}) collective-permute-start(bf16[192,512]{1,0:T(8,128)(2,1)S(1)} %get-tuple-element.101.refs_1_.att_b), channel_id=1, source_target_pairs={{0,2},{1,3},{2,0},{3,1},{4,6},{5,7},{6,4},{7,5},{8,10},{9,11},{10,... | collective-permute-start | bytes 589832 | tf_op jit(solution)/shard_map/ppermute | solution.py:659
  53.8 11.2 %collective-permute-start.21 = (bf16[192,512]{1,0:T(8,128)(2,1)S(1)}, bf16[192,512]{1,0:T(8,128)(2,1)S(1)}, u32[]{:S(2)}, u32[]{:S(2)}) collective-permute-start(bf16[192,512]{1,0:T(8,128)(2,1)S(1)} %get-tuple-element.101.refs_1_.att_b), channel_id=1, source_target_pairs={{0,1},{1,0},{2,3},{3,2},{4,5},{5,4},{6,7},{7,6},{8,9},{9,8},{10,11... | collective-permute-start | bytes 589832 | tf_op jit(solution)/shard_map/ppermute | solution.py:659
  64.4 1.5 %collective-permute-start.23 = (bf16[192,512]{1,0:T(8,128)(2,1)S(1)}, bf16[192,512]{1,0:T(8,128)(2,1)S(1)}, u32[]{:S(2)}, u32[]{:S(2)}) collective-permute-start(bf16[192,512]{1,0:T(8,128)(2,1)S(1)} %collective-permute-done.22.refs_3_), channel_id=1, source_target_pairs={{0,1},{1,0},{2,3},{3,2},{4,5},{5,4},{6,7},{7,6},{8,9},{9,8},{10,11... | collective-permute-start | bytes 589832 | tf_op jit(solution)/shard_map/ppermute | solution.py:659
  64.5 12.5 %collective-permute-start.25 = (bf16[512,768]{1,0:T(8,128)(2,1)S(1)}, bf16[512,768]{1,0:T(8,128)(2,1)S(1)}, u32[]{:S(2)}, u32[]{:S(2)}) collective-permute-start(bf16[512,768]{1,0:T(8,128)(2,1)S(1)} %get-tuple-element.83.refs_6_), channel_id=1, source_target_pairs={{0,1},{1,0},{2,3},{3,2},{4,5},{5,4},{6,7},{7,6},{8,9},{9,8},{10,11... | collective-permute-start | bytes 2359304 | tf_op jit(solution)/shard_map/ppermute | solution.py:659
  74.2 2.7 %collective-permute-start.26 = (bf16[512,768]{1,0:T(8,128)(2,1)S(1)}, bf16[512,768]{1,0:T(8,128)(2,1)S(1)}, u32[]{:S(2)}, u32[]{:S(2)}) collective-permute-start(bf16[512,768]{1,0:T(8,128)(2,1)S(1)} %get-tuple-element.84.refs_7_), channel_id=1, source_target_pairs={{0,1},{1,0},{2,3},{3,2},{4,5},{5,4},{6,7},{7,6},{8,9},{9,8},{10,11... | collective-permute-start | bytes 2359304 | tf_op jit(solution)/shard_map/ppermute | solution.py:659
  92.3 1.5 %collective-permute-start.27 = (bf16[144,768]{1,0:T(8,128)(2,1)S(1)}, bf16[144,768]{1,0:T(8,128)(2,1)S(1)}, u32[]{:S(2)}, u32[]{:S(2)}) collective-permute-start(bf16[144,768]{1,0:T(8,128)(2,1)S(1)} %get-tuple-element.100.message), channel_id=1, source_target_pairs={{0,1},{1,0},{2,3},{3,2},{4,5},{5,4},{6,7},{7,6},{8,9},{9,8},{10,11... | collective-permute-start | bytes 663560 | tf_op jit(solution)/shard_map/ppermute | solution.py:659
  92.7 3.4 %collective-permute-start.24 = (bf16[128,768]{1,0:T(8,128)(2,1)}, bf16[128,768]{1,0:T(8,128)(2,1)}, u32[]{:S(2)}, u32[]{:S(2)}) collective-permute-start(bf16[128,768]{1,0:T(8,128)(2,1)} %get-tuple-element.76.part), channel_id=1, source_target_pairs={{0,1},{1,0},{2,3},{3,2},{4,5},{5,4},{6,7},{7,6},{8,9},{9,8},{10,11... | collective-permute-start | bytes 589832 | tf_op jit(solution)/shard_map/ppermute | solution.py:659
  93.9 7.8 %collective-permute-start.28 = (bf16[144,768]{1,0:T(8,128)(2,1)S(1)}, bf16[144,768]{1,0:T(8,128)(2,1)S(1)}, u32[]{:S(2)}, u32[]{:S(2)}) collective-permute-start(bf16[144,768]{1,0:T(8,128)(2,1)S(1)} %shard_map.149.mine), channel_id=1, source_target_pairs={{0,2},{1,3},{2,0},{3,1},{4,6},{5,7},{6,4},{7,5},{8,10},{9,11},{10,... | collective-permute-start | bytes 663560 | tf_op jit(solution)/shard_map/ppermute | solution.py:659
  (23 other events, 113.1 us)

commit v5 on v4

--- a/solution.py
+++ b/solution.py
@@ -255,8 +255,12 @@
 
 
 class Away:
-    def __init__(self, value):
-        self.value = value
+    def __init__(self, value, anywhere=False):
+        self.value, self.anywhere = value, anywhere
+
+
+def loose(value):
+    return Away(value, True)
 
 
 def call(kernel, outs, args, scratch=(), copies=0, flops=0, cells=0, room=16):
@@ -268,6 +272,8 @@
             values.append(value)
             continue
         space = pltpu.HBM if isinstance(arg, Away) else pltpu.VMEM
+        if isinstance(arg, Away) and arg.anywhere:
+            space = pl.ANY
         in_specs.append(pl.BlockSpec(memory_space=space))
         values.append(pltpu.with_memory_space_constraint(value, space))
     out_specs = [
@@ -740,7 +746,7 @@
             place,
             Away(tokens),
             *map(Away, near),
-            *map(Away, far),
+            *map(loose, far),
             first_gain[None, :],
             Away(qkv_t),
             cosine,
@@ -792,11 +798,17 @@
         ],
         [
             place,
-            *map(Away, [tok_all, cotangent, *cot_near, *cot_far]),
+            *map(Away, [tok_all, cotangent, *cot_near]),
+            *map(loose, cot_far),
             att_a,
-            *map(Away, atts_a[1:]),
-            *map(Away, [attn_weight, attn_core, rest_both]),
-            *map(Away, [in_t, in_side, in_rest, mlp_weight, rest_side]),
+            loose(atts_a[1]),
+            Away(atts_a[2]),
+            loose(atts_a[3]),
+            *map(Away, [attn_weight, attn_core]),
+            loose(rest_both),
+            *map(Away, [in_t, in_side]),
+            loose(in_rest),
+            *map(Away, [mlp_weight, rest_side]),
             second_row,
         ],
         scratch=[(wide, BF16), *room],
@@ -816,7 +828,7 @@
             tok_b,
             cot_all,
             att_b,
-            *map(Away, atts_b[1:]),
+            *map(loose, atts_b[1:]),
             second_row,
             attn_all,
             in_all,

time: 103 us -> 101 us (0.981)
  local copies, waits for them, and re-layouts: 4.56 us -> 2.99 us
    unnamed x52 -> x30, local copies, waits for them, and re-layouts: 2.65 us -> 0.08 us
  transfers between devices with their start and end apart: 29 -> 29, of which waited for: 10 -> 10; matrix products, arithmetic and copies ran while one was open for 3% -> 4% of each run, Pallas kernels for 34% -> 36%
where the time goes in v5:
time: 101 us
  Pallas kernels  52.3 us (52%)
  starting transfers between devices  28.2 us (28%)
  waiting for transfers between devices  14.1 us (14%)
  local copies, waits for them, and re-layouts  2.99 us (3%)
  other arithmetic  2.55 us (3%)
  between operations  1.04 us (1%)
    pallas_call x9, Pallas kernels, call(): pl.pallas_call(kernel, out_shape=[o.value if isinstance(o, Away) else o f...  52.3 us
    ppermute x9, starting transfers between devices, over_ctx(): lax.ppermute(value, 'ctx', [(spot, spot ^ step) for spot in range(spots)])  17.5 us
    ppermute x20, starting transfers between devices, swap(): return lax.ppermute(value, 'wt', [(spot, spot ^ mask) for spot in range(4)])  10.7 us
    ppermute x9, waiting for transfers between devices, over_ctx(): lax.ppermute(value, 'ctx', [(spot, spot ^ step) for spot in range(spots)])  7.65 us
    ppermute x20, waiting for transfers between devices, swap(): return lax.ppermute(value, 'wt', [(spot, spot ^ mask) for spot in range(4)])  6.42 us
  transfers between devices with their start and end apart: 29, of which 10 were waited for; matrix products, arithmetic and copies ran while one was open for 4% of the time, Pallas kernels for 36%

profile of v5, /device:TPU:0, one launch (start us, length us, event | category | flops | bytes accessed | tf_op | source)
XLA Modules:
  0.0 101.2 jit_solution(3330317418580064355)
XLA Ops:
  0.7 1.0 constant_dynamic-slice_fusion
  1.6 4.0 %collective-permute-start.2 = (bf16[64,768]{1,0:T(8,128)(2,1)S(1)}, bf16[64,768]{1,0:T(8,128)(2,1)S(1)}, u32[]{:S(2)}, u32[]{:S(2)}) collective-permute-start(bf16[64,768]{1,0:T(8,128)(2,1)S(1)} %constant_dynamic-slice_fusion), channel_id=1, source_target_pairs={{0,16},{4,20},{8,24},{12,28},{16,0},{20,4},{24,8},{28,12},{1,17},{... | collective-permute-start | bytes 294920 | tf_op jit(solution)/shard_map/ppermute | solution.py:661
  5.7 1.3 %collective-permute-start.3 = (bf16[64,768]{1,0:T(8,128)(2,1)S(1)}, bf16[64,768]{1,0:T(8,128)(2,1)S(1)}, u32[]{:S(2)}, u32[]{:S(2)}) collective-permute-start(bf16[64,768]{1,0:T(8,128)(2,1)S(1)} %constant_dynamic-slice_fusion), channel_id=1, source_target_pairs={{0,24},{4,28},{8,16},{12,20},{16,8},{20,12},{24,0},{28,4},{1,25},{... | collective-permute-start | bytes 294920 | tf_op jit(solution)/shard_map/ppermute | solution.py:661
  7.2 0.9 dynamic-slice_bitcast_fusion.1
  8.1 1.6 %collective-permute-start.9 = (bf16[1,64,768]{2,1,0:T(8,128)(2,1)S(1)}, bf16[1,64,768]{2,1,0:T(8,128)(2,1)S(1)}, u32[]{:S(2)}, u32[]{:S(2)}) collective-permute-start(bf16[1,64,768]{2,1,0:T(8,128)(2,1)S(1)} %dynamic-slice_bitcast_fusion.1), channel_id=1, source_target_pairs={{0,4},{4,0},{8,12},{12,8},{16,20},{20,16},{24,28},{28,24},{1,5},{5... | collective-permute-start | bytes 294920 | tf_op jit(solution)/shard_map/ppermute | solution.py:661
  9.7 1.2 %pad_maximum_fusion.1 = bf16[480,768]{1,0:T(8,128)(2,1)S(1)} fusion(bf16[192,768]{1,0:T(8,128)(2,1)} %refs_12_.1, bf16[288,768]{1,0:T(8,128)(2,1)} %refs_13_.1), kind=kLoop, calls=%fused_computation.1 | loop fusion | flops 1474560 | bytes 1474560 | tf_op jit(solution)/shard_map/concatenate | solution.py:729
  10.9 1.6 %collective-permute-start.17 = (bf16[480,768]{1,0:T(8,128)(2,1)S(1)}, bf16[480,768]{1,0:T(8,128)(2,1)}, u32[]{:S(2)}, u32[]{:S(2)}) collective-permute-start(bf16[480,768]{1,0:T(8,128)(2,1)S(1)} %pad_maximum_fusion.1), channel_id=1, source_target_pairs={{0,2},{1,3},{2,0},{3,1},{4,6},{5,7},{6,4},{7,5},{8,10},{9,11},{10,... | collective-permute-start | bytes 2211848 | tf_op jit(solution)/shard_map/ppermute | solution.py:665
  12.9 2.7 %collective-permute-start.10 = (bf16[2,64,768]{2,1,0:T(8,128)(2,1)S(1)}, bf16[2,64,768]{2,1,0:T(8,128)(2,1)S(1)}, u32[]{:S(2)}, u32[]{:S(2)}) collective-permute-start(bf16[2,64,768]{2,1,0:T(8,128)(2,1)S(1)} %pad_maximum_fusion.5), channel_id=1, source_target_pairs={{0,8},{4,12},{8,0},{12,4},{16,24},{20,28},{24,16},{28,20},{1,9},{5... | collective-permute-start | bytes 589832 | tf_op jit(solution)/shard_map/ppermute | solution.py:661
  15.6 1.6 %collective-permute-start.4 = (bf16[2,64,768]{2,1,0:T(8,128)(2,1)S(1)}, bf16[2,64,768]{2,1,0:T(8,128)(2,1)S(1)}, u32[]{:S(2)}, u32[]{:S(2)}) collective-permute-start(bf16[2,64,768]{2,1,0:T(8,128)(2,1)S(1)} %pad_maximum_fusion.4.refs_2_), channel_id=1, source_target_pairs={{0,4},{4,0},{8,12},{12,8},{16,20},{20,16},{24,28},{28,24},{1,5},{5... | collective-permute-start | bytes 589832 | tf_op jit(solution)/shard_map/ppermute | solution.py:661
  17.8 2.8 %collective-permute-done.10 = bf16[2,64,768]{2,1,0:T(8,128)(2,1)S(1)} collective-permute-done((bf16[2,64,768]{2,1,0:T(8,128)(2,1)S(1)}, bf16[2,64,768]{2,1,0:T(8,128)(2,1)S(1)}, u32[]{:S(2)}, u32[]{:S(2)}) %collective-permute-start.10) | collective-permute-done | bytes 196640 | tf_op jit(solution)/shard_map/ppermute | solution.py:661
  20.7 3.7 %collective-permute-start.11 = (bf16[4,64,768]{2,1,0:T(8,128)(2,1)S(1)}, bf16[4,64,768]{2,1,0:T(8,128)(2,1)S(1)}, u32[]{:S(2)}, u32[]{:S(2)}) collective-permute-start(bf16[4,64,768]{2,1,0:T(8,128)(2,1)S(1)} %pad_maximum_fusion.2), channel_id=1, source_target_pairs={{0,16},{4,20},{8,24},{12,28},{16,0},{20,4},{24,8},{28,12},{1,17},{... | collective-permute-start | bytes 1179656 | tf_op jit(solution)/shard_map/ppermute | solution.py:661
  24.5 1.0 %dynamic-slice_bitcast_fusion = bf16[288,768]{1,0:T(8,128)(2,1)S(1)} fusion(bf16[768,2,288]{0,2,1:T(8,128)(2,1)} %param.13, s32[]{:T(128)S(6)} %select_n.27), kind=kLoop, calls=%fused_computation.2 | loop fusion | bytes 884740 | tf_op jit(solution)/shard_map/jit(dynamic_index_in_dim)/squeeze | solution.py:726
  27.5 1.6 %collective-permute-start.19 = (bf16[288,768]{1,0:T(8,128)(2,1)S(1)}, bf16[288,768]{1,0:T(8,128)(2,1)S(1)}, u32[]{:S(2)}, u32[]{:S(2)}) collective-permute-start(bf16[288,768]{1,0:T(8,128)(2,1)S(1)} %dynamic-slice_bitcast_fusion), channel_id=1, source_target_pairs={{0,2},{1,3},{2,0},{3,1},{4,6},{5,7},{6,4},{7,5},{8,10},{9,11},{10,... | collective-permute-start | bytes 1327112 | tf_op jit(solution)/shard_map/ppermute | solution.py:665
  29.1 9.4 %shard_map.143 = (bf16[1024,768]{1,0:T(8,128)(2,1)}, bf16[1024,768]{1,0:T(8,128)(2,1)S(1)}, bf16[576,1024]{1,0:T(8,128)(2,1)S(1)}, bf16[192,512]{1,0:T(8,128)(2,...) custom-call(s32[4]{0:T(128)S(1)} %pad_add_fusion.place, bf16[128,768]{1,0:T(8,128)(2,1)} %tokens.1, ...), custom_call_target="tpu_custom_call" | custom-call | tf_op jit(solution)/shard_map/pallas_call | solution.py:283
  38.5 2.8 %collective-permute-done.11 = bf16[4,64,768]{2,1,0:T(8,128)(2,1)S(1)} collective-permute-done((bf16[4,64,768]{2,1,0:T(8,128)(2,1)S(1)}, bf16[4,64,768]{2,1,0:T(8,128)(2,1)S(1)}, u32[]{:S(2)}, u32[]{:S(2)}) %collective-permute-start.11) | collective-permute-done | bytes 393248 | tf_op jit(solution)/shard_map/ppermute | solution.py:661
  42.1 1.7 %collective-permute-start.20 = (bf16[288,768]{1,0:T(8,128)(2,1)S(1)}, bf16[288,768]{1,0:T(8,128)(2,1)S(1)}, u32[]{:S(2)}, u32[]{:S(2)}) collective-permute-start(bf16[288,768]{1,0:T(8,128)(2,1)S(1)} %collective-permute-done.19.refs_11_), channel_id=1, source_target_pairs={{0,4},{4,0},{8,12},{12,8},{16,20},{20,16},{24,28},{28,24},{1,5},{5... | collective-permute-start | bytes 1327112 | tf_op jit(solution)/shard_map/ppermute | solution.py:661
  43.9 1.5 %collective-permute-start.14 = (bf16[192,512]{1,0:T(8,128)(2,1)S(1)}, bf16[192,512]{1,0:T(8,128)(2,1)S(1)}, u32[]{:S(2)}, u32[]{:S(2)}) collective-permute-start(bf16[192,512]{1,0:T(8,128)(2,1)S(1)} %get-tuple-element.61.refs_3_.att_a), channel_id=1, source_target_pairs={{0,2},{1,3},{2,0},{3,1},{4,6},{5,7},{6,4},{7,5},{8,10},{9,11},{10,... | collective-permute-start | bytes 589832 | tf_op jit(solution)/shard_map/ppermute | solution.py:665
  45.4 4.4 %shard_map.144 = (bf16[192,512]{1,0:T(8,128)(2,1)S(1)}, f32[192,512]{1,0:T(8,128)S(1)}, f32[8,512]{1,0:T(8,128)S(1)}) custom-call(bf16[576,1024]{1,0:T(8,128)(2,1)S(1)} %get-tuple-element.65.qkv.refs_13_), custom_call_target="tpu_custom_call" | custom-call | tf_op jit(solution)/shard_map/pallas_call | solution.py:283
  49.7 1.1 %collective-permute-done.14.refs_5_ = bf16[192,512]{1,0:T(8,128)(2,1)S(1)} collective-permute-done((bf16[192,512]{1,0:T(8,128)(2,1)S(1)}, bf16[192,512]{1,0:T(8,128)(2,1)S(1)}, u32[]{:S(2)}, u32[]{:S(2)}) %collective-permute-start.14) | collective-permute-done | bytes 196640 | tf_op jit(solution)/shard_map/ppermute | solution.py:665
  51.4 0.9 collective-permute-done.13.refs_4_
  52.3 1.5 %collective-permute-start.22 = (bf16[192,512]{1,0:T(8,128)(2,1)S(1)}, bf16[192,512]{1,0:T(8,128)(2,1)S(1)}, u32[]{:S(2)}, u32[]{:S(2)}) collective-permute-start(bf16[192,512]{1,0:T(8,128)(2,1)S(1)} %get-tuple-element.101.refs_1_.att_b), channel_id=1, source_target_pairs={{0,2},{1,3},{2,0},{3,1},{4,6},{5,7},{6,4},{7,5},{8,10},{9,11},{10,... | collective-permute-start | bytes 589832 | tf_op jit(solution)/shard_map/ppermute | solution.py:665
  53.8 0.9 collective-permute-done.20.refs_12_
  54.7 9.0 %shard_map.145 = (bf16[1024,768]{1,0:T(8,128)(2,1)S(1)}, bf16[768,768]{1,0:T(8,128)(2,1)S(1)}, bf16[1152,768]{1,0:T(8,128)(2,1)S(1)}, bf16[576,768]{1,0:T(8,128)...) custom-call(s32[4]{0:T(128)S(1)} %pad_add_fusion.place, ...), custom_call_target="tpu_custom_call" | custom-call | flops 2868903936 | bytes 8408080 | tf_op jit(solution)/shard_map/pallas_call | solution.py:283
  64.3 0.9 collective-permute-done.23.refs_4_
  65.3 7.4 %shard_map.146 = (f32[512,768]{1,0:T(8,128)S(1)}, bf16[512,768]{1,0:T(8,128)(2,1)S(1)}, bf16[288,512]{1,0:T(8,128)(2,1)S(1)}, bf16[576,512]{1,0:T(8,128)(2,1)S(1...) custom-call(s32[4]{0:T(128)S(1)} %pad_add_fusion.place, ...), custom_call_target="tpu_custom_call" | custom-call | flops 2868903936 | bytes 7572496 | tf_op jit(solution)/shard_map/pallas_call | solution.py:283
  72.9 2.5 %shard_map.147 = (f32[576,768]{1,0:T(8,128)}, f32[288,768]{1,0:T(8,128)}) custom-call(bf16[576,512]{1,0:T(8,128)(2,1)S(1)} %get-tuple-element.85.gate_a, bf16[576,512]{1,0:T(8,128)(2,1)S(1)} %get-tuple-element.86.gate_b, bf16[288,512]{1,0:T(8,128)(2,1)S(1)} %get-tuple-element.87.hidden_a, bf16[288,512]{1,0:T(8,128)(2,1)S(1)} %get-tuple-element.88.hidden_b, ...), custom_call_target="tpu_custom_call" | custom-call | flops 1358954496 | bytes 4915200 | tf_op jit(solution)/shard_map/pallas_call | solution.py:283
  75.4 15.3 %shard_map.148 = (f32[1,768]{1,0:T(1,128)S(1)}, bf16[1024,768]{1,0:T(8,128)(2,1)S(1)}, f32[128,768]{1,0:T(8,128)S(1)}, bf16[144,768]{1,0:T(8,128)(2,1)S(1)}, f32[576,768]{1,0:T(8,128)}) custom-call(s32[4]{0:T(128)S(1)} %pad_add_fusion.place, f32[512,768]{1,0:T(8,128)S(1)} %get-tuple-element.77.refs_0_, f32[512,768]{1,0:T(8,128)S(1)} %get-tuple-element.78.refs_1_, ...), custom_call_target="tpu_custom_call" | custom-call | flops 9261023232 | bytes 12892176 | tf_op jit(solution)/shard_map/pallas_call | solution.py:283
  91.3 1.0 collective-permute-done.27.far
  92.4 1.6 %collective-permute-start.28 = (bf16[144,768]{1,0:T(8,128)(2,1)S(1)}, bf16[144,768]{1,0:T(8,128)(2,1)S(1)}, u32[]{:S(2)}, u32[]{:S(2)}) collective-permute-start(bf16[144,768]{1,0:T(8,128)(2,1)S(1)} %shard_map.149.mine), channel_id=1, source_target_pairs={{0,2},{1,3},{2,0},{3,1},{4,6},{5,7},{6,4},{7,5},{8,10},{9,11},{10,... | collective-permute-start | bytes 663560 | tf_op jit(solution)/shard_map/ppermute | solution.py:665
  94.6 3.1 %shard_map.150 = (f32[192,768]{1,0:T(8,128)}, bf16[128,768]{1,0:T(8,128)(2,1)}) custom-call(bf16[192,512]{1,0:T(8,128)(2,1)S(1)} %get-tuple-element.61.refs_3_.att_a, bf16[192,512]{1,0:T(8,128)(2,1)S(1)} %get-tuple-element.101.refs_1_.att_b, bf16[1024,768]{1,0:T(8,128)(2,1)S(1)} %get-tuple-element.102.branch, f32[128,768]{1,0:T(8,128)S(1)} %get-tuple-element.103.middle, ...), custom_call_target="tpu_custom_call" | custom-call | flops 301989888 | bytes 2752512 | tf_op jit(solution)/shard_map/pallas_call | solution.py:283
  97.7 2.5 %collective-permute-done.28.far = bf16[144,768]{1,0:T(8,128)(2,1)S(1)} collective-permute-done((bf16[144,768]{1,0:T(8,128)(2,1)S(1)}, bf16[144,768]{1,0:T(8,128)(2,1)S(1)}, u32[]{:S(2)}, u32[]{:S(2)}) %collective-permute-start.28) | collective-permute-done | bytes 221216 | tf_op jit(solution)/shard_map/ppermute | solution.py:665
  100.1 1.0 %shard_map.151 = (bf16[128,768]{1,0:T(8,128)(2,1)}, f32[768]{0:T(1024)}) custom-call(bf16[144,768]{1,0:T(8,128)(2,1)S(1)} %shard_map.149.mine, bf16[144,768]{1,0:T(8,128)(2,1)S(1)} %collective-permute-done.28.far, bf16[128,768]{1,0:T(8,128)(2,1)S(1)} %copy-done.1, f32[1,768]{1,0:T(1,128)S(1)} %broadcast_in_dim.6.refs_8_.refs_22_.gain, ...), custom_call_target="tpu_custom_call" | custom-call | flops 1572864 | bytes 1035264 | tf_op jit(solution)/shard_map/pallas_call | solution.py:283
  (82 shorter events, 6.6 us)
Async XLA Ops:
  1.6 13.9 %collective-permute-start.2 = (bf16[64,768]{1,0:T(8,128)(2,1)S(1)}, bf16[64,768]{1,0:T(8,128)(2,1)S(1)}, u32[]{:S(2)}, u32[]{:S(2)}) collective-permute-start(bf16[64,768]{1,0:T(8,128)(2,1)S(1)} %constant_dynamic-slice_fusion), channel_id=1, source_target_pairs={{0,16},{4,20},{8,24},{12,28},{16,0},{20,4},{24,8},{28,12},{1,17},{... | collective-permute-start | bytes 294920 | tf_op jit(solution)/shard_map/ppermute | solution.py:661
  5.7 7.2 %collective-permute-start.3 = (bf16[64,768]{1,0:T(8,128)(2,1)S(1)}, bf16[64,768]{1,0:T(8,128)(2,1)S(1)}, u32[]{:S(2)}, u32[]{:S(2)}) collective-permute-start(bf16[64,768]{1,0:T(8,128)(2,1)S(1)} %constant_dynamic-slice_fusion), channel_id=1, source_target_pairs={{0,24},{4,28},{8,16},{12,20},{16,8},{20,12},{24,0},{28,4},{1,25},{... | collective-permute-start | bytes 294920 | tf_op jit(solution)/shard_map/ppermute | solution.py:661
  7.0 10.2 %collective-permute-start = (bf16[64,768]{1,0:T(8,128)(2,1)S(1)}, bf16[64,768]{1,0:T(8,128)(2,1)S(1)}, u32[]{:S(2)}, u32[]{:S(2)}) collective-permute-start(bf16[64,768]{1,0:T(8,128)(2,1)S(1)} %constant_dynamic-slice_fusion), channel_id=1, source_target_pairs={{0,8},{4,12},{8,0},{12,4},{16,24},{20,28},{24,16},{28,20},{1,9},{5... | collective-permute-start | bytes 294920 | tf_op jit(solution)/shard_map/ppermute | solution.py:661
  8.1 16.3 %copy-start.10 = (f32[768]{0:T(1024)S(1)}, f32[768]{0:T(1024)}, u32[]{:S(2)}) copy-start(f32[768]{0:T(1024)} %param.9) | copy-start | bytes 9220
  8.1 4.7 %collective-permute-start.9 = (bf16[1,64,768]{2,1,0:T(8,128)(2,1)S(1)}, bf16[1,64,768]{2,1,0:T(8,128)(2,1)S(1)}, u32[]{:S(2)}, u32[]{:S(2)}) collective-permute-start(bf16[1,64,768]{2,1,0:T(8,128)(2,1)S(1)} %dynamic-slice_bitcast_fusion.1), channel_id=1, source_target_pairs={{0,4},{4,0},{8,12},{12,8},{16,20},{20,16},{24,28},{28,24},{1,5},{5... | collective-permute-start | bytes 294920 | tf_op jit(solution)/shard_map/ppermute | solution.py:661
  10.9 30.7 %collective-permute-start.17 = (bf16[480,768]{1,0:T(8,128)(2,1)S(1)}, bf16[480,768]{1,0:T(8,128)(2,1)}, u32[]{:S(2)}, u32[]{:S(2)}) collective-permute-start(bf16[480,768]{1,0:T(8,128)(2,1)S(1)} %pad_maximum_fusion.1), channel_id=1, source_target_pairs={{0,2},{1,3},{2,0},{3,1},{4,6},{5,7},{6,4},{7,5},{8,10},{9,11},{10,... | collective-permute-start | bytes 2211848 | tf_op jit(solution)/shard_map/ppermute | solution.py:665
  12.9 7.8 %collective-permute-start.10 = (bf16[2,64,768]{2,1,0:T(8,128)(2,1)S(1)}, bf16[2,64,768]{2,1,0:T(8,128)(2,1)S(1)}, u32[]{:S(2)}, u32[]{:S(2)}) collective-permute-start(bf16[2,64,768]{2,1,0:T(8,128)(2,1)S(1)} %pad_maximum_fusion.5), channel_id=1, source_target_pairs={{0,8},{4,12},{8,0},{12,4},{16,24},{20,28},{24,16},{28,20},{1,9},{5... | collective-permute-start | bytes 589832 | tf_op jit(solution)/shard_map/ppermute | solution.py:661
  15.6 13.5 %copy-start.5 = (bf16[2,64,768]{2,1,0:T(8,128)(2,1)}, bf16[2,64,768]{2,1,0:T(8,128)(2,1)S(1)}, u32[]{:S(2)}) copy-start(bf16[2,64,768]{2,1,0:T(8,128)(2,1)S(1)} %pad_maximum_fusion.4.refs_2_) | copy-start | bytes 589828
  15.6 9.9 %collective-permute-start.4 = (bf16[2,64,768]{2,1,0:T(8,128)(2,1)S(1)}, bf16[2,64,768]{2,1,0:T(8,128)(2,1)S(1)}, u32[]{:S(2)}, u32[]{:S(2)}) collective-permute-start(bf16[2,64,768]{2,1,0:T(8,128)(2,1)S(1)} %pad_maximum_fusion.4.refs_2_), channel_id=1, source_target_pairs={{0,4},{4,0},{8,12},{12,8},{16,20},{20,16},{24,28},{28,24},{1,5},{5... | collective-permute-start | bytes 589832 | tf_op jit(solution)/shard_map/ppermute | solution.py:661
  17.2 9.2 %collective-permute-start.7 = (bf16[2,64,768]{2,1,0:T(8,128)(2,1)S(1)}, bf16[2,64,768]{2,1,0:T(8,128)(2,1)S(1)}, u32[]{:S(2)}, u32[]{:S(2)}) collective-permute-start(bf16[2,64,768]{2,1,0:T(8,128)(2,1)S(1)} %pad_maximum_fusion.4.refs_2_), channel_id=1, source_target_pairs={{0,1},{1,0},{2,3},{3,2},{4,5},{5,4},{6,7},{7,6},{8,9},{9,8},{10,11... | collective-permute-start | bytes 589832 | tf_op jit(solution)/shard_map/ppermute | solution.py:665
  17.2 9.2 %collective-permute-start.1 = (bf16[2,64,768]{2,1,0:T(8,128)(2,1)S(1)}, bf16[2,64,768]{2,1,0:T(8,128)(2,1)S(1)}, u32[]{:S(2)}, u32[]{:S(2)}) collective-permute-start(bf16[2,64,768]{2,1,0:T(8,128)(2,1)S(1)} %pad_maximum_fusion.3.refs_0_), channel_id=1, source_target_pairs={{0,4},{4,0},{8,12},{12,8},{16,20},{20,16},{24,28},{28,24},{1,5},{5... | collective-permute-start | bytes 589832 | tf_op jit(solution)/shard_map/ppermute | solution.py:661
  20.7 20.7 %collective-permute-start.11 = (bf16[4,64,768]{2,1,0:T(8,128)(2,1)S(1)}, bf16[4,64,768]{2,1,0:T(8,128)(2,1)S(1)}, u32[]{:S(2)}, u32[]{:S(2)}) collective-permute-start(bf16[4,64,768]{2,1,0:T(8,128)(2,1)S(1)} %pad_maximum_fusion.2), channel_id=1, source_target_pairs={{0,16},{4,20},{8,24},{12,28},{16,0},{20,4},{24,8},{28,12},{1,17},{... | collective-permute-start | bytes 1179656 | tf_op jit(solution)/shard_map/ppermute | solution.py:661
  25.5 1.9 %collective-permute-start.5 = (bf16[2,64,768]{2,1,0:T(8,128)(2,1)S(1)}, bf16[2,64,768]{2,1,0:T(8,128)(2,1)S(1)}, u32[]{:S(2)}, u32[]{:S(2)}) collective-permute-start(bf16[2,64,768]{2,1,0:T(8,128)(2,1)S(1)} %pad_maximum_fusion.3.refs_0_), channel_id=1, source_target_pairs={{0,1},{1,0},{2,3},{3,2},{4,5},{5,4},{6,7},{7,6},{8,9},{9,8},{10,11... | collective-permute-start | bytes 589832 | tf_op jit(solution)/shard_map/ppermute | solution.py:665
  26.4 2.6 %collective-permute-start.8 = (bf16[2,64,768]{2,1,0:T(8,128)(2,1)S(1)}, bf16[2,64,768]{2,1,0:T(8,128)(2,1)S(1)}, u32[]{:S(2)}, u32[]{:S(2)}) collective-permute-start(bf16[2,64,768]{2,1,0:T(8,128)(2,1)S(1)} %collective-permute-done.4.refs_3_), channel_id=1, source_target_pairs={{0,1},{1,0},{2,3},{3,2},{4,5},{5,4},{6,7},{7,6},{8,9},{9,8},{10,11... | collective-permute-start | bytes 589832 | tf_op jit(solution)/shard_map/ppermute | solution.py:665
  26.4 2.6 %collective-permute-start.6 = (bf16[2,64,768]{2,1,0:T(8,128)(2,1)S(1)}, bf16[2,64,768]{2,1,0:T(8,128)(2,1)S(1)}, u32[]{:S(2)}, u32[]{:S(2)}) collective-permute-start(bf16[2,64,768]{2,1,0:T(8,128)(2,1)S(1)} %collective-permute-done.1.refs_1_), channel_id=1, source_target_pairs={{0,1},{1,0},{2,3},{3,2},{4,5},{5,4},{6,7},{7,6},{8,9},{9,8},{10,11... | collective-permute-start | bytes 589832 | tf_op jit(solution)/shard_map/ppermute | solution.py:665
  27.5 14.7 %collective-permute-start.19 = (bf16[288,768]{1,0:T(8,128)(2,1)S(1)}, bf16[288,768]{1,0:T(8,128)(2,1)S(1)}, u32[]{:S(2)}, u32[]{:S(2)}) collective-permute-start(bf16[288,768]{1,0:T(8,128)(2,1)S(1)} %dynamic-slice_bitcast_fusion), channel_id=1, source_target_pairs={{0,2},{1,3},{2,0},{3,1},{4,6},{5,7},{6,4},{7,5},{8,10},{9,11},{10,... | collective-permute-start | bytes 1327112 | tf_op jit(solution)/shard_map/ppermute | solution.py:665
  41.4 13.2 %copy-start.7 = (bf16[8,64,768]{2,1,0:T(8,128)(2,1)}, bf16[8,64,768]{2,1,0:T(8,128)(2,1)S(1)}, u32[]{:S(2)}) copy-start(bf16[8,64,768]{2,1,0:T(8,128)(2,1)S(1)} %pad_maximum_fusion.refs_1_) | copy-start | bytes 2359300
  41.5 13.2 %collective-permute-start.12 = (bf16[8,64,768]{2,1,0:T(8,128)(2,1)S(1)}, bf16[8,64,768]{2,1,0:T(8,128)(2,1)S(1)}, u32[]{:S(2)}, u32[]{:S(2)}) collective-permute-start(bf16[8,64,768]{2,1,0:T(8,128)(2,1)S(1)} %pad_maximum_fusion.refs_1_), channel_id=1, source_target_pairs={{0,1},{1,0},{2,3},{3,2},{4,5},{5,4},{6,7},{7,6},{8,9},{9,8},{10,11... | collective-permute-start | bytes 2359304 | tf_op jit(solution)/shard_map/ppermute | solution.py:665
  41.6 13.1 %collective-permute-start.18 = (bf16[480,768]{1,0:T(8,128)(2,1)}, bf16[480,768]{1,0:T(8,128)(2,1)S(1)}, u32[]{:S(2)}, u32[]{:S(2)}) collective-permute-start(bf16[480,768]{1,0:T(8,128)(2,1)} %collective-permute-done.17.refs_14_), channel_id=1, source_target_pairs={{0,1},{1,0},{2,3},{3,2},{4,5},{5,4},{6,7},{7,6},{8,9},{9,8},{10,11... | collective-permute-start | bytes 2211848 | tf_op jit(solution)/shard_map/ppermute | solution.py:665
  42.0 8.8 %collective-permute-start.16 = (bf16[192,768]{1,0:T(8,128)(2,1)S(1)}, bf16[192,768]{1,0:T(8,128)(2,1)S(1)}, u32[]{:S(2)}, u32[]{:S(2)}) collective-permute-start(bf16[192,768]{1,0:T(8,128)(2,1)S(1)} %copy-done.3), channel_id=1, source_target_pairs={{0,1},{1,0},{2,3},{3,2},{4,5},{5,4},{6,7},{7,6},{8,9},{9,8},{10,11... | collective-permute-start | bytes 884744 | tf_op jit(solution)/shard_map/ppermute | solution.py:665
  42.1 12.5 %collective-permute-start.20 = (bf16[288,768]{1,0:T(8,128)(2,1)S(1)}, bf16[288,768]{1,0:T(8,128)(2,1)S(1)}, u32[]{:S(2)}, u32[]{:S(2)}) collective-permute-start(bf16[288,768]{1,0:T(8,128)(2,1)S(1)} %collective-permute-done.19.refs_11_), channel_id=1, source_target_pairs={{0,4},{4,0},{8,12},{12,8},{16,20},{20,16},{24,28},{28,24},{1,5},{5... | collective-permute-start | bytes 1327112 | tf_op jit(solution)/shard_map/ppermute | solution.py:661
  43.9 7.0 %collective-permute-start.14 = (bf16[192,512]{1,0:T(8,128)(2,1)S(1)}, bf16[192,512]{1,0:T(8,128)(2,1)S(1)}, u32[]{:S(2)}, u32[]{:S(2)}) collective-permute-start(bf16[192,512]{1,0:T(8,128)(2,1)S(1)} %get-tuple-element.61.refs_3_.att_a), channel_id=1, source_target_pairs={{0,2},{1,3},{2,0},{3,1},{4,6},{5,7},{6,4},{7,5},{8,10},{9,11},{10,... | collective-permute-start | bytes 589832 | tf_op jit(solution)/shard_map/ppermute | solution.py:665
  50.8 1.4 %collective-permute-start.13 = (bf16[192,512]{1,0:T(8,128)(2,1)S(1)}, bf16[192,512]{1,0:T(8,128)(2,1)S(1)}, u32[]{:S(2)}, u32[]{:S(2)}) collective-permute-start(bf16[192,512]{1,0:T(8,128)(2,1)S(1)} %get-tuple-element.61.refs_3_.att_a), channel_id=1, source_target_pairs={{0,1},{1,0},{2,3},{3,2},{4,5},{5,4},{6,7},{7,6},{8,9},{9,8},{10,11... | collective-permute-start | bytes 589832 | tf_op jit(solution)/shard_map/ppermute | solution.py:665
  50.9 2.9 %collective-permute-start.15 = (bf16[192,512]{1,0:T(8,128)(2,1)S(1)}, bf16[192,512]{1,0:T(8,128)(2,1)S(1)}, u32[]{:S(2)}, u32[]{:S(2)}) collective-permute-start(bf16[192,512]{1,0:T(8,128)(2,1)S(1)} %collective-permute-done.14.refs_5_), channel_id=1, source_target_pairs={{0,1},{1,0},{2,3},{3,2},{4,5},{5,4},{6,7},{7,6},{8,9},{9,8},{10,11... | collective-permute-start | bytes 589832 | tf_op jit(solution)/shard_map/ppermute | solution.py:665
  52.3 11.4 %collective-permute-start.22 = (bf16[192,512]{1,0:T(8,128)(2,1)S(1)}, bf16[192,512]{1,0:T(8,128)(2,1)S(1)}, u32[]{:S(2)}, u32[]{:S(2)}) collective-permute-start(bf16[192,512]{1,0:T(8,128)(2,1)S(1)} %get-tuple-element.101.refs_1_.att_b), channel_id=1, source_target_pairs={{0,2},{1,3},{2,0},{3,1},{4,6},{5,7},{6,4},{7,5},{8,10},{9,11},{10,... | collective-permute-start | bytes 589832 | tf_op jit(solution)/shard_map/ppermute | solution.py:665
  53.8 10.5 %collective-permute-start.21 = (bf16[192,512]{1,0:T(8,128)(2,1)S(1)}, bf16[192,512]{1,0:T(8,128)(2,1)S(1)}, u32[]{:S(2)}, u32[]{:S(2)}) collective-permute-start(bf16[192,512]{1,0:T(8,128)(2,1)S(1)} %get-tuple-element.101.refs_1_.att_b), channel_id=1, source_target_pairs={{0,1},{1,0},{2,3},{3,2},{4,5},{5,4},{6,7},{7,6},{8,9},{9,8},{10,11... | collective-permute-start | bytes 589832 | tf_op jit(solution)/shard_map/ppermute | solution.py:665
  63.7 1.5 %collective-permute-start.23 = (bf16[192,512]{1,0:T(8,128)(2,1)S(1)}, bf16[192,512]{1,0:T(8,128)(2,1)S(1)}, u32[]{:S(2)}, u32[]{:S(2)}) collective-permute-start(bf16[192,512]{1,0:T(8,128)(2,1)S(1)} %collective-permute-done.22.refs_3_), channel_id=1, source_target_pairs={{0,1},{1,0},{2,3},{3,2},{4,5},{5,4},{6,7},{7,6},{8,9},{9,8},{10,11... | collective-permute-start | bytes 589832 | tf_op jit(solution)/shard_map/ppermute | solution.py:665
  63.8 11.6 %collective-permute-start.25 = (bf16[512,768]{1,0:T(8,128)(2,1)S(1)}, bf16[512,768]{1,0:T(8,128)(2,1)S(1)}, u32[]{:S(2)}, u32[]{:S(2)}) collective-permute-start(bf16[512,768]{1,0:T(8,128)(2,1)S(1)} %get-tuple-element.83.refs_6_), channel_id=1, source_target_pairs={{0,1},{1,0},{2,3},{3,2},{4,5},{5,4},{6,7},{7,6},{8,9},{9,8},{10,11... | collective-permute-start | bytes 2359304 | tf_op jit(solution)/shard_map/ppermute | solution.py:665
  72.7 2.7 %collective-permute-start.26 = (bf16[512,768]{1,0:T(8,128)(2,1)S(1)}, bf16[512,768]{1,0:T(8,128)(2,1)S(1)}, u32[]{:S(2)}, u32[]{:S(2)}) collective-permute-start(bf16[512,768]{1,0:T(8,128)(2,1)S(1)} %get-tuple-element.84.refs_7_), channel_id=1, source_target_pairs={{0,1},{1,0},{2,3},{3,2},{4,5},{5,4},{6,7},{7,6},{8,9},{9,8},{10,11... | collective-permute-start | bytes 2359304 | tf_op jit(solution)/shard_map/ppermute | solution.py:665
  90.7 1.5 %collective-permute-start.27 = (bf16[144,768]{1,0:T(8,128)(2,1)S(1)}, bf16[144,768]{1,0:T(8,128)(2,1)S(1)}, u32[]{:S(2)}, u32[]{:S(2)}) collective-permute-start(bf16[144,768]{1,0:T(8,128)(2,1)S(1)} %get-tuple-element.100.message), channel_id=1, source_target_pairs={{0,1},{1,0},{2,3},{3,2},{4,5},{5,4},{6,7},{7,6},{8,9},{9,8},{10,11... | collective-permute-start | bytes 663560 | tf_op jit(solution)/shard_map/ppermute | solution.py:665
  91.2 3.4 %collective-permute-start.24 = (bf16[128,768]{1,0:T(8,128)(2,1)}, bf16[128,768]{1,0:T(8,128)(2,1)}, u32[]{:S(2)}, u32[]{:S(2)}) collective-permute-start(bf16[128,768]{1,0:T(8,128)(2,1)} %get-tuple-element.76.part), channel_id=1, source_target_pairs={{0,1},{1,0},{2,3},{3,2},{4,5},{5,4},{6,7},{7,6},{8,9},{9,8},{10,11... | collective-permute-start | bytes 589832 | tf_op jit(solution)/shard_map/ppermute | solution.py:665
  92.4 7.8 %collective-permute-start.28 = (bf16[144,768]{1,0:T(8,128)(2,1)S(1)}, bf16[144,768]{1,0:T(8,128)(2,1)S(1)}, u32[]{:S(2)}, u32[]{:S(2)}) collective-permute-start(bf16[144,768]{1,0:T(8,128)(2,1)S(1)} %shard_map.149.mine), channel_id=1, source_target_pairs={{0,2},{1,3},{2,0},{3,1},{4,6},{5,7},{6,4},{7,5},{8,10},{9,11},{10,... | collective-permute-start | bytes 663560 | tf_op jit(solution)/shard_map/ppermute | solution.py:665
  (12 other events, 89.8 us)

commit v6 on v5

--- a/solution.py
+++ b/solution.py
@@ -408,7 +408,7 @@
                 qkv[base : base + HEAD, at] = turned
         qkv[2 * local :, at] = raw[2 * local :].astype(BF16)
 
-    loop(tokens // chunk, one_chunk, 2)
+    loop(tokens // chunk, one_chunk, tokens // chunk)
     attend(heads, 0, qkv, att, exact, lse, keys)
     move.finish()
 
@@ -561,14 +561,14 @@
             own_v[...] = grad
 
     for turn in range(2):
-        loop(spots, functools.partial(norm_block, turn), 2)
+        loop(spots, functools.partial(norm_block, turn), spots)
     chunk = 256
 
     def grad_chunk(i):
         at = part_of(i, chunk)
         back_rows[:, at] = mm(attn[...], branch[at, :], NT).astype(BF16)
 
-    loop(tokens // chunk, grad_chunk, 2)
+    loop(tokens // chunk, grad_chunk, tokens // chunk)
     for turn in range(2):
         lse[:, turn * turns : (turn + 1) * turns] = lses[turn][...]
     scale = HEAD ** (-0.5)
@@ -686,14 +686,14 @@
 def gather_cotangent(block, core, spots, after, gate):
     near = half_of(block, core)[None]
     ids, step = (0,), 1
-    while step < spots:
+    while 2 * step < spots:
         if step == 2:
             near, _ = lax.optimization_barrier((near, after))
         near = jnp.concatenate([near, over_ctx(near, step, spots)], axis=0)
         ids += tuple(i + step for i in ids)
         step *= 2
-    near, _ = lax.optimization_barrier((near, gate))
-    return [near], [swap(near, 1)], (ids,)
+    last, _ = lax.optimization_barrier((over_ctx(near, step, spots), gate))
+    return [near, last], [swap(near, 1), swap(last, 1)], (ids, tuple(i + step for i in ids))
 
 
 def replicated_body(

time: 101 us -> 101 us (level)
  starting transfers between devices: 28.2 us -> 24.9 us
  waiting for transfers between devices: 14.1 us -> 16.5 us
  local copies, waits for them, and re-layouts: 2.99 us -> 4.14 us
    ppermute x9, starting transfers between devices: 17.5 us -> 14.4 us  [over_ctx(): lax.ppermute(value, 'ctx', [(spot, spot ^ step) for spot in range(spots)])]
    ppermute x9, waiting for transfers between devices: 7.65 us -> 9.56 us  [over_ctx(): lax.ppermute(value, 'ctx', [(spot, spot ^ step) for spot in range(spots)])]
    ppermute x20 -> x21, waiting for transfers between devices: 6.42 us -> 6.96 us  [swap(): return lax.ppermute(value, 'wt', [(spot, spot ^ mask) for spot in range(4)])]
    ppermute x20 -> x21, starting transfers between devices: 10.7 us -> 10.5 us  [swap(): return lax.ppermute(value, 'wt', [(spot, spot ^ mask) for spot in range(4)])]
  transfers between devices with their start and end apart: 29 -> 30, of which waited for: 10 -> 10; matrix products, arithmetic and copies ran while one was open for 4% -> 6% of each run, Pallas kernels for 36% -> 35%
where the time goes in v6:
time: 101 us; the launch traced here: 100 us
  Pallas kernels  51.4 us (51%)
  starting transfers between devices  24.9 us (25%)
  waiting for transfers between devices  16.5 us (16%)
  local copies, waits for them, and re-layouts  4.14 us (4%)
  other arithmetic  2.44 us (2%)
    pallas_call x9, Pallas kernels, call(): pl.pallas_call(kernel, out_shape=[o.value if isinstance(o, Away) else o f...  51.4 us
    ppermute x9, starting transfers between devices, over_ctx(): lax.ppermute(value, 'ctx', [(spot, spot ^ step) for spot in range(spots)])  14.4 us
    ppermute x21, starting transfers between devices, swap(): return lax.ppermute(value, 'wt', [(spot, spot ^ mask) for spot in range(4)])  10.5 us
    ppermute x9, waiting for transfers between devices, over_ctx(): lax.ppermute(value, 'ctx', [(spot, spot ^ step) for spot in range(spots)])  9.56 us
    ppermute x21, waiting for transfers between devices, swap(): return lax.ppermute(value, 'wt', [(spot, spot ^ mask) for spot in range(4)])  6.96 us
  transfers between devices with their start and end apart: 30, of which 10 were waited for; matrix products, arithmetic and copies ran while one was open for 6% of the time, Pallas kernels for 35%

profile of v6, /device:TPU:0, one launch (start us, length us, event | category | flops | bytes accessed | tf_op | source)
XLA Modules:
  0.0 100.4 jit_solution(3546372453244549945)
XLA Ops:
  0.7 1.0 constant_dynamic-slice_fusion
  1.7 4.0 %collective-permute-start.2 = (bf16[64,768]{1,0:T(8,128)(2,1)S(1)}, bf16[64,768]{1,0:T(8,128)(2,1)S(1)}, u32[]{:S(2)}, u32[]{:S(2)}) collective-permute-start(bf16[64,768]{1,0:T(8,128)(2,1)S(1)} %constant_dynamic-slice_fusion), channel_id=1, source_target_pairs={{0,16},{4,20},{8,24},{12,28},{16,0},{20,4},{24,8},{28,12},{1,17},{... | collective-permute-start | bytes 294920 | tf_op jit(solution)/shard_map/ppermute | solution.py:661
  5.7 1.3 %collective-permute-start.3 = (bf16[64,768]{1,0:T(8,128)(2,1)S(1)}, bf16[64,768]{1,0:T(8,128)(2,1)S(1)}, u32[]{:S(2)}, u32[]{:S(2)}) collective-permute-start(bf16[64,768]{1,0:T(8,128)(2,1)S(1)} %constant_dynamic-slice_fusion), channel_id=1, source_target_pairs={{0,24},{4,28},{8,16},{12,20},{16,8},{20,12},{24,0},{28,4},{1,25},{... | collective-permute-start | bytes 294920 | tf_op jit(solution)/shard_map/ppermute | solution.py:661
  7.3 0.9 dynamic-slice_bitcast_fusion.1
  8.2 1.5 %collective-permute-start.9 = (bf16[1,64,768]{2,1,0:T(8,128)(2,1)S(1)}, bf16[1,64,768]{2,1,0:T(8,128)(2,1)S(1)}, u32[]{:S(2)}, u32[]{:S(2)}) collective-permute-start(bf16[1,64,768]{2,1,0:T(8,128)(2,1)S(1)} %dynamic-slice_bitcast_fusion.1), channel_id=1, source_target_pairs={{0,4},{4,0},{8,12},{12,8},{16,20},{20,16},{24,28},{28,24},{1,5},{5... | collective-permute-start | bytes 294920 | tf_op jit(solution)/shard_map/ppermute | solution.py:661
  9.7 1.2 %pad_maximum_fusion = bf16[480,768]{1,0:T(8,128)(2,1)S(1)} fusion(bf16[192,768]{1,0:T(8,128)(2,1)} %refs_12_.1, bf16[288,768]{1,0:T(8,128)(2,1)} %refs_15_.1), kind=kLoop, calls=%fused_computation | loop fusion | flops 1474560 | bytes 1474560 | tf_op jit(solution)/shard_map/concatenate | solution.py:729
  10.9 1.6 %collective-permute-start.18 = (bf16[480,768]{1,0:T(8,128)(2,1)S(1)}, bf16[480,768]{1,0:T(8,128)(2,1)}, u32[]{:S(2)}, u32[]{:S(2)}) collective-permute-start(bf16[480,768]{1,0:T(8,128)(2,1)S(1)} %pad_maximum_fusion), channel_id=1, source_target_pairs={{0,2},{1,3},{2,0},{3,1},{4,6},{5,7},{6,4},{7,5},{8,10},{9,11},{10,... | collective-permute-start | bytes 2211848 | tf_op jit(solution)/shard_map/ppermute | solution.py:665
  12.5 0.8 dynamic-slice_bitcast_fusion
  13.3 2.3 %collective-permute-start.10 = (bf16[2,64,768]{2,1,0:T(8,128)(2,1)S(1)}, bf16[2,64,768]{2,1,0:T(8,128)(2,1)S(1)}, u32[]{:S(2)}, u32[]{:S(2)}) collective-permute-start(bf16[2,64,768]{2,1,0:T(8,128)(2,1)S(1)} %pad_maximum_fusion.3), channel_id=1, source_target_pairs={{0,8},{4,12},{8,0},{12,4},{16,24},{20,28},{24,16},{28,20},{1,9},{5... | collective-permute-start | bytes 589832 | tf_op jit(solution)/shard_map/ppermute | solution.py:661
  15.6 1.6 %collective-permute-start.4 = (bf16[2,64,768]{2,1,0:T(8,128)(2,1)S(1)}, bf16[2,64,768]{2,1,0:T(8,128)(2,1)}, u32[]{:S(2)}, u32[]{:S(2)}) collective-permute-start(bf16[2,64,768]{2,1,0:T(8,128)(2,1)S(1)} %pad_maximum_fusion.2.refs_2_), channel_id=1, source_target_pairs={{0,4},{4,0},{8,12},{12,8},{16,20},{20,16},{24,28},{28,24},{1,5},{5... | collective-permute-start | bytes 589832 | tf_op jit(solution)/shard_map/ppermute | solution.py:661
  17.8 2.8 %collective-permute-done.10 = bf16[2,64,768]{2,1,0:T(8,128)(2,1)S(1)} collective-permute-done((bf16[2,64,768]{2,1,0:T(8,128)(2,1)S(1)}, bf16[2,64,768]{2,1,0:T(8,128)(2,1)S(1)}, u32[]{:S(2)}, u32[]{:S(2)}) %collective-permute-start.10) | collective-permute-done | bytes 196640 | tf_op jit(solution)/shard_map/ppermute | solution.py:661
  22.1 1.6 %collective-permute-done.4.refs_3_ = bf16[2,64,768]{2,1,0:T(8,128)(2,1)} collective-permute-done((bf16[2,64,768]{2,1,0:T(8,128)(2,1)S(1)}, bf16[2,64,768]{2,1,0:T(8,128)(2,1)}, u32[]{:S(2)}, u32[]{:S(2)}) %collective-permute-start.4) | collective-permute-done | bytes 196640 | tf_op jit(solution)/shard_map/ppermute | solution.py:661
  23.6 1.5 %collective-permute-start.20 = (bf16[288,768]{1,0:T(8,128)(2,1)}, bf16[288,768]{1,0:T(8,128)(2,1)}, u32[]{:S(2)}, u32[]{:S(2)}) collective-permute-start(bf16[288,768]{1,0:T(8,128)(2,1)} %dynamic-slice_bitcast_fusion), channel_id=1, source_target_pairs={{0,2},{1,3},{2,0},{3,1},{4,6},{5,7},{6,4},{7,5},{8,10},{9,11},{10,... | collective-permute-start | bytes 1327112 | tf_op jit(solution)/shard_map/ppermute | solution.py:665
  25.1 1.5 %collective-permute-done.1.refs_1_ = bf16[2,64,768]{2,1,0:T(8,128)(2,1)} collective-permute-done((bf16[2,64,768]{2,1,0:T(8,128)(2,1)S(1)}, bf16[2,64,768]{2,1,0:T(8,128)(2,1)}, u32[]{:S(2)}, u32[]{:S(2)}) %collective-permute-start.1) | collective-permute-done | bytes 196640 | tf_op jit(solution)/shard_map/ppermute | solution.py:661
  26.6 2.3 %collective-permute-start.11 = (bf16[4,64,768]{2,1,0:T(8,128)(2,1)}, bf16[4,64,768]{2,1,0:T(8,128)(2,1)}, u32[]{:S(2)}, u32[]{:S(2)}) collective-permute-start(bf16[4,64,768]{2,1,0:T(8,128)(2,1)} %constant_dynamic-update-slice_fusion.refs_1_), channel_id=1, source_target_pairs={{0,16},{4,20},{8,24},{12,28},{16,0},{20,4},{24,8},{28,12},{1,17},{... | collective-permute-start | bytes 1179656 | tf_op jit(solution)/shard_map/ppermute | solution.py:661
  29.4 1.1 %collective-permute-done.18.refs_16_ = bf16[480,768]{1,0:T(8,128)(2,1)} collective-permute-done((bf16[480,768]{1,0:T(8,128)(2,1)S(1)}, bf16[480,768]{1,0:T(8,128)(2,1)}, u32[]{:S(2)}, u32[]{:S(2)}) %collective-permute-start.18) | collective-permute-done | bytes 737312 | tf_op jit(solution)/shard_map/ppermute | solution.py:665
  31.7 8.7 %shard_map.143 = (bf16[1024,768]{1,0:T(8,128)(2,1)}, bf16[1024,768]{1,0:T(8,128)(2,1)S(1)}, bf16[576,1024]{1,0:T(8,128)(2,1)S(1)}, bf16[192,512]{1,0:T(8,128)(2,...) custom-call(s32[4]{0:T(128)S(1)} %pad_add_fusion.place, bf16[128,768]{1,0:T(8,128)(2,1)} %tokens.1, ...), custom_call_target="tpu_custom_call" | custom-call | tf_op jit(solution)/shard_map/pallas_call | solution.py:283
  40.5 1.6 %collective-permute-start.15 = (bf16[192,512]{1,0:T(8,128)(2,1)S(1)}, bf16[192,512]{1,0:T(8,128)(2,1)S(1)}, u32[]{:S(2)}, u32[]{:S(2)}) collective-permute-start(bf16[192,512]{1,0:T(8,128)(2,1)S(1)} %get-tuple-element.61.refs_5_.att_a), channel_id=1, source_target_pairs={{0,2},{1,3},{2,0},{3,1},{4,6},{5,7},{6,4},{7,5},{8,10},{9,11},{10,... | collective-permute-start | bytes 589832 | tf_op jit(solution)/shard_map/ppermute | solution.py:665
  42.6 3.5 %collective-permute-done.11.refs_2_ = bf16[4,64,768]{2,1,0:T(8,128)(2,1)} collective-permute-done((bf16[4,64,768]{2,1,0:T(8,128)(2,1)}, bf16[4,64,768]{2,1,0:T(8,128)(2,1)}, u32[]{:S(2)}, u32[]{:S(2)}) %collective-permute-start.11) | collective-permute-done | bytes 393248 | tf_op jit(solution)/shard_map/ppermute | solution.py:661
  46.2 1.2 %collective-permute-done.15.refs_7_ = bf16[192,512]{1,0:T(8,128)(2,1)S(1)} collective-permute-done((bf16[192,512]{1,0:T(8,128)(2,1)S(1)}, bf16[192,512]{1,0:T(8,128)(2,1)S(1)}, u32[]{:S(2)}, u32[]{:S(2)}) %collective-permute-start.15) | collective-permute-done | bytes 196640 | tf_op jit(solution)/shard_map/ppermute | solution.py:665
  47.4 4.4 %shard_map.144 = (bf16[192,512]{1,0:T(8,128)(2,1)S(1)}, f32[192,512]{1,0:T(8,128)S(1)}, f32[8,512]{1,0:T(8,128)S(1)}) custom-call(bf16[576,1024]{1,0:T(8,128)(2,1)S(1)} %get-tuple-element.65.qkv.refs_13_), custom_call_target="tpu_custom_call" | custom-call | tf_op jit(solution)/shard_map/pallas_call | solution.py:283
  52.3 1.6 %collective-permute-start.23 = (bf16[192,512]{1,0:T(8,128)(2,1)S(1)}, bf16[192,512]{1,0:T(8,128)(2,1)S(1)}, u32[]{:S(2)}, u32[]{:S(2)}) collective-permute-start(bf16[192,512]{1,0:T(8,128)(2,1)S(1)} %get-tuple-element.101.refs_1_.att_b), channel_id=1, source_target_pairs={{0,2},{1,3},{2,0},{3,1},{4,6},{5,7},{6,4},{7,5},{8,10},{9,11},{10,... | collective-permute-start | bytes 589832 | tf_op jit(solution)/shard_map/ppermute | solution.py:665
  54.1 9.0 %shard_map.145 = (bf16[1024,768]{1,0:T(8,128)(2,1)S(1)}, bf16[768,768]{1,0:T(8,128)(2,1)S(1)}, bf16[1152,768]{1,0:T(8,128)(2,1)S(1)}, bf16[576,768]{1,0:T(8,128)...) custom-call(s32[4]{0:T(128)S(1)} %pad_add_fusion.place, ...), custom_call_target="tpu_custom_call" | custom-call | flops 2868903936 | bytes 8408080 | tf_op jit(solution)/shard_map/pallas_call | solution.py:283
  63.7 0.9 collective-permute-done.24.refs_4_
  64.6 7.5 %shard_map.146 = (f32[512,768]{1,0:T(8,128)S(1)}, bf16[512,768]{1,0:T(8,128)(2,1)S(1)}, bf16[288,512]{1,0:T(8,128)(2,1)S(1)}, bf16[576,512]{1,0:T(8,128)(2,1)S(1...) custom-call(s32[4]{0:T(128)S(1)} %pad_add_fusion.place, ...), custom_call_target="tpu_custom_call" | custom-call | flops 2868903936 | bytes 7572496 | tf_op jit(solution)/shard_map/pallas_call | solution.py:283
  72.6 2.5 %shard_map.147 = (f32[576,768]{1,0:T(8,128)}, f32[288,768]{1,0:T(8,128)}) custom-call(bf16[576,512]{1,0:T(8,128)(2,1)S(1)} %get-tuple-element.85.gate_a, bf16[576,512]{1,0:T(8,128)(2,1)S(1)} %get-tuple-element.86.gate_b, bf16[288,512]{1,0:T(8,128)(2,1)S(1)} %get-tuple-element.87.hidden_a, bf16[288,512]{1,0:T(8,128)(2,1)S(1)} %get-tuple-element.88.hidden_b, ...), custom_call_target="tpu_custom_call" | custom-call | flops 1358954496 | bytes 4915200 | tf_op jit(solution)/shard_map/pallas_call | solution.py:283
  75.1 15.0 %shard_map.148 = (f32[1,768]{1,0:T(1,128)S(1)}, bf16[1024,768]{1,0:T(8,128)(2,1)S(1)}, f32[128,768]{1,0:T(8,128)S(1)}, bf16[144,768]{1,0:T(8,128)(2,1)S(1)}, f32[576,768]{1,0:T(8,128)}) custom-call(s32[4]{0:T(128)S(1)} %pad_add_fusion.place, f32[512,768]{1,0:T(8,128)S(1)} %get-tuple-element.77.refs_0_, f32[512,768]{1,0:T(8,128)S(1)} %get-tuple-element.78.refs_1_, ...), custom_call_target="tpu_custom_call" | custom-call | flops 9261023232 | bytes 12892176 | tf_op jit(solution)/shard_map/pallas_call | solution.py:283
  90.7 1.0 collective-permute-done.28.far
  91.8 1.1 %collective-permute-start.29 = (bf16[144,768]{1,0:T(8,128)(2,1)S(1)}, bf16[144,768]{1,0:T(8,128)(2,1)S(1)}, u32[]{:S(2)}, u32[]{:S(2)}) collective-permute-start(bf16[144,768]{1,0:T(8,128)(2,1)S(1)} %shard_map.149.mine), channel_id=1, source_target_pairs={{0,2},{1,3},{2,0},{3,1},{4,6},{5,7},{6,4},{7,5},{8,10},{9,11},{10,... | collective-permute-start | bytes 663560 | tf_op jit(solution)/shard_map/ppermute | solution.py:665
  93.4 3.1 %shard_map.150 = (f32[192,768]{1,0:T(8,128)}, bf16[128,768]{1,0:T(8,128)(2,1)}) custom-call(bf16[192,512]{1,0:T(8,128)(2,1)S(1)} %get-tuple-element.61.refs_5_.att_a, bf16[192,512]{1,0:T(8,128)(2,1)S(1)} %get-tuple-element.101.refs_1_.att_b, bf16[1024,768]{1,0:T(8,128)(2,1)S(1)} %get-tuple-element.102.branch, f32[128,768]{1,0:T(8,128)S(1)} %get-tuple-element.103.middle, ...), custom_call_target="tpu_custom_call" | custom-call | flops 301989888 | bytes 2752512 | tf_op jit(solution)/shard_map/pallas_call | solution.py:283
  96.6 2.8 %collective-permute-done.29.far = bf16[144,768]{1,0:T(8,128)(2,1)S(1)} collective-permute-done((bf16[144,768]{1,0:T(8,128)(2,1)S(1)}, bf16[144,768]{1,0:T(8,128)(2,1)S(1)}, u32[]{:S(2)}, u32[]{:S(2)}) %collective-permute-start.29) | collective-permute-done | bytes 221216 | tf_op jit(solution)/shard_map/ppermute | solution.py:665
  99.3 1.0 %shard_map.151 = (bf16[128,768]{1,0:T(8,128)(2,1)}, f32[768]{0:T(1024)}) custom-call(bf16[144,768]{1,0:T(8,128)(2,1)S(1)} %shard_map.149.mine, bf16[144,768]{1,0:T(8,128)(2,1)S(1)} %collective-permute-done.29.far, bf16[128,768]{1,0:T(8,128)(2,1)S(1)} %copy-done.1, f32[1,768]{1,0:T(1,128)S(1)} %broadcast_in_dim.6.refs_8_.refs_22_.gain, ...), custom_call_target="tpu_custom_call" | custom-call | flops 1572864 | bytes 1035264 | tf_op jit(solution)/shard_map/pallas_call | solution.py:283
  (78 shorter events, 7.7 us)
Async XLA Ops:
  1.7 13.9 %collective-permute-start.2 = (bf16[64,768]{1,0:T(8,128)(2,1)S(1)}, bf16[64,768]{1,0:T(8,128)(2,1)S(1)}, u32[]{:S(2)}, u32[]{:S(2)}) collective-permute-start(bf16[64,768]{1,0:T(8,128)(2,1)S(1)} %constant_dynamic-slice_fusion), channel_id=1, source_target_pairs={{0,16},{4,20},{8,24},{12,28},{16,0},{20,4},{24,8},{28,12},{1,17},{... | collective-permute-start | bytes 294920 | tf_op jit(solution)/shard_map/ppermute | solution.py:661
  5.7 7.6 %collective-permute-start.3 = (bf16[64,768]{1,0:T(8,128)(2,1)S(1)}, bf16[64,768]{1,0:T(8,128)(2,1)S(1)}, u32[]{:S(2)}, u32[]{:S(2)}) collective-permute-start(bf16[64,768]{1,0:T(8,128)(2,1)S(1)} %constant_dynamic-slice_fusion), channel_id=1, source_target_pairs={{0,24},{4,28},{8,16},{12,20},{16,8},{20,12},{24,0},{28,4},{1,25},{... | collective-permute-start | bytes 294920 | tf_op jit(solution)/shard_map/ppermute | solution.py:661
  7.1 10.2 %collective-permute-start = (bf16[64,768]{1,0:T(8,128)(2,1)S(1)}, bf16[64,768]{1,0:T(8,128)(2,1)S(1)}, u32[]{:S(2)}, u32[]{:S(2)}) collective-permute-start(bf16[64,768]{1,0:T(8,128)(2,1)S(1)} %constant_dynamic-slice_fusion), channel_id=1, source_target_pairs={{0,8},{4,12},{8,0},{12,4},{16,24},{20,28},{24,16},{28,20},{1,9},{5... | collective-permute-start | bytes 294920 | tf_op jit(solution)/shard_map/ppermute | solution.py:661
  8.2 5.1 %collective-permute-start.9 = (bf16[1,64,768]{2,1,0:T(8,128)(2,1)S(1)}, bf16[1,64,768]{2,1,0:T(8,128)(2,1)S(1)}, u32[]{:S(2)}, u32[]{:S(2)}) collective-permute-start(bf16[1,64,768]{2,1,0:T(8,128)(2,1)S(1)} %dynamic-slice_bitcast_fusion.1), channel_id=1, source_target_pairs={{0,4},{4,0},{8,12},{12,8},{16,20},{20,16},{24,28},{28,24},{1,5},{5... | collective-permute-start | bytes 294920 | tf_op jit(solution)/shard_map/ppermute | solution.py:661
  10.9 19.6 %collective-permute-start.18 = (bf16[480,768]{1,0:T(8,128)(2,1)S(1)}, bf16[480,768]{1,0:T(8,128)(2,1)}, u32[]{:S(2)}, u32[]{:S(2)}) collective-permute-start(bf16[480,768]{1,0:T(8,128)(2,1)S(1)} %pad_maximum_fusion), channel_id=1, source_target_pairs={{0,2},{1,3},{2,0},{3,1},{4,6},{5,7},{6,4},{7,5},{8,10},{9,11},{10,... | collective-permute-start | bytes 2211848 | tf_op jit(solution)/shard_map/ppermute | solution.py:665
  12.5 18.6 %copy-start.3 = (bf16[192,768]{1,0:T(8,128)(2,1)S(1)}, bf16[192,768]{1,0:T(8,128)(2,1)}, u32[]{:S(2)}) copy-start(bf16[192,768]{1,0:T(8,128)(2,1)} %refs_12_.1) | copy-start | bytes 884740
  13.3 7.3 %collective-permute-start.10 = (bf16[2,64,768]{2,1,0:T(8,128)(2,1)S(1)}, bf16[2,64,768]{2,1,0:T(8,128)(2,1)S(1)}, u32[]{:S(2)}, u32[]{:S(2)}) collective-permute-start(bf16[2,64,768]{2,1,0:T(8,128)(2,1)S(1)} %pad_maximum_fusion.3), channel_id=1, source_target_pairs={{0,8},{4,12},{8,0},{12,4},{16,24},{20,28},{24,16},{28,20},{1,9},{5... | collective-permute-start | bytes 589832 | tf_op jit(solution)/shard_map/ppermute | solution.py:661
  15.6 8.0 %collective-permute-start.4 = (bf16[2,64,768]{2,1,0:T(8,128)(2,1)S(1)}, bf16[2,64,768]{2,1,0:T(8,128)(2,1)}, u32[]{:S(2)}, u32[]{:S(2)}) collective-permute-start(bf16[2,64,768]{2,1,0:T(8,128)(2,1)S(1)} %pad_maximum_fusion.2.refs_2_), channel_id=1, source_target_pairs={{0,4},{4,0},{8,12},{12,8},{16,20},{20,16},{24,28},{28,24},{1,5},{5... | collective-permute-start | bytes 589832 | tf_op jit(solution)/shard_map/ppermute | solution.py:661
  17.2 11.7 %collective-permute-start.7 = (bf16[2,64,768]{2,1,0:T(8,128)(2,1)S(1)}, bf16[2,64,768]{2,1,0:T(8,128)(2,1)S(1)}, u32[]{:S(2)}, u32[]{:S(2)}) collective-permute-start(bf16[2,64,768]{2,1,0:T(8,128)(2,1)S(1)} %pad_maximum_fusion.2.refs_2_), channel_id=1, source_target_pairs={{0,1},{1,0},{2,3},{3,2},{4,5},{5,4},{6,7},{7,6},{8,9},{9,8},{10,11... | collective-permute-start | bytes 589832 | tf_op jit(solution)/shard_map/ppermute | solution.py:665
  17.3 9.3 %collective-permute-start.1 = (bf16[2,64,768]{2,1,0:T(8,128)(2,1)S(1)}, bf16[2,64,768]{2,1,0:T(8,128)(2,1)}, u32[]{:S(2)}, u32[]{:S(2)}) collective-permute-start(bf16[2,64,768]{2,1,0:T(8,128)(2,1)S(1)} %pad_maximum_fusion.1.refs_0_), channel_id=1, source_target_pairs={{0,4},{4,0},{8,12},{12,8},{16,20},{20,16},{24,28},{28,24},{1,5},{5... | collective-permute-start | bytes 589832 | tf_op jit(solution)/shard_map/ppermute | solution.py:661
  20.7 8.2 %collective-permute-start.5 = (bf16[2,64,768]{2,1,0:T(8,128)(2,1)S(1)}, bf16[2,64,768]{2,1,0:T(8,128)(2,1)S(1)}, u32[]{:S(2)}, u32[]{:S(2)}) collective-permute-start(bf16[2,64,768]{2,1,0:T(8,128)(2,1)S(1)} %pad_maximum_fusion.1.refs_0_), channel_id=1, source_target_pairs={{0,1},{1,0},{2,3},{3,2},{4,5},{5,4},{6,7},{7,6},{8,9},{9,8},{10,11... | collective-permute-start | bytes 589832 | tf_op jit(solution)/shard_map/ppermute | solution.py:665
  23.6 18.4 %collective-permute-start.20 = (bf16[288,768]{1,0:T(8,128)(2,1)}, bf16[288,768]{1,0:T(8,128)(2,1)}, u32[]{:S(2)}, u32[]{:S(2)}) collective-permute-start(bf16[288,768]{1,0:T(8,128)(2,1)} %dynamic-slice_bitcast_fusion), channel_id=1, source_target_pairs={{0,2},{1,3},{2,0},{3,1},{4,6},{5,7},{6,4},{7,5},{8,10},{9,11},{10,... | collective-permute-start | bytes 1327112 | tf_op jit(solution)/shard_map/ppermute | solution.py:665
  26.6 19.6 %collective-permute-start.11 = (bf16[4,64,768]{2,1,0:T(8,128)(2,1)}, bf16[4,64,768]{2,1,0:T(8,128)(2,1)}, u32[]{:S(2)}, u32[]{:S(2)}) collective-permute-start(bf16[4,64,768]{2,1,0:T(8,128)(2,1)} %constant_dynamic-update-slice_fusion.refs_1_), channel_id=1, source_target_pairs={{0,16},{4,20},{8,24},{12,28},{16,0},{20,4},{24,8},{28,12},{1,17},{... | collective-permute-start | bytes 1179656 | tf_op jit(solution)/shard_map/ppermute | solution.py:661
  28.9 2.2 %collective-permute-start.8 = (bf16[2,64,768]{2,1,0:T(8,128)(2,1)}, bf16[2,64,768]{2,1,0:T(8,128)(2,1)S(1)}, u32[]{:S(2)}, u32[]{:S(2)}) collective-permute-start(bf16[2,64,768]{2,1,0:T(8,128)(2,1)} %collective-permute-done.4.refs_3_), channel_id=1, source_target_pairs={{0,1},{1,0},{2,3},{3,2},{4,5},{5,4},{6,7},{7,6},{8,9},{9,8},{10,11... | collective-permute-start | bytes 589832 | tf_op jit(solution)/shard_map/ppermute | solution.py:665
  28.9 2.8 %collective-permute-start.6 = (bf16[2,64,768]{2,1,0:T(8,128)(2,1)}, bf16[2,64,768]{2,1,0:T(8,128)(2,1)S(1)}, u32[]{:S(2)}, u32[]{:S(2)}) collective-permute-start(bf16[2,64,768]{2,1,0:T(8,128)(2,1)} %collective-permute-done.1.refs_1_), channel_id=1, source_target_pairs={{0,1},{1,0},{2,3},{3,2},{4,5},{5,4},{6,7},{7,6},{8,9},{9,8},{10,11... | collective-permute-start | bytes 589832 | tf_op jit(solution)/shard_map/ppermute | solution.py:665
  30.5 23.6 %collective-permute-start.19 = (bf16[480,768]{1,0:T(8,128)(2,1)}, bf16[480,768]{1,0:T(8,128)(2,1)S(1)}, u32[]{:S(2)}, u32[]{:S(2)}) collective-permute-start(bf16[480,768]{1,0:T(8,128)(2,1)} %collective-permute-done.18.refs_16_), channel_id=1, source_target_pairs={{0,1},{1,0},{2,3},{3,2},{4,5},{5,4},{6,7},{7,6},{8,9},{9,8},{10,11... | collective-permute-start | bytes 2211848 | tf_op jit(solution)/shard_map/ppermute | solution.py:665
  31.1 11.6 %collective-permute-start.17 = (bf16[192,768]{1,0:T(8,128)(2,1)S(1)}, bf16[192,768]{1,0:T(8,128)(2,1)S(1)}, u32[]{:S(2)}, u32[]{:S(2)}) collective-permute-start(bf16[192,768]{1,0:T(8,128)(2,1)S(1)} %copy-done.3), channel_id=1, source_target_pairs={{0,1},{1,0},{2,3},{3,2},{4,5},{5,4},{6,7},{7,6},{8,9},{9,8},{10,11... | collective-permute-start | bytes 884744 | tf_op jit(solution)/shard_map/ppermute | solution.py:665
  31.7 20.6 %copy-start.9 = (f32[768]{0:T(1024)S(1)}, f32[768]{0:T(1024)}, u32[]{:S(2)}) copy-start(f32[768]{0:T(1024)} %param.12) | copy-start | bytes 9220
  40.5 6.9 %collective-permute-start.15 = (bf16[192,512]{1,0:T(8,128)(2,1)S(1)}, bf16[192,512]{1,0:T(8,128)(2,1)S(1)}, u32[]{:S(2)}, u32[]{:S(2)}) collective-permute-start(bf16[192,512]{1,0:T(8,128)(2,1)S(1)} %get-tuple-element.61.refs_5_.att_a), channel_id=1, source_target_pairs={{0,2},{1,3},{2,0},{3,1},{4,6},{5,7},{6,4},{7,5},{8,10},{9,11},{10,... | collective-permute-start | bytes 589832 | tf_op jit(solution)/shard_map/ppermute | solution.py:665
  42.0 12.0 %collective-permute-start.21 = (bf16[288,768]{1,0:T(8,128)(2,1)}, bf16[288,768]{1,0:T(8,128)(2,1)S(1)}, u32[]{:S(2)}, u32[]{:S(2)}) collective-permute-start(bf16[288,768]{1,0:T(8,128)(2,1)} %collective-permute-done.20.refs_13_), channel_id=1, source_target_pairs={{0,4},{4,0},{8,12},{12,8},{16,20},{20,16},{24,28},{28,24},{1,5},{5... | collective-permute-start | bytes 1327112 | tf_op jit(solution)/shard_map/ppermute | solution.py:661
  42.6 9.7 %collective-permute-start.12 = (bf16[4,64,768]{2,1,0:T(8,128)(2,1)}, bf16[4,64,768]{2,1,0:T(8,128)(2,1)S(1)}, u32[]{:S(2)}, u32[]{:S(2)}) collective-permute-start(bf16[4,64,768]{2,1,0:T(8,128)(2,1)} %constant_dynamic-update-slice_fusion.refs_1_), channel_id=1, source_target_pairs={{0,1},{1,0},{2,3},{3,2},{4,5},{5,4},{6,7},{7,6},{8,9},{9,8},{10,11... | collective-permute-start | bytes 1179656 | tf_op jit(solution)/shard_map/ppermute | solution.py:665
  46.2 5.6 %collective-permute-start.14 = (bf16[192,512]{1,0:T(8,128)(2,1)S(1)}, bf16[192,512]{1,0:T(8,128)(2,1)S(1)}, u32[]{:S(2)}, u32[]{:S(2)}) collective-permute-start(bf16[192,512]{1,0:T(8,128)(2,1)S(1)} %get-tuple-element.61.refs_5_.att_a), channel_id=1, source_target_pairs={{0,1},{1,0},{2,3},{3,2},{4,5},{5,4},{6,7},{7,6},{8,9},{9,8},{10,11... | collective-permute-start | bytes 589832 | tf_op jit(solution)/shard_map/ppermute | solution.py:665
  47.4 6.7 %collective-permute-start.13 = (bf16[4,64,768]{2,1,0:T(8,128)(2,1)}, bf16[4,64,768]{2,1,0:T(8,128)(2,1)S(1)}, u32[]{:S(2)}, u32[]{:S(2)}) collective-permute-start(bf16[4,64,768]{2,1,0:T(8,128)(2,1)} %collective-permute-done.11.refs_2_), channel_id=1, source_target_pairs={{0,1},{1,0},{2,3},{3,2},{4,5},{5,4},{6,7},{7,6},{8,9},{9,8},{10,11... | collective-permute-start | bytes 1179656 | tf_op jit(solution)/shard_map/ppermute | solution.py:665
  51.7 2.1 %collective-permute-start.16 = (bf16[192,512]{1,0:T(8,128)(2,1)S(1)}, bf16[192,512]{1,0:T(8,128)(2,1)S(1)}, u32[]{:S(2)}, u32[]{:S(2)}) collective-permute-start(bf16[192,512]{1,0:T(8,128)(2,1)S(1)} %collective-permute-done.15.refs_7_), channel_id=1, source_target_pairs={{0,1},{1,0},{2,3},{3,2},{4,5},{5,4},{6,7},{7,6},{8,9},{9,8},{10,11... | collective-permute-start | bytes 589832 | tf_op jit(solution)/shard_map/ppermute | solution.py:665
  52.3 10.8 %collective-permute-start.23 = (bf16[192,512]{1,0:T(8,128)(2,1)S(1)}, bf16[192,512]{1,0:T(8,128)(2,1)S(1)}, u32[]{:S(2)}, u32[]{:S(2)}) collective-permute-start(bf16[192,512]{1,0:T(8,128)(2,1)S(1)} %get-tuple-element.101.refs_1_.att_b), channel_id=1, source_target_pairs={{0,2},{1,3},{2,0},{3,1},{4,6},{5,7},{6,4},{7,5},{8,10},{9,11},{10,... | collective-permute-start | bytes 589832 | tf_op jit(solution)/shard_map/ppermute | solution.py:665
  53.9 9.8 %collective-permute-start.22 = (bf16[192,512]{1,0:T(8,128)(2,1)S(1)}, bf16[192,512]{1,0:T(8,128)(2,1)S(1)}, u32[]{:S(2)}, u32[]{:S(2)}) collective-permute-start(bf16[192,512]{1,0:T(8,128)(2,1)S(1)} %get-tuple-element.101.refs_1_.att_b), channel_id=1, source_target_pairs={{0,1},{1,0},{2,3},{3,2},{4,5},{5,4},{6,7},{7,6},{8,9},{9,8},{10,11... | collective-permute-start | bytes 589832 | tf_op jit(solution)/shard_map/ppermute | solution.py:665
  63.1 1.5 %collective-permute-start.24 = (bf16[192,512]{1,0:T(8,128)(2,1)S(1)}, bf16[192,512]{1,0:T(8,128)(2,1)S(1)}, u32[]{:S(2)}, u32[]{:S(2)}) collective-permute-start(bf16[192,512]{1,0:T(8,128)(2,1)S(1)} %collective-permute-done.23.refs_3_), channel_id=1, source_target_pairs={{0,1},{1,0},{2,3},{3,2},{4,5},{5,4},{6,7},{7,6},{8,9},{9,8},{10,11... | collective-permute-start | bytes 589832 | tf_op jit(solution)/shard_map/ppermute | solution.py:665
  63.6 11.5 %collective-permute-start.26 = (bf16[512,768]{1,0:T(8,128)(2,1)S(1)}, bf16[512,768]{1,0:T(8,128)(2,1)S(1)}, u32[]{:S(2)}, u32[]{:S(2)}) collective-permute-start(bf16[512,768]{1,0:T(8,128)(2,1)S(1)} %get-tuple-element.83.refs_6_), channel_id=1, source_target_pairs={{0,1},{1,0},{2,3},{3,2},{4,5},{5,4},{6,7},{7,6},{8,9},{9,8},{10,11... | collective-permute-start | bytes 2359304 | tf_op jit(solution)/shard_map/ppermute | solution.py:665
  72.1 2.9 %collective-permute-start.27 = (bf16[512,768]{1,0:T(8,128)(2,1)S(1)}, bf16[512,768]{1,0:T(8,128)(2,1)S(1)}, u32[]{:S(2)}, u32[]{:S(2)}) collective-permute-start(bf16[512,768]{1,0:T(8,128)(2,1)S(1)} %get-tuple-element.84.refs_7_), channel_id=1, source_target_pairs={{0,1},{1,0},{2,3},{3,2},{4,5},{5,4},{6,7},{7,6},{8,9},{9,8},{10,11... | collective-permute-start | bytes 2359304 | tf_op jit(solution)/shard_map/ppermute | solution.py:665
  90.1 1.5 %collective-permute-start.28 = (bf16[144,768]{1,0:T(8,128)(2,1)S(1)}, bf16[144,768]{1,0:T(8,128)(2,1)S(1)}, u32[]{:S(2)}, u32[]{:S(2)}) collective-permute-start(bf16[144,768]{1,0:T(8,128)(2,1)S(1)} %get-tuple-element.100.message), channel_id=1, source_target_pairs={{0,1},{1,0},{2,3},{3,2},{4,5},{5,4},{6,7},{7,6},{8,9},{9,8},{10,11... | collective-permute-start | bytes 663560 | tf_op jit(solution)/shard_map/ppermute | solution.py:665
  90.4 3.1 %collective-permute-start.25 = (bf16[128,768]{1,0:T(8,128)(2,1)}, bf16[128,768]{1,0:T(8,128)(2,1)}, u32[]{:S(2)}, u32[]{:S(2)}) collective-permute-start(bf16[128,768]{1,0:T(8,128)(2,1)} %get-tuple-element.76.part), channel_id=1, source_target_pairs={{0,1},{1,0},{2,3},{3,2},{4,5},{5,4},{6,7},{7,6},{8,9},{9,8},{10,11... | collective-permute-start | bytes 589832 | tf_op jit(solution)/shard_map/ppermute | solution.py:665
  91.8 7.6 %collective-permute-start.29 = (bf16[144,768]{1,0:T(8,128)(2,1)S(1)}, bf16[144,768]{1,0:T(8,128)(2,1)S(1)}, u32[]{:S(2)}, u32[]{:S(2)}) collective-permute-start(bf16[144,768]{1,0:T(8,128)(2,1)S(1)} %shard_map.149.mine), channel_id=1, source_target_pairs={{0,2},{1,3},{2,0},{3,1},{4,6},{5,7},{6,4},{7,5},{8,10},{9,11},{10,... | collective-permute-start | bytes 663560 | tf_op jit(solution)/shard_map/ppermute | solution.py:665
  (10 other events, 104.9 us)
